TPU v7x, 32 devices: a whole 2x2x4 slice. The times are simulated.
32 devices in a mesh: day: 8 (over z, y), sta: 4 (over x, core).
Axes of the slice: x: 2, y: 2, z: 4, core: 2. Of those that a mesh axis runs over, the one named last changes fastest.
Arguments:
- spectra: bfloat16 [512, 2, 3, 96, 128], P('day', None, None, 'sta'), may hold values from -6 to 6
- src_block: int32 [2], replicated, may hold values from 0 to 3, as said below
- group_of: int32 [512], replicated, may hold values from 0 to 1, as said below
- owner: int32 [8], replicated, may hold values from 0 to 7, each once
Outputs:
- owned_stacks: float32 [8, 96, 2, 9, 128], P('day', 'sta')
Inputs may be any that keep to these rules, and one draw needn't show every extreme that they name: `src_block`: the two entries differ. `group_of`: every one of the 2 groups has at least one segment. `owner`: each day index owns exactly one pair block.
All inputs are finite; a program needn't handle non-finite values.
Results may differ from a plain program's by a relative error of at most 0.0003.
Values may be sent and summed in bfloat16 or wider, within the bound.
No kernel may reach another device: no remote copies, remote signals or barrier semaphores. Data moves between devices by JAX's collectives and lax.ppermute only.
A program may use at most 64 MiB of HBM per device.

v0:
```python
import jax
import jax.numpy as jnp
from jax import lax
from jax.sharding import PartitionSpec as P

F = 128
LAG = 128
G = 2
SB = 4
S = 8


def from_root(value, axis, source):
    kept = jnp.where(lax.axis_index(axis) == source, value, 0).astype(value.dtype)
    return lax.psum(kept, axis)


def lag_table(freqs, lags):
    freq_ids = jnp.arange(freqs, dtype=jnp.int32)
    lag_ids = jnp.arange(lags, dtype=jnp.int32) - lags // 2
    phase = jnp.mod(freq_ids[:, None] * lag_ids[None, :], 2 * freqs)
    angle = 2.0 * jnp.pi / (2 * freqs) * phase.astype(jnp.float32)
    weight = jnp.where(freq_ids == 0, 1.0, 2.0).astype(jnp.float32) / jnp.sqrt(jnp.float32(freqs))
    return jnp.concatenate(
        [weight[:, None] * jnp.cos(angle), -weight[:, None] * jnp.sin(angle)], axis=0
    )


def cross_terms(onehot, sources, spectra, scale_rows):
    weighted = onehot[:, :, None, None, None, None] * sources[None]
    real_part = jnp.einsum(
        "gtpasf,tpbrf->srgabf", weighted, spectra, preferred_element_type=jnp.float32
    )
    swapped = jnp.stack([spectra[:, 1], -spectra[:, 0]], axis=1)
    imag_part = jnp.einsum(
        "gtpasf,tpbrf->srgabf", weighted, swapped, preferred_element_type=jnp.float32
    )
    scaled = scale_rows[None, None, :, None, None, None]
    return (real_part * scaled, imag_part * scaled)


def owner_order(blocks, owner, day_count):
    day_ids = jnp.arange(day_count, dtype=jnp.int32)
    inverse = jnp.sum(
        day_ids[None, :] * (owner[None, :] == day_ids[:, None]).astype(jnp.int32), axis=1
    )
    return jnp.take(blocks, inverse, axis=0)


def local(spectra, src_block, group_of, owner):
    seg_count = spectra.shape[0]
    receivers = spectra.shape[3]
    day_count = lax.axis_size("day")
    day_index = lax.axis_index("day")
    group_ids = jnp.arange(G, dtype=jnp.int32)
    all_hot = (group_of[None, :] == group_ids[:, None]).astype(jnp.float32)
    counts = jnp.sum(all_hot, axis=1)
    scale_rows = 1.0 / jnp.sqrt(counts)
    pair_count = S * receivers
    block_rows = pair_count // day_count
    table = lag_table(F, LAG)
    my_groups = lax.dynamic_slice_in_dim(group_of, day_index * seg_count, seg_count)
    onehot = (my_groups[None, :] == group_ids[:, None]).astype(jnp.bfloat16)
    first_rows = spectra[:, :, :, :SB, :]
    gathered = []
    for block_number in range(2):
        gathered.append(from_root(first_rows, "sta", src_block[block_number]))
    sources = jnp.concatenate(gathered, axis=3)
    real_part, imag_part = cross_terms(onehot, sources, spectra, scale_rows)
    spectra_pairs = jnp.concatenate([real_part, imag_part], axis=-1)
    blocks = spectra_pairs.reshape(day_count, block_rows, G, 9, 2 * F)
    ordered = owner_order(blocks, owner, day_count).reshape(day_count * block_rows, G, 9, 2 * F)
    result = jnp.dot(ordered.reshape(-1, 2 * F), table, precision=lax.Precision.HIGHEST)
    mine = lax.psum_scatter(
        result.reshape(block_rows * lax.axis_size("day"), G, 9, LAG),
        "day",
        scatter_dimension=0,
        tiled=True,
    )
    return mine.reshape(1, block_rows, G, 9, LAG)


def solution(mesh):
    return jax.shard_map(
        local,
        mesh=mesh,
        in_specs=(P("day", None, None, "sta", None), P(), P(), P()),
        out_specs=P("day", "sta", None, None, None),
        check_vma=False,
    )
```

profile of v0, /device:TPU:0, one launch (start us, length us, event | category | flops | bytes accessed | tf_op | source)
XLA Modules:
  0.0 175.8 jit_solution(10725715226113361504)
XLA Ops:
  6.5 1.3 fusion.24
  9.2 2.3 %broadcast_select_fusion.1 = (bf16[64,2,3,4,128]{4,3,2,1,0:T(4,128)(2,1)}, bf16[64,2,3,4,128]{4,3,2,1,0:T(4,128)(2,1)}) fusion(pred[]{:T(512)S(6)} %eq.72, bf16[64,2,3,24,128]{4,3,2,1,0:T(8,128)(2,1)} %param.4, pred[]{:T(512)S(6)} %eq.73), kind=kLoop, calls=%fused_computation.19 | loop fusion | flops 393216 | bytes 1179650 | tf_op jit(solution)/shard_map/jit(_where)/select_n | solution.py:14
  11.6 2.1 %fusion.23 = (bf16[64,1,3,24,128]{4,3,2,1,0:T(8,128)(2,1)S(1)}, bf16[64,1,3,24,128]{4,3,2,1,0:T(8,128)(2,1)S(1)}) fusion(bf16[64,2,3,24,128]{4,3,2,1,0:T(8,128)(2,1)} %param.4), kind=kLoop, calls=%fused_computation.51 | loop fusion | bytes 4718592 | tf_op jit(solution)/shard_map/slice | solution.py:34
  13.8 0.5 fusion.19
  14.3 0.5 fusion.18
  14.8 0.1 fusion.17
  15.0 0.5 iota_add_fusion
  15.5 2.8 %copy.72 = bf16[64,1,3,24,128]{0,3,1,2,4:T(8,128)(2,1)} copy(bf16[64,1,3,24,128]{4,3,2,1,0:T(8,128)(2,1)S(1)} %get-tuple-element.10) | data formatting | bytes 2359296
  18.3 3.8 %neg.12 = bf16[64,1,3,24,128]{0,3,1,2,4:T(8,128)(2,1)} negate(bf16[64,1,3,24,128]{0,3,1,2,4:T(8,128)(2,1)} %copy.72) | non-fusion elementwise | flops 589824 | bytes 2359296 | tf_op jit(solution)/shard_map/neg | solution.py:34
  22.2 2.8 %copy.71 = bf16[64,1,3,24,128]{0,3,1,2,4:T(8,128)(2,1)} copy(bf16[64,1,3,24,128]{4,3,2,1,0:T(8,128)(2,1)S(1)} %get-tuple-element.9) | data formatting | bytes 2359296
  25.0 4.8 %copy.63 = bf16[64,2,3,24,128,1,1]{0,3,1,2,6,5,4:T(8,128)(2,1)} copy(bf16[64,2,3,24,128,1,1]{4,3,2,1,0,6,5:T(8,128)(2,1)S(1)} %bitcast.45) | data formatting | bytes 4718592 | tf_op args[0]
  30.1 0.9 cosine_multiply_fusion
  31.0 18.1 %all-reduce.3.cloned.1.call-done = (bf16[64,2,3,4,128]{4,3,2,1,0:T(4,128)(2,1)}, bf16[64,2,3,4,128]{4,3,2,1,0:T(4,128)(2,1)}) async-done(((bf16[64,2,3,4,128]{4,3,2,1,0:T(4,128)(2,1)}, bf16[64,2,3,4,128]{4,3,2,1,0:T(4,128)(2,1)}), (bf16[64,2,3,4,128]{4,3,2,1,0:T(4,128)(2,1)}, bf16[64,2,3,4,128]{4,3,2,1,0:T(4,128)(2,1)})) %all-reduce.3.cloned.1.call-update) | async-done | bytes 786448 | tf_op jit(solution)/shard_map/psum | solution.py:15
  49.1 1.5 pad_maximum_fusion.1
  50.6 1.2 copy.52
  51.9 9.7 %fusion.3 = f32[128,3,24,2,3,8]{2,5,4,3,1,0:T(8,128)} fusion(bf16[64,1,3,24,128]{0,3,1,2,4:T(8,128)(2,1)} %neg.12, bf16[64,1,3,24,128]{0,3,1,2,4:T(8,128)(2,1)} %copy.71, bf16[64,2,3,8,128]{0,3,1,2,4:T(8,128)(2,1)S(1)} %copy.52, bf16[2,64]{1,0:T(2,128)(2,1)S(1)} %compare_convert_fusion.1), kind=kOutput, calls=%fused_computation.9 | convolution fusion | flops 121110528 | bytes 4915456 | tf_op jit(solution)/shard_map/gtpasf,tpbrf->srgabf/dot_general | solution.py:35
  61.5 6.4 %copy.57 = f32[128,3,24,2,3,8]{0,5,4,3,2,1:T(8,128)S(1)} copy(f32[128,3,24,2,3,8]{2,5,4,3,1,0:T(8,128)} %fusion.3) | data formatting | bytes 3538944 | tf_op jit(solution)/shard_map/gtpasf,tpbrf->srgabf/dot_general | solution.py:35
  67.9 11.9 %convolution_bitcast_fusion = f32[128,2,3,8,3,24]{5,3,4,2,1,0:T(8,128)} fusion(bf16[64,2,3,24,128,1,1]{0,3,1,2,6,5,4:T(8,128)(2,1)} %copy.63, bf16[64,2,3,8,128]{0,3,1,2,4:T(8,128)(2,1)S(1)} %copy.52, bf16[2,64]{1,0:T(2,128)(2,1)S(1)} %compare_convert_fusion.1), kind=kOutput, calls=%fused_computation.10 | convolution fusion | flops 116391936 | bytes 4915456 | tf_op jit(solution)/shard_map/gtpasf,tpbrf->srgabf/dot_general | solution.py:31
  79.9 7.5 %copy.54 = f32[128,2,3,8,3,24]{0,3,2,1,5,4:T(8,128)} copy(f32[128,2,3,8,3,24]{5,3,4,2,1,0:T(8,128)} %convolution_bitcast_fusion) | data formatting | bytes 3538944 | tf_op jit(solution)/shard_map/gtpasf,tpbrf->srgabf/dot_general | solution.py:31
  87.4 0.2 multiply_bitcast_fusion.4
  87.6 1.3 copy-done.1
  88.9 0.2 multiply_bitcast_fusion.5
  89.1 0.3 pad_maximum_fusion
  89.4 2.1 %copy.58 = f32[8,24,2,3,3,256]{5,1,4,3,2,0:T(8,128)S(1)} copy(f32[8,24,2,3,3,256]{5,0,3,2,1,4:T(8,128)S(1)} %pad_maximum_fusion) | data formatting | bytes 7077888 | tf_op jit(solution)/shard_map/concatenate | solution.py:70
  91.5 0.4 copy.59
  91.9 2.5 %gather_fusion = f32[8,24,2,9,256]{4,1,2,3,0:T(8,128)} fusion(f32[8,24,2,9,256]{4,1,2,3,0:T(8,128)S(1)} %copy.59, s32[1024]{0:T(1024)S(1)} %pad_clamp_fusion), kind=kCustom, calls=%fused_computation | custom fusion | bytes 7077920 | tf_op jit(solution)/shard_map/jit(_take)/gather | solution.py:47
  94.4 2.4 %copy.60 = f32[8,24,2,9,256]{4,1,0,3,2:T(8,128)S(1)} copy(f32[8,24,2,9,256]{4,1,2,3,0:T(8,128)} %gather_fusion) | data formatting | bytes 7077888 | tf_op jit(solution)/shard_map/jit(_take)/gather | solution.py:47
  96.8 0.5 bitcast_select_fusion
  97.3 0.4 copy-done.2
  97.7 4.1 %fusion.8 = f32[192,2,9,128]{3,0,2,1:T(8,128)} fusion(f32[192,2,9,256]{3,0,2,1:T(8,128)S(1)} %bitcast_select_fusion, f32[128,128]{1,0:T(8,128)S(1)} %copy-done.3, f32[128,128]{1,0:T(8,128)S(1)} %copy-done.2), kind=kOutput, calls=%fused_computation.21 | convolution fusion | flops 1358987264 | bytes 5439488 | tf_op jit(solution)/shard_map/dot_general | solution.py:73
  101.8 65.4 %reduce-scatter.2.cloned.1.call-done = f32[24,2,9,128]{3,0,2,1:T(8,128)} async-done(((f32[192,2,9,128]{3,0,2,1:T(8,128)}), f32[24,2,9,128]{3,0,2,1:T(8,128)}) %reduce-scatter.2.cloned.1.call-update) | async-done | bytes 221200 | tf_op jit(solution)/shard_map/reduce_scatter | solution.py:74
  167.2 1.7 copy.61
  (28 shorter events, 0.5 us)
Async XLA Ops:
  6.5 42.6 %all-reduce.3.cloned.1.call-start = ((), (), s32[]{:S(2)}) async-start(), calls=%async_computation.2 | async-start | bytes 1572864 | tf_op jit(solution)/shard_map/psum | solution.py:15
  9.2 4.5 %copy-start.8 = (s32[8]{0:T(128)S(1)}, s32[8]{0:T(128)}, u32[]{:S(2)}) copy-start(s32[8]{0:T(128)} %param.7) | copy-start | bytes 100
  9.2 5.7 %copy-start.4 = (s32[512]{0:T(512)S(1)}, s32[512]{0:T(512)}, u32[]{:S(2)}) copy-start(s32[512]{0:T(512)} %param.6) | copy-start | bytes 6148
  11.5 155.7 %reduce-scatter.2.cloned.1.call-start = ((), (), s32[]{:S(2)}) async-start(), calls=%async_computation.1 | async-start | bytes 1990656 | tf_op jit(solution)/shard_map/reduce_scatter | solution.py:74
  18.3 6.6 %copy-start = (bf16[64,2,3,24,128]{4,3,2,1,0:T(8,128)(2,1)S(1)}, bf16[64,2,3,24,128]{4,3,2,1,0:T(8,128)(2,1)}, u32[]{:S(2)}) copy-start(bf16[64,2,3,24,128]{4,3,2,1,0:T(8,128)(2,1)} %param.4) | copy-start | bytes 7077892
  25.0 5.0 %copy-start.7 = (s32[8]{0:T(128)S(1)}, s32[8]{0:T(128)}, u32[]{:S(2)}) copy-start(s32[8]{0:T(128)} %fusion.19) | copy-start | bytes 100
  25.0 5.1 %copy-start.5 = (f32[128]{0:T(128)S(1)}, f32[128]{0:T(128)}, u32[]{:S(2)}) copy-start(f32[128]{0:T(128)} %get-tuple-element.16) | copy-start | bytes 1540
  25.0 5.1 %copy-start.6 = (s32[128]{0:T(128)S(1)}, s32[128]{0:T(128)}, u32[]{:S(2)}) copy-start(s32[128]{0:T(128)} %iota_add_fusion) | copy-start | bytes 1540
  87.4 1.5 copy-start.1
  96.8 0.8 copy-start.2
  96.8 0.9 copy-start.3
Sparse Core Ops, SparseCore 0:
  11.6 37.4 all-reduce.2
  102.0 65.2 reduce-scatter.1
where the time goes:
time: 176 us
  waiting for transfers between devices  83.5 us (47%)
  local copies, waits for them, and re-layouts  40.1 us (23%)
  matrix products  25.7 us (15%)
  between operations  14.9 us (8%)
  other arithmetic  11.6 us (7%)
    reduce_scatter x1, waiting for transfers between devices, local(): lax.psum_scatter(result.reshape(block_rows * lax.axis_size('day'), G, 9,...  65.4 us
    psum x1, waiting for transfers between devices, from_root(): return lax.psum(kept, axis)  18.1 us
    unnamed x21, local copies, waits for them, and re-layouts  12.2 us
    dot_general x1, matrix products, cross_terms(): jnp.einsum('gtpasf,tpbrf->srgabf', weighted, spectra, preferred_element_t...  11.9 us
    dot_general x1, matrix products, cross_terms(): jnp.einsum('gtpasf,tpbrf->srgabf', weighted, swapped, preferred_element_t...  9.66 us
    dot_general x1, local copies, waits for them, and re-layouts, cross_terms(): jnp.einsum('gtpasf,tpbrf->srgabf', weighted, spectra, preferred_element_t...  7.52 us
    dot_general x1, local copies, waits for them, and re-layouts, cross_terms(): jnp.einsum('gtpasf,tpbrf->srgabf', weighted, swapped, preferred_element_t...  6.4 us
    gather x2, local copies, waits for them, and re-layouts, owner_order(): return jnp.take(blocks, inverse, axis=0)  4.88 us
  transfers between devices with their start and end apart: 2, of which 2 were waited for; matrix products, arithmetic and copies ran while one was open for 11% of the time, Pallas kernels for 0%

commit v1 on v0

v1 whole, which is shorter than its diff:
```python
import functools

import jax
import jax.numpy as jnp
import numpy as np
from jax import lax
from jax.experimental import pallas as pl
from jax.experimental.pallas import tpu as pltpu
from jax.sharding import PartitionSpec as P

F = 128
LAG = 128
G = 2
SB = 4
S = 8
COMPS = 3
XS = 2 * F + 8

f32 = jnp.float32
bf16 = jnp.bfloat16
PARAMS = pltpu.CompilerParams(vmem_limit_bytes=48 << 20)
VMEM = pl.BlockSpec(memory_space=pltpu.VMEM)
SMEM = pl.BlockSpec(memory_space=pltpu.SMEM)


def lag_table(freqs, lags):
    freq_ids = np.arange(freqs)
    lag_ids = np.arange(lags) - lags // 2
    angle = 2.0 * np.pi / (2 * freqs) * np.mod(freq_ids[:, None] * lag_ids[None, :], 2 * freqs)
    weight = np.where(freq_ids == 0, 1.0, 2.0)[:, None] / np.sqrt(freqs)
    table = np.concatenate([weight * np.cos(angle), -weight * np.sin(angle)], axis=0).astype(np.float32)
    high = table.astype(bf16)
    low = (table - high.astype(np.float32)).astype(bf16)
    return np.concatenate([high, low], axis=1)


def first_kernel(x_ref, o_ref, wide):
    rows = x_ref.shape[0] * 2
    for part in range(2):
        wide[part] = x_ref[:, part, 0].astype(f32)
    flat = wide.reshape(rows * 8, F)
    for s in range(SB):
        o_ref[0, s] = flat[pl.ds(s, rows, stride=8), :].T.astype(bf16)


def first_block(spectra):
    segs = spectra.shape[0]
    return pl.pallas_call(
        first_kernel,
        grid=(COMPS,),
        in_specs=[pl.BlockSpec((segs, 2, 1, 8, F), lambda b: (0, 0, b, 0, 0))],
        out_specs=pl.BlockSpec((1, SB, F, 2 * segs), lambda b: (b, 0, 0, 0)),
        out_shape=jax.ShapeDtypeStruct((COMPS, SB, F, 2 * segs), bf16),
        scratch_shapes=[pltpu.VMEM((2, segs, 8, F), f32)],
        compiler_params=PARAMS,
        name="first_block",
    )(spectra)


def receivers_kernel(x_ref, o_ref, wide, turned):
    b = pl.program_id(0)
    rows = x_ref.shape[0] * 2
    stations = x_ref.shape[3]
    for part in range(2):
        wide[part] = x_ref[:, part, 0].astype(f32)
    flat = wide.reshape(rows * stations, F)
    for r in range(stations):
        turned[pl.ds(b * stations + r, F, stride=COMPS * stations), :] = flat[pl.ds(r, rows, stride=stations), :].T

    @pl.when(b == COMPS - 1)
    def _():
        def body(f, carry):
            o_ref[f] = turned[pl.ds(pl.multiple_of(f * COMPS * stations, 8), COMPS * stations), :].astype(bf16)
            return carry

        lax.fori_loop(0, F, body, 0, unroll=8)


def receivers_by_freq(spectra):
    segs, stations = spectra.shape[0], spectra.shape[3]
    columns = COMPS * stations
    return pl.pallas_call(
        receivers_kernel,
        grid=(COMPS,),
        in_specs=[pl.BlockSpec((segs, 2, 1, stations, F), lambda b: (0, 0, b, 0, 0))],
        out_specs=pl.BlockSpec((F, columns, 2 * segs), lambda b: (0, 0, 0)),
        out_shape=jax.ShapeDtypeStruct((F, columns, 2 * segs), bf16),
        scratch_shapes=[pltpu.VMEM((2, segs, stations, F), f32), pltpu.VMEM((F * columns, 2 * segs), f32)],
        compiler_params=PARAMS,
        cost_estimate=pl.CostEstimate(flops=0, bytes_accessed=12 << 20, transcendentals=0),
        name="receivers_by_freq",
    )(spectra)


def stack_kernel(count, block_of, source_of, scale_ref, masks_ref, table_ref, recv_ref, *rest):
    blocks, (o_ref, src, cross) = rest[:-3], rest[-3:]
    columns = recv_ref.shape[1]
    half = recv_ref.shape[2] // 2
    rows = count * COMPS
    for d in range(count):
        which = block_of[source_of[d] // SB]
        station = source_of[d] % SB
        for j in range(len(blocks)):

            @pl.when(which == j)
            def _():
                for a in range(COMPS):
                    src[pl.ds(d * COMPS + a, F, stride=rows), :] = blocks[j][a, station].astype(f32)

    masks = masks_ref[...]

    def one_freq(f, carry):
        plain = src[pl.ds(f * rows, rows), :]
        rolled = pltpu.roll(plain, half, 1)
        left = [plain * masks[0:1], plain * masks[1:2], rolled * masks[2:3], rolled * masks[3:4]]
        left = jnp.concatenate(left, axis=0).astype(bf16)
        out = lax.dot_general(left, recv_ref[f], (((1,), (1,)), ((), ())), preferred_element_type=f32)
        cross[pl.ds(f, G * rows, stride=XS), 0:columns] = out[: G * rows]
        cross[pl.ds(F + f, G * rows, stride=XS), 0:columns] = out[G * rows :]
        return carry

    lax.fori_loop(0, F, one_freq, 0, unroll=4)
    table = table_ref[...]
    part = COMPS * columns
    for d in range(count):
        turned = []
        for g in range(G):
            for a in range(COMPS):
                first = (g * rows + d * COMPS + a) * XS
                turned.append(cross[first : first + 2 * F, :].T[:columns])
        turned = jnp.concatenate(turned, axis=0)
        high = turned.astype(bf16)
        low = (turned - high.astype(f32)).astype(bf16)
        both = jnp.dot(high, table, preferred_element_type=f32)
        lagged = both[:, :LAG] + both[:, LAG:] + jnp.dot(low, table[:, :LAG], preferred_element_type=f32)
        for g in range(G):
            o_ref[d, g * part : (g + 1) * part] = lagged[g * part : (g + 1) * part] * scale_ref[g]


def stacks(source_of, block_of, scale, masks, table, recv, blocks):
    count = source_of.shape[0]
    columns, depth = recv.shape[1:]
    rows = count * COMPS
    return pl.pallas_call(
        functools.partial(stack_kernel, count),
        in_specs=[SMEM, SMEM, SMEM, VMEM, VMEM, VMEM] + [VMEM] * len(blocks),
        out_specs=VMEM,
        out_shape=jax.ShapeDtypeStruct((count, G * COMPS * columns, LAG), f32),
        scratch_shapes=[pltpu.VMEM((F * rows, depth), f32), pltpu.VMEM((G * rows * XS, 128), f32)],
        compiler_params=PARAMS,
        cost_estimate=pl.CostEstimate(flops=0, bytes_accessed=16 << 20, transcendentals=0),
        name="stacks",
    )(block_of, source_of, scale, masks, table, recv, *blocks)


def total_kernel(stations, *refs):
    parts, o_ref = refs[:-1], refs[-1]
    per_station = G * COMPS * COMPS
    for g in range(G):
        for c in range(COMPS * COMPS):
            rows = pl.ds((g * COMPS * COMPS + c) * stations, stations)
            value = parts[0][rows, :]
            for part in parts[1:]:
                value = value + part[rows, :]
            o_ref[pl.ds(c * G + g, stations, stride=per_station), :] = value


def total(parts, stations):
    return pl.pallas_call(
        functools.partial(total_kernel, stations),
        in_specs=[VMEM] * len(parts),
        out_specs=VMEM,
        out_shape=jax.ShapeDtypeStruct(parts[0].shape, f32),
        compiler_params=PARAMS,
        name="total",
    )(*parts)


def swap(value, axis, mask):
    size = lax.axis_size(axis)
    return lax.ppermute(value, axis, [(i, i ^ mask) for i in range(size)])


def owned_block(owner):
    ids = jnp.arange(owner.shape[0], dtype=jnp.int32)
    return jnp.sum(ids[None, :] * (owner[None, :] == ids[:, None]).astype(jnp.int32), axis=1)


def local(spectra, src_block, group_of, owner):
    segs, stations = spectra.shape[0], spectra.shape[3]
    days = lax.axis_size("day")
    day = lax.axis_index("day")
    me = lax.axis_index("sta")
    group_ids = jnp.arange(G, dtype=jnp.int32)
    scale = 1.0 / jnp.sqrt(jnp.sum((group_of[None, :] == group_ids[:, None]).astype(f32), axis=1))
    mine = lax.dynamic_slice_in_dim(group_of, day * segs, segs)
    hot = (mine[None, :] == group_ids[:, None]).astype(f32)
    masks = jnp.concatenate([jnp.concatenate([hot, hot], axis=1), jnp.concatenate([-hot, hot], axis=1)], axis=0)
    table = jnp.asarray(lag_table(F, LAG))
    first = first_block(spectra)
    block_rows = S * stations // days

    if days == S and lax.axis_size("sta") == 4:
        across = swap(first, "sta", 2)
        blocks = [first, swap(first, "sta", 1), across, swap(across, "sta", 1)]
        recv = receivers_by_freq(spectra)
        owned = owned_block(owner)
        block_of = src_block ^ me
        z_masks = 2 * jnp.arange(days // 2, dtype=jnp.int32)
        away = stacks(jnp.take(owned, day ^ 1 ^ z_masks), block_of, scale, masks, table, recv, blocks)
        arrived = swap(away, "day", 1)
        kept = stacks(jnp.take(owned, day ^ z_masks), block_of, scale, masks, table, recv, blocks)
        kept = kept + arrived
        parts = [kept[0]] + [swap(kept[j], "day", 2 * j) for j in range(1, days // 2)]
        result = total(parts, stations)
        result = result.reshape(block_rows, COMPS * COMPS, G, LAG).transpose(0, 2, 1, 3)
        return result[None]

    gathered = lax.all_gather(first, "sta")
    blocks = [lax.dynamic_index_in_dim(gathered, src_block[k], 0, keepdims=False) for k in range(2)]
    recv = receivers_by_freq(spectra)
    every = jnp.arange(S, dtype=jnp.int32)
    partial = stacks(every, jnp.arange(2, dtype=jnp.int32), scale, masks, table, recv, blocks)
    partial = partial.reshape(S, G, COMPS * COMPS, stations, LAG).transpose(0, 3, 1, 2, 4)
    partial = partial.reshape(days, block_rows, G, COMPS * COMPS, LAG)
    ordered = jnp.take(partial, owned_block(owner), axis=0)
    return lax.psum_scatter(ordered, "day", scatter_dimension=0, tiled=True)


def solution(mesh):
    return jax.shard_map(
        local,
        mesh=mesh,
        in_specs=(P("day", None, None, "sta", None), P(), P(), P()),
        out_specs=P("day", "sta", None, None, None),
        check_vma=False,
    )
```

time: 176 us -> 73.3 us (0.42)
  waiting for transfers between devices: 83.5 us -> 29.3 us
  local copies, waits for them, and re-layouts: 40.1 us -> 7.45 us
  matrix products: 25.7 us -> 0 us
  Pallas kernels: 0 us -> 22.1 us
  between operations: 14.9 us -> 0.08 us
  starting transfers between devices: 0.04 us -> 9.31 us
  other arithmetic: 11.6 us -> 4.78 us
    reduce_scatter x1 -> x0, waiting for transfers between devices: 65.4 us -> none  [local(): lax.psum_scatter(result.reshape(block_rows * lax.axis_size('day'), G, 9,...]
    ppermute x0 -> x7, waiting for transfers between devices: none -> 29.3 us  [swap(): return lax.ppermute(value, axis, [(i, i ^ mask) for i in range(size)])]
    dot_general x3 -> x0, matrix products: 25.7 us -> none  [the longest x1 11.9 us: cross_terms(): jnp.einsum('gtpasf,tpbrf->srgabf', weighted, spectra, preferred_element_t...]
    pallas_call x0 -> x5, Pallas kernels: none -> 22.1 us  [the longest x2 18.5 us: stacks(): pl.pallas_call(functools.partial(stack_kernel, count), in_specs=[SMEM, SM...]
    psum x1 -> x0, waiting for transfers between devices: 18.1 us -> none  [from_root(): return lax.psum(kept, axis)]
    dot_general x2 -> x0, local copies, waits for them, and re-layouts: 13.9 us -> none  [the longest x1 7.52 us: cross_terms(): jnp.einsum('gtpasf,tpbrf->srgabf', weighted, spectra, preferred_element_t...]
    ppermute x0 -> x7, starting transfers between devices: none -> 9.31 us  [swap(): return lax.ppermute(value, axis, [(i, i ^ mask) for i in range(size)])]
    unnamed x21 -> x16, local copies, waits for them, and re-layouts: 12.2 us -> 4.85 us
  transfers between devices with their start and end apart: 2 -> 7, of which waited for: 2 -> 5; matrix products, arithmetic and copies ran while one was open for 11% -> 8% of each run, Pallas kernels for 0% -> 15%
where the time goes in v1:
time: 73.3 us; the launch traced here: 73 us
  waiting for transfers between devices  29.3 us (40%)
  Pallas kernels  22.1 us (30%)
  starting transfers between devices  9.31 us (13%)
  local copies, waits for them, and re-layouts  7.45 us (10%)
  other arithmetic  4.78 us (7%)
    ppermute x7, waiting for transfers between devices, swap(): return lax.ppermute(value, axis, [(i, i ^ mask) for i in range(size)])  29.3 us
    pallas_call x2, Pallas kernels, stacks(): pl.pallas_call(functools.partial(stack_kernel, count), in_specs=[SMEM, SM...  18.5 us
    ppermute x7, starting transfers between devices, swap(): return lax.ppermute(value, axis, [(i, i ^ mask) for i in range(size)])  9.31 us
    unnamed x16, local copies, waits for them, and re-layouts  4.85 us
    pallas_call x1, Pallas kernels, receivers_by_freq(): pl.pallas_call(receivers_kernel, grid=(COMPS,), in_specs=[pl.BlockSpec((s...  2.2 us
  transfers between devices with their start and end apart: 7, of which 5 were waited for; matrix products, arithmetic and copies ran while one was open for 8% of the time, Pallas kernels for 15%

profile of v1, /device:TPU:0, one launch (start us, length us, event | category | flops | bytes accessed | tf_op | source)
XLA Modules:
  0.0 73.0 jit_solution(5952930796103173331)
XLA Ops:
  0.0 1.7 %copy-done = bf16[64,2,3,24,128]{4,3,2,1,0:T(8,128)(2,1)S(1)} copy-done((bf16[64,2,3,24,128]{4,3,2,1,0:T(8,128)(2,1)S(1)}, bf16[64,2,3,24,128]{4,3,2,1,0:T(8,128)(2,1)}, u32[]{:S(2)}) %copy-start) | copy-done | bytes 2359320
  1.7 0.6 first_block.1.rest_0_
  2.3 3.0 %collective-permute-start.1 = (bf16[3,4,128,128]{3,2,1,0:T(8,128)(2,1)S(1)}, bf16[3,4,128,128]{3,2,1,0:T(8,128)(2,1)S(1)}, u32[]{:S(2)}, u32[]{:S(2)}) collective-permute-start(bf16[3,4,128,128]{3,2,1,0:T(8,128)(2,1)S(1)} %first_block.1.rest_0_), channel_id=1, source_target_pairs={{0,2},{1,3},{2,0},{3,1},{4,6},{5,7},{6,4},{7,5},{8,10},{9,11},{10,... | collective-permute-start | bytes 1179656 | tf_op jit(solution)/shard_map/ppermute | solution.py:181
  5.3 2.2 %receivers_by_freq.1.recv_ref = bf16[128,72,128]{2,1,0:T(8,128)(2,1)S(1)} custom-call(bf16[64,2,3,24,128]{4,3,2,1,0:T(8,128)(2,1)S(1)} %copy-done), custom_call_target="tpu_custom_call" | custom-call | bytes 12582912 | tf_op jit(solution)/shard_map/receivers_by_freq/pallas_call | solution.py:82
  7.5 0.1 fusion
  7.6 0.1 dynamic_slice.3
  7.7 0.1 select_reduce_fusion
  7.8 0.4 copy-done.7
  8.2 1.2 %gather_fusion.1 = s32[4]{0:T(128)} fusion(s32[8]{0:T(128)S(1)} %select_reduce_fusion, s32[1024]{0:T(1024)S(1)} %pad_clamp_fusion), kind=kCustom, calls=%fused_computation.1.clone | custom fusion | bytes 48 | tf_op jit(solution)/shard_map/jit(_take)/gather | solution.py:210
  9.4 0.7 compare_convert_fusion.1
  10.1 0.1 maximum_maximum_fusion.masks_ref
  10.1 4.3 %collective-permute-done.1.rest_2_ = bf16[3,4,128,128]{3,2,1,0:T(8,128)(2,1)S(1)} collective-permute-done((bf16[3,4,128,128]{3,2,1,0:T(8,128)(2,1)S(1)}, bf16[3,4,128,128]{3,2,1,0:T(8,128)(2,1)S(1)}, u32[]{:S(2)}, u32[]{:S(2)}) %collective-permute-start.1) | collective-permute-done | bytes 393248 | tf_op jit(solution)/shard_map/ppermute | solution.py:181
  14.4 0.6 and_select_fusion.source_of
  15.0 0.7 broadcast_xor_fusion.block_of
  15.7 0.4 collective-permute-done.2.rest_3_
  16.1 0.9 %copy-done.3 = bf16[256,256]{1,0:T(8,128)(2,1)S(1)} copy-done((bf16[256,256]{1,0:T(8,128)(2,1)S(1)}, bf16[256,256]{1,0:T(8,128)(2,1)}, u32[]{:S(2)}) %copy-start.3) | copy-done | bytes 131096
  17.0 9.7 %stacks.3 = f32[4,432,128]{2,1,0:T(8,128)} custom-call(s32[2]{0:T(128)S(1)} %broadcast_xor_fusion.block_of, s32[4]{0:T(128)S(1)} %and_select_fusion.source_of, f32[2]{0:T(128)S(1)} %sqrt.3.scale_ref, f32[4,128]{1,0:T(4,128)S(1)} %maximum_maximum_fusion.masks_ref, bf16[256,256]{1,0:T(8,128)(2,1)S(1)} %copy-done.3, ...), custom_call_target="tpu_custom_call" | custom-call | bytes 16777216 | tf_op jit(solution)/shard_map/stacks/pallas_call | solution.py:144
  26.8 1.8 %collective-permute-start.3 = (f32[4,432,128]{2,1,0:T(8,128)}, f32[4,432,128]{2,1,0:T(8,128)}, u32[]{:S(2)}, u32[]{:S(2)}) collective-permute-start(f32[4,432,128]{2,1,0:T(8,128)} %stacks.3), channel_id=1, source_target_pairs={{0,4},{4,0},{8,12},{12,8},{16,20},{20,16},{24,28},{28,24},{1,5},{5... | collective-permute-start | bytes 2654216 | tf_op jit(solution)/shard_map/ppermute | solution.py:181
  28.5 0.6 pad_clamp_fusion.1
  29.1 1.3 %gather_fusion = s32[4]{0:T(128)} fusion(s32[8]{0:T(128)S(1)} %select_reduce_fusion, s32[1024]{0:T(1024)} %pad_clamp_fusion.1), kind=kCustom, calls=%fused_computation.clone | custom fusion | bytes 48 | tf_op jit(solution)/shard_map/jit(_take)/gather | solution.py:212
  30.4 0.6 and_select_fusion.1.source_of
  31.1 1.0 %copy-done.2 = bf16[3,4,128,128]{3,2,1,0:T(8,128)(2,1)S(1)} copy-done((bf16[3,4,128,128]{3,2,1,0:T(8,128)(2,1)S(1)}, bf16[3,4,128,128]{3,2,1,0:T(8,128)(2,1)}, u32[]{:S(2)}) %copy-start.2) | copy-done | bytes 393240
  32.1 0.9 %copy-done.4 = bf16[256,256]{1,0:T(8,128)(2,1)S(1)} copy-done((bf16[256,256]{1,0:T(8,128)(2,1)S(1)}, bf16[256,256]{1,0:T(8,128)(2,1)}, u32[]{:S(2)}) %copy-start.4) | copy-done | bytes 131096
  33.0 8.8 %stacks.2 = f32[4,432,128]{2,1,0:T(8,128)S(1)} custom-call(s32[2]{0:T(128)S(1)} %broadcast_xor_fusion.block_of, s32[4]{0:T(128)S(1)} %and_select_fusion.1.source_of, f32[2]{0:T(128)S(1)} %sqrt.3.scale_ref, f32[4,128]{1,0:T(4,128)S(1)} %maximum_maximum_fusion.masks_ref, bf16[256,256]{1,0:T(8,128)(2,1)S(1)} %copy-done.4, ...), custom_call_target="tpu_custom_call" | custom-call | bytes 16777216 | tf_op jit(solution)/shard_map/stacks/pallas_call | solution.py:144
  41.7 7.0 %collective-permute-done.3 = f32[4,432,128]{2,1,0:T(8,128)} collective-permute-done((f32[4,432,128]{2,1,0:T(8,128)}, f32[4,432,128]{2,1,0:T(8,128)}, u32[]{:S(2)}, u32[]{:S(2)}) %collective-permute-start.3) | collective-permute-done | bytes 884768 | tf_op jit(solution)/shard_map/ppermute | solution.py:181
  48.8 1.3 %add.10 = f32[4,432,128]{2,1,0:T(8,128)S(1)} add(f32[4,432,128]{2,1,0:T(8,128)S(1)} %stacks.2, f32[4,432,128]{2,1,0:T(8,128)} %collective-permute-done.3) | non-fusion elementwise | flops 221184 | bytes 2654208 | tf_op jit(solution)/shard_map/add | solution.py:213
  50.0 0.1 slice_bitcast_fusion
  50.1 3.9 %collective-permute-start.6 = (f32[432,128]{1,0:T(8,128)S(1)}, f32[432,128]{1,0:T(8,128)S(1)}, u32[]{:S(2)}, u32[]{:S(2)}) collective-permute-start(f32[432,128]{1,0:T(8,128)S(1)} %get-tuple-element.6), channel_id=1, source_target_pairs={{0,24},{4,28},{8,16},{12,20},{16,8},{20,12},{24,0},{28,4},{1,25},{... | collective-permute-start | bytes 663560 | tf_op jit(solution)/shard_map/ppermute | solution.py:181
  54.0 0.6 collective-permute-start.4
  54.6 5.8 %collective-permute-done.6.refs_3_ = f32[432,128]{1,0:T(8,128)S(1)} collective-permute-done((f32[432,128]{1,0:T(8,128)S(1)}, f32[432,128]{1,0:T(8,128)S(1)}, u32[]{:S(2)}, u32[]{:S(2)}) %collective-permute-start.6) | collective-permute-done | bytes 221216 | tf_op jit(solution)/shard_map/ppermute | solution.py:181
  60.4 11.8 %collective-permute-done.5.refs_2_ = f32[432,128]{1,0:T(8,128)S(1)} collective-permute-done((f32[432,128]{1,0:T(8,128)S(1)}, f32[432,128]{1,0:T(8,128)S(1)}, u32[]{:S(2)}, u32[]{:S(2)}) %collective-permute-start.5) | collective-permute-done | bytes 221216 | tf_op jit(solution)/shard_map/ppermute | solution.py:181
  72.3 0.8 %total.1 = f32[432,128]{1,0:T(8,128)} custom-call(f32[432,128]{1,0:T(8,128)S(1)} %get-tuple-element.9.refs_0_, f32[432,128]{1,0:T(8,128)S(1)} %collective-permute-done.4.refs_1_, f32[432,128]{1,0:T(8,128)S(1)} %collective-permute-done.5.refs_2_, f32[432,128]{1,0:T(8,128)S(1)} %collective-permute-done.6.refs_3_), custom_call_target="tpu_custom_call" | custom-call | tf_op jit(solution)/shard_map/total/pallas_call | solution.py:169
  (21 shorter events, 0.1 us)
Async XLA Ops:
  0.0 1.7 %copy-start = (bf16[64,2,3,24,128]{4,3,2,1,0:T(8,128)(2,1)S(1)}, bf16[64,2,3,24,128]{4,3,2,1,0:T(8,128)(2,1)}, u32[]{:S(2)}) copy-start(bf16[64,2,3,24,128]{4,3,2,1,0:T(8,128)(2,1)} %x_ref.3) | copy-start | bytes 7077892
  2.3 12.1 %collective-permute-start.1 = (bf16[3,4,128,128]{3,2,1,0:T(8,128)(2,1)S(1)}, bf16[3,4,128,128]{3,2,1,0:T(8,128)(2,1)S(1)}, u32[]{:S(2)}, u32[]{:S(2)}) collective-permute-start(bf16[3,4,128,128]{3,2,1,0:T(8,128)(2,1)S(1)} %first_block.1.rest_0_), channel_id=1, source_target_pairs={{0,2},{1,3},{2,0},{3,1},{4,6},{5,7},{6,4},{7,5},{8,10},{9,11},{10,... | collective-permute-start | bytes 1179656 | tf_op jit(solution)/shard_map/ppermute | solution.py:181
  5.3 10.4 %collective-permute-start = (bf16[3,4,128,128]{3,2,1,0:T(8,128)(2,1)S(1)}, bf16[3,4,128,128]{3,2,1,0:T(8,128)(2,1)S(1)}, u32[]{:S(2)}, u32[]{:S(2)}) collective-permute-start(bf16[3,4,128,128]{3,2,1,0:T(8,128)(2,1)S(1)} %first_block.1.rest_0_), channel_id=1, source_target_pairs={{0,1},{1,0},{2,3},{3,2},{4,5},{5,4},{6,7},{7,6},{8,9},{9,8},{10,11... | collective-permute-start | bytes 1179656 | tf_op jit(solution)/shard_map/ppermute | solution.py:181
  5.3 2.2 %copy-start.5 = (s32[512]{0:T(512)S(1)}, s32[512]{0:T(512)}, u32[]{:S(2)}) copy-start(s32[512]{0:T(512)} %param.9) | copy-start | bytes 6148
  5.3 2.4 %copy-start.6 = (s32[8]{0:T(128)S(1)}, s32[8]{0:T(128)}, u32[]{:S(2)}) copy-start(s32[8]{0:T(128)} %param.10) | copy-start | bytes 100
  7.7 0.5 copy-start.7
  14.4 1.7 %collective-permute-start.2 = (bf16[3,4,128,128]{3,2,1,0:T(8,128)(2,1)S(1)}, bf16[3,4,128,128]{3,2,1,0:T(8,128)(2,1)S(1)}, u32[]{:S(2)}, u32[]{:S(2)}) collective-permute-start(bf16[3,4,128,128]{3,2,1,0:T(8,128)(2,1)S(1)} %collective-permute-done.1.rest_2_), channel_id=1, source_target_pairs={{0,1},{1,0},{2,3},{3,2},{4,5},{5,4},{6,7},{7,6},{8,9},{9,8},{10,11... | collective-permute-start | bytes 1179656 | tf_op jit(solution)/shard_map/ppermute | solution.py:181
  16.1 0.9 %copy-start.3 = (bf16[256,256]{1,0:T(8,128)(2,1)S(1)}, bf16[256,256]{1,0:T(8,128)(2,1)}, u32[]{:S(2)}) copy-start(bf16[256,256]{1,0:T(8,128)(2,1)} %constant.35.clone.table_ref) | copy-start | bytes 393220
  17.0 9.7 %copy-start.1 = (bf16[3,4,128,128]{3,2,1,0:T(8,128)(2,1)}, bf16[3,4,128,128]{3,2,1,0:T(8,128)(2,1)S(1)}, u32[]{:S(2)}) copy-start(bf16[3,4,128,128]{3,2,1,0:T(8,128)(2,1)S(1)} %collective-permute-done.2.rest_3_) | copy-start | bytes 1179652
  26.8 22.0 %collective-permute-start.3 = (f32[4,432,128]{2,1,0:T(8,128)}, f32[4,432,128]{2,1,0:T(8,128)}, u32[]{:S(2)}, u32[]{:S(2)}) collective-permute-start(f32[4,432,128]{2,1,0:T(8,128)} %stacks.3), channel_id=1, source_target_pairs={{0,4},{4,0},{8,12},{12,8},{16,20},{20,16},{24,28},{28,24},{1,5},{5... | collective-permute-start | bytes 2654216 | tf_op jit(solution)/shard_map/ppermute | solution.py:181
  31.1 1.0 %copy-start.2 = (bf16[3,4,128,128]{3,2,1,0:T(8,128)(2,1)S(1)}, bf16[3,4,128,128]{3,2,1,0:T(8,128)(2,1)}, u32[]{:S(2)}) copy-start(bf16[3,4,128,128]{3,2,1,0:T(8,128)(2,1)} %copy-done.1) | copy-start | bytes 1179652
  32.1 0.9 %copy-start.4 = (bf16[256,256]{1,0:T(8,128)(2,1)S(1)}, bf16[256,256]{1,0:T(8,128)(2,1)}, u32[]{:S(2)}) copy-start(bf16[256,256]{1,0:T(8,128)(2,1)} %constant.35.clone.table_ref) | copy-start | bytes 393220
  50.1 10.3 %collective-permute-start.6 = (f32[432,128]{1,0:T(8,128)S(1)}, f32[432,128]{1,0:T(8,128)S(1)}, u32[]{:S(2)}, u32[]{:S(2)}) collective-permute-start(f32[432,128]{1,0:T(8,128)S(1)} %get-tuple-element.6), channel_id=1, source_target_pairs={{0,24},{4,28},{8,16},{12,20},{16,8},{20,12},{24,0},{28,4},{1,25},{... | collective-permute-start | bytes 663560 | tf_op jit(solution)/shard_map/ppermute | solution.py:181
  54.0 18.3 %collective-permute-start.5 = (f32[432,128]{1,0:T(8,128)S(1)}, f32[432,128]{1,0:T(8,128)S(1)}, u32[]{:S(2)}, u32[]{:S(2)}) collective-permute-start(f32[432,128]{1,0:T(8,128)S(1)} %get-tuple-element.7), channel_id=1, source_target_pairs={{0,16},{4,20},{8,24},{12,28},{16,0},{20,4},{24,8},{28,12},{1,17},{... | collective-permute-start | bytes 663560 | tf_op jit(solution)/shard_map/ppermute | solution.py:181
  54.0 18.3 %collective-permute-start.4 = (f32[432,128]{1,0:T(8,128)S(1)}, f32[432,128]{1,0:T(8,128)S(1)}, u32[]{:S(2)}, u32[]{:S(2)}) collective-permute-start(f32[432,128]{1,0:T(8,128)S(1)} %get-tuple-element.8), channel_id=1, source_target_pairs={{0,8},{4,12},{8,0},{12,4},{16,24},{20,28},{24,16},{28,20},{1,9},{5... | collective-permute-start | bytes 663560 | tf_op jit(solution)/shard_map/ppermute | solution.py:181

commit v2 on v1

--- a/solution.py
+++ b/solution.py
@@ -18,6 +18,8 @@
 
 f32 = jnp.float32
 bf16 = jnp.bfloat16
+f16 = jnp.float16
+TOP = 14
 PARAMS = pltpu.CompilerParams(vmem_limit_bytes=48 << 20)
 VMEM = pl.BlockSpec(memory_space=pltpu.VMEM)
 SMEM = pl.BlockSpec(memory_space=pltpu.SMEM)
@@ -92,14 +94,33 @@
     )(spectra)
 
 
-def stack_kernel(count, block_of, source_of, scale_ref, masks_ref, table_ref, recv_ref, *rest):
+def power_of_two(n):
+    size = jnp.abs(n)
+    result = jnp.ones(n.shape, f32)
+    for i in range(7):
+        factor = jnp.where(n < 0, np.float32(2.0 ** -(2**i)), np.float32(2.0 ** (2**i)))
+        result = result * jnp.where((size >> i) & 1 == 1, factor, np.float32(1.0))
+    return result
+
+
+def exponent_of(value):
+    largest = jnp.max(jnp.abs(value), axis=(0, 1), keepdims=True)
+    return jnp.ceil(jnp.log(jnp.maximum(largest, 1e-30)) * np.float32(1.4426950408889634)).astype(jnp.int32)
+
+
+def stack_kernel(masks, coded, ids_ref, src_block_ref, owner_ref, scale_ref, masks_ref, table_ref, recv_ref, *rest):
     blocks, (o_ref, src, cross) = rest[:-3], rest[-3:]
+    count = len(masks)
     columns = recv_ref.shape[1]
     half = recv_ref.shape[2] // 2
     rows = count * COMPS
     for d in range(count):
-        which = block_of[source_of[d] // SB]
-        station = source_of[d] % SB
+        dest = ids_ref[0] ^ masks[d]
+        source = jnp.int32(0)
+        for k in range(S):
+            source = source + jnp.where(owner_ref[k] == dest, k, 0)
+        which = ids_ref[1] ^ src_block_ref[source // SB]
+        station = source % SB
         for j in range(len(blocks)):
 
             @pl.when(which == j)
@@ -107,21 +128,22 @@
                 for a in range(COMPS):
                     src[pl.ds(d * COMPS + a, F, stride=rows), :] = blocks[j][a, station].astype(f32)
 
-    masks = masks_ref[...]
+    signs = masks_ref[...]
 
     def one_freq(f, carry):
         plain = src[pl.ds(f * rows, rows), :]
         rolled = pltpu.roll(plain, half, 1)
-        left = [plain * masks[0:1], plain * masks[1:2], rolled * masks[2:3], rolled * masks[3:4]]
+        left = [plain * signs[0:1], plain * signs[1:2], rolled * signs[2:3], rolled * signs[3:4]]
         left = jnp.concatenate(left, axis=0).astype(bf16)
         out = lax.dot_general(left, recv_ref[f], (((1,), (1,)), ((), ())), preferred_element_type=f32)
         cross[pl.ds(f, G * rows, stride=XS), 0:columns] = out[: G * rows]
         cross[pl.ds(F + f, G * rows, stride=XS), 0:columns] = out[G * rows :]
         return carry
 
-    lax.fori_loop(0, F, one_freq, 0, unroll=4)
+    lax.fori_loop(0, F, one_freq, 0, unroll=32)
     table = table_ref[...]
     part = COMPS * columns
+    exponents = jnp.zeros((16, LAG), f32)
     for d in range(count):
         turned = []
         for g in range(G):
@@ -133,47 +155,85 @@
         low = (turned - high.astype(f32)).astype(bf16)
         both = jnp.dot(high, table, preferred_element_type=f32)
         lagged = both[:, :LAG] + both[:, LAG:] + jnp.dot(low, table[:, :LAG], preferred_element_type=f32)
-        for g in range(G):
-            o_ref[d, g * part : (g + 1) * part] = lagged[g * part : (g + 1) * part] * scale_ref[g]
-
-
-def stacks(source_of, block_of, scale, masks, table, recv, blocks):
-    count = source_of.shape[0]
+        lagged = jnp.concatenate([lagged[g * part : (g + 1) * part] * scale_ref[g] for g in range(G)], axis=0)
+        if coded:
+            e = exponent_of(lagged)
+            lagged = lagged * power_of_two(TOP - e)
+            exponents = jnp.where(lax.broadcasted_iota(jnp.int32, (16, LAG), 0) == d, e.astype(f32), exponents)
+        o_ref[d * G * part : (d + 1) * G * part] = lagged
+    if coded:
+        o_ref[count * G * part :] = exponents
+
+
+def stacks(masks, coded, ids, src_block, owner, scale, signs, table, recv, blocks):
+    count = len(masks)
     columns, depth = recv.shape[1:]
     rows = count * COMPS
-    return pl.pallas_call(
-        functools.partial(stack_kernel, count),
-        in_specs=[SMEM, SMEM, SMEM, VMEM, VMEM, VMEM] + [VMEM] * len(blocks),
+    out_rows = count * G * COMPS * columns + (16 if coded else 0)
+    return pl.pallas_call(
+        functools.partial(stack_kernel, masks, coded),
+        in_specs=[SMEM] * 4 + [VMEM] * 3 + [VMEM] * len(blocks),
         out_specs=VMEM,
-        out_shape=jax.ShapeDtypeStruct((count, G * COMPS * columns, LAG), f32),
+        out_shape=jax.ShapeDtypeStruct((out_rows, LAG), f32),
         scratch_shapes=[pltpu.VMEM((F * rows, depth), f32), pltpu.VMEM((G * rows * XS, 128), f32)],
         compiler_params=PARAMS,
         cost_estimate=pl.CostEstimate(flops=0, bytes_accessed=16 << 20, transcendentals=0),
         name="stacks",
-    )(block_of, source_of, scale, masks, table, recv, *blocks)
-
-
-def total_kernel(stations, *refs):
+    )(ids, src_block, owner, scale, signs, table, recv, *blocks)
+
+
+def merge_kernel(kept_ref, arrived_ref, own_ref, *out_refs):
+    size = own_ref.shape[0]
+    count = len(out_refs) + 1
+    tail = arrived_ref[count * size : count * size + 8]
+    for j in range(count):
+        back = power_of_two(tail[j : j + 1, 0:1].astype(jnp.int32) - TOP)
+        rows = slice(j * size, (j + 1) * size)
+        value = kept_ref[rows] + arrived_ref[rows] * back
+        if j == 0:
+            own_ref[...] = value
+        else:
+            e = exponent_of(value)
+            out_refs[j - 1][0:size] = value * power_of_two(TOP - e)
+            out_refs[j - 1][size:] = jnp.broadcast_to(e.astype(f32), (16, LAG))
+
+
+def merge(kept, arrived, count):
+    size = kept.shape[0] // count
+    coded = jax.ShapeDtypeStruct((size + 16, LAG), f32)
+    return pl.pallas_call(
+        merge_kernel,
+        in_specs=[VMEM] * 2,
+        out_specs=[VMEM] * count,
+        out_shape=[jax.ShapeDtypeStruct((size, LAG), f32)] + [coded] * (count - 1),
+        compiler_params=PARAMS,
+        name="merge",
+    )(kept, arrived)
+
+
+def total_kernel(stations, own_ref, *refs):
     parts, o_ref = refs[:-1], refs[-1]
     per_station = G * COMPS * COMPS
+    size = own_ref.shape[0]
+    back = [power_of_two(part[size : size + 1, 0:1].astype(jnp.int32) - TOP) for part in parts]
     for g in range(G):
         for c in range(COMPS * COMPS):
             rows = pl.ds((g * COMPS * COMPS + c) * stations, stations)
-            value = parts[0][rows, :]
-            for part in parts[1:]:
-                value = value + part[rows, :]
+            value = own_ref[rows, :]
+            for part, factor in zip(parts, back):
+                value = value + part[rows, :] * factor
             o_ref[pl.ds(c * G + g, stations, stride=per_station), :] = value
 
 
-def total(parts, stations):
+def total(own, parts, stations):
     return pl.pallas_call(
         functools.partial(total_kernel, stations),
-        in_specs=[VMEM] * len(parts),
+        in_specs=[VMEM] * (1 + len(parts)),
         out_specs=VMEM,
-        out_shape=jax.ShapeDtypeStruct(parts[0].shape, f32),
+        out_shape=jax.ShapeDtypeStruct(own.shape, f32),
         compiler_params=PARAMS,
         name="total",
-    )(*parts)
+    )(own, *parts)
 
 
 def swap(value, axis, mask):
@@ -195,7 +255,7 @@
     scale = 1.0 / jnp.sqrt(jnp.sum((group_of[None, :] == group_ids[:, None]).astype(f32), axis=1))
     mine = lax.dynamic_slice_in_dim(group_of, day * segs, segs)
     hot = (mine[None, :] == group_ids[:, None]).astype(f32)
-    masks = jnp.concatenate([jnp.concatenate([hot, hot], axis=1), jnp.concatenate([-hot, hot], axis=1)], axis=0)
+    signs = jnp.concatenate([jnp.concatenate([hot, hot], axis=1), jnp.concatenate([-hot, hot], axis=1)], axis=0)
     table = jnp.asarray(lag_table(F, LAG))
     first = first_block(spectra)
     block_rows = S * stations // days
@@ -204,15 +264,15 @@
         across = swap(first, "sta", 2)
         blocks = [first, swap(first, "sta", 1), across, swap(across, "sta", 1)]
         recv = receivers_by_freq(spectra)
-        owned = owned_block(owner)
-        block_of = src_block ^ me
-        z_masks = 2 * jnp.arange(days // 2, dtype=jnp.int32)
-        away = stacks(jnp.take(owned, day ^ 1 ^ z_masks), block_of, scale, masks, table, recv, blocks)
-        arrived = swap(away, "day", 1)
-        kept = stacks(jnp.take(owned, day ^ z_masks), block_of, scale, masks, table, recv, blocks)
-        kept = kept + arrived
-        parts = [kept[0]] + [swap(kept[j], "day", 2 * j) for j in range(1, days // 2)]
-        result = total(parts, stations)
+        ids = jnp.stack([day, me])
+        masks = range(0, days, 2)
+        operands = (ids, src_block, owner, scale, signs, table, recv, blocks)
+        away = stacks([1 ^ mask for mask in masks], True, *operands)
+        arrived = swap(away.astype(f16), "day", 1)
+        kept = stacks(masks, False, *operands)
+        own, *others = merge(kept, arrived.astype(f32), len(masks))
+        parts = [swap(other.astype(f16), "day", mask).astype(f32) for other, mask in zip(others, masks[1:])]
+        result = total(own, parts, stations)
         result = result.reshape(block_rows, COMPS * COMPS, G, LAG).transpose(0, 2, 1, 3)
         return result[None]
 
@@ -220,7 +280,7 @@
     blocks = [lax.dynamic_index_in_dim(gathered, src_block[k], 0, keepdims=False) for k in range(2)]
     recv = receivers_by_freq(spectra)
     every = jnp.arange(S, dtype=jnp.int32)
-    partial = stacks(every, jnp.arange(2, dtype=jnp.int32), scale, masks, table, recv, blocks)
+    partial = stacks(range(S), False, jnp.zeros(2, jnp.int32), every[:2], every, scale, signs, table, recv, blocks)
     partial = partial.reshape(S, G, COMPS * COMPS, stations, LAG).transpose(0, 3, 1, 2, 4)
     partial = partial.reshape(days, block_rows, G, COMPS * COMPS, LAG)
     ordered = jnp.take(partial, owned_block(owner), axis=0)

time: 73.3 us -> 48.6 us (0.66)
  Pallas kernels: 22.1 us -> 12.5 us
  waiting for transfers between devices: 29.3 us -> 23.2 us
  local copies, waits for them, and re-layouts: 7.45 us -> 2.66 us
  other arithmetic: 4.78 us -> 0.51 us
    pallas_call x2 -> x3, Pallas kernels: 18.5 us -> 8.94 us  [the longest x2 8.38 us: stacks(): pl.pallas_call(functools.partial(stack_kernel, masks, coded), in_specs=[S...]
    ppermute x7, waiting for transfers between devices: 29.3 us -> 23.2 us  [swap(): return lax.ppermute(value, axis, [(i, i ^ mask) for i in range(size)])]
    gather x2 -> x0, local copies, waits for them, and re-layouts: 2.46 us -> none  [the longest x1 1.29 us: local(): jnp.take(owned, day ^ z_masks)]
    unnamed x16 -> x10, local copies, waits for them, and re-layouts: 4.85 us -> 2.58 us
    select_n x4 -> x0, other arithmetic: 1.28 us -> none  [the longest x2 0.64 us: local(): jnp.take(owned, day ^ z_masks)]
    add x1 -> x0, other arithmetic: 1.26 us -> none  [local(): kept = kept + arrived]
  transfers between devices with their start and end apart: 7 -> 7, of which waited for: 5 -> 5; matrix products, arithmetic and copies ran while one was open for 8% -> 1% of each run, Pallas kernels for 15% -> 13%
where the time goes in v2:
time: 48.6 us; the launch traced here: 48.4 us
  waiting for transfers between devices  23.2 us (48%)
  Pallas kernels  12.5 us (26%)
  starting transfers between devices  9.43 us (19%)
  local copies, waits for them, and re-layouts  2.66 us (5%)
  other arithmetic  0.51 us (1%)
    ppermute x7, waiting for transfers between devices, swap(): return lax.ppermute(value, axis, [(i, i ^ mask) for i in range(size)])  23.2 us
    ppermute x7, starting transfers between devices, swap(): return lax.ppermute(value, axis, [(i, i ^ mask) for i in range(size)])  9.43 us
    pallas_call x2, Pallas kernels, stacks(): pl.pallas_call(functools.partial(stack_kernel, masks, coded), in_specs=[S...  8.38 us
    unnamed x10, local copies, waits for them, and re-layouts  2.58 us
    pallas_call x1, Pallas kernels, receivers_by_freq(): pl.pallas_call(receivers_kernel, grid=(COMPS,), in_specs=[pl.BlockSpec((s...  2.21 us
  transfers between devices with their start and end apart: 7, of which 5 were waited for; matrix products, arithmetic and copies ran while one was open for 1% of the time, Pallas kernels for 13%

profile of v2, /device:TPU:0, one launch (start us, length us, event | category | flops | bytes accessed | tf_op | source)
XLA Modules:
  0.0 48.4 jit_solution(892824593226079423)
XLA Ops:
  0.0 0.0 copy-start
  0.0 1.7 %copy-done = bf16[64,2,3,24,128]{4,3,2,1,0:T(8,128)(2,1)S(1)} copy-done((bf16[64,2,3,24,128]{4,3,2,1,0:T(8,128)(2,1)S(1)}, bf16[64,2,3,24,128]{4,3,2,1,0:T(8,128)(2,1)}, u32[]{:S(2)}) %copy-start) | copy-done | bytes 2359320
  1.7 0.6 %first_block.1.rest_0_ = bf16[3,4,128,128]{3,2,1,0:T(8,128)(2,1)S(1)} custom-call(bf16[64,2,3,24,128]{4,3,2,1,0:T(8,128)(2,1)S(1)} %copy-done), custom_call_target="tpu_custom_call" | custom-call | tf_op jit(solution)/shard_map/first_block/pallas_call | solution.py:50
  2.3 3.0 %collective-permute-start.1 = (bf16[3,4,128,128]{3,2,1,0:T(8,128)(2,1)S(1)}, bf16[3,4,128,128]{3,2,1,0:T(8,128)(2,1)S(1)}, u32[]{:S(2)}, u32[]{:S(2)}) collective-permute-start(bf16[3,4,128,128]{3,2,1,0:T(8,128)(2,1)S(1)} %first_block.1.rest_0_), channel_id=1, source_target_pairs={{0,2},{1,3},{2,0},{3,1},{4,6},{5,7},{6,4},{7,5},{8,10},{9,11},{10,... | collective-permute-start | bytes 1179656 | tf_op jit(solution)/shard_map/ppermute | solution.py:241
  5.3 0.0 collective-permute-start
  5.3 2.2 %receivers_by_freq.1.recv_ref = bf16[128,72,128]{2,1,0:T(8,128)(2,1)S(1)} custom-call(bf16[64,2,3,24,128]{4,3,2,1,0:T(8,128)(2,1)S(1)} %copy-done), custom_call_target="tpu_custom_call" | custom-call | bytes 12582912 | tf_op jit(solution)/shard_map/receivers_by_freq/pallas_call | solution.py:84
  7.5 0.0 copy-done.4
  7.5 0.1 dynamic_slice.3
  7.6 0.1 fusion
  7.7 6.7 %collective-permute-done.1.rest_2_ = bf16[3,4,128,128]{3,2,1,0:T(8,128)(2,1)S(1)} collective-permute-done((bf16[3,4,128,128]{3,2,1,0:T(8,128)(2,1)S(1)}, bf16[3,4,128,128]{3,2,1,0:T(8,128)(2,1)S(1)}, u32[]{:S(2)}, u32[]{:S(2)}) %collective-permute-start.1) | collective-permute-done | bytes 393248 | tf_op jit(solution)/shard_map/ppermute | solution.py:241
  14.4 0.0 collective-permute-start.2
  14.4 0.1 pad_add_fusion.ids_ref
  14.5 0.1 maximum_maximum_fusion.masks_ref
  14.6 0.0 collective-permute-done.rest_1_
  14.6 1.6 %collective-permute-done.2.rest_3_ = bf16[3,4,128,128]{3,2,1,0:T(8,128)(2,1)S(1)} collective-permute-done((bf16[3,4,128,128]{3,2,1,0:T(8,128)(2,1)S(1)}, bf16[3,4,128,128]{3,2,1,0:T(8,128)(2,1)S(1)}, u32[]{:S(2)}, u32[]{:S(2)}) %collective-permute-start.2) | collective-permute-done | bytes 393248 | tf_op jit(solution)/shard_map/ppermute | solution.py:241
  16.1 0.0 copy-done.2
  16.1 0.0 copy-done.3
  16.1 0.9 %copy-done.1 = bf16[256,256]{1,0:T(8,128)(2,1)S(1)} copy-done((bf16[256,256]{1,0:T(8,128)(2,1)S(1)}, bf16[256,256]{1,0:T(8,128)(2,1)}, u32[]{:S(2)}) %copy-start.1) | copy-done | bytes 131096
  17.0 4.4 %stacks.3 = f32[1744,128]{1,0:T(8,128)S(1)} custom-call(s32[2]{0:T(128)S(1)} %pad_add_fusion.ids_ref, s32[2]{0:T(128)S(1)} %copy-done.2, s32[8]{0:T(128)S(1)} %copy-done.3, f32[2]{0:T(128)S(1)} %sqrt.3.scale_ref, f32[4,128]{1,0:T(4,128)S(1)} %maximum_maximum_fusion.masks_ref, bf16[256,256]{1,0:T(8,128)(2,1)S(1)} %copy-done.1, ...), custom_call_target="tpu_custom_call" | custom-call | bytes 16777216 | tf_op jit(solution)/shard_map/stacks/pallas_call | solution.py:173
  21.4 0.1 convert_element_type.32
  21.5 1.8 %collective-permute-start.3 = (f16[1744,128]{1,0:T(8,128)(2,1)S(1)}, f16[1744,128]{1,0:T(8,128)(2,1)S(1)}, u32[]{:S(2)}, u32[]{:S(2)}) collective-permute-start(f16[1744,128]{1,0:T(8,128)(2,1)S(1)} %convert_element_type.32), channel_id=1, source_target_pairs={{0,4},{4,0},{8,12},{12,8},{16,20},{20,16},{24,28},{28,24},{1,5},{5... | collective-permute-start | bytes 1339400 | tf_op jit(solution)/shard_map/ppermute | solution.py:241
  23.3 4.0 %stacks.2.kept_ref = f32[1728,128]{1,0:T(8,128)S(1)} custom-call(s32[2]{0:T(128)S(1)} %pad_add_fusion.ids_ref, s32[2]{0:T(128)S(1)} %copy-done.2, s32[8]{0:T(128)S(1)} %copy-done.3, f32[2]{0:T(128)S(1)} %sqrt.3.scale_ref, f32[4,128]{1,0:T(4,128)S(1)} %maximum_maximum_fusion.masks_ref, bf16[256,256]{1,0:T(8,128)(2,1)S(1)} %copy-done.1, ...), custom_call_target="tpu_custom_call" | custom-call | bytes 16777216 | tf_op jit(solution)/shard_map/stacks/pallas_call | solution.py:173
  27.3 6.6 %collective-permute-done.3 = f16[1744,128]{1,0:T(8,128)(2,1)S(1)} collective-permute-done((f16[1744,128]{1,0:T(8,128)(2,1)S(1)}, f16[1744,128]{1,0:T(8,128)(2,1)S(1)}, u32[]{:S(2)}, u32[]{:S(2)}) %collective-permute-start.3) | collective-permute-done | bytes 446496 | tf_op jit(solution)/shard_map/ppermute | solution.py:241
  33.9 0.1 convert_element_type.33.arrived_ref
  34.0 0.6 %merge.1 = (f32[432,128]{1,0:T(8,128)S(1)}, f32[448,128]{1,0:T(8,128)S(1)}, f32[448,128]{1,0:T(8,128)S(1)}, f32[448,128]{1,0:T(8,128)S(1)}) custom-call(f32[1728,128]{1,0:T(8,128)S(1)} %stacks.2.kept_ref, f32[1744,128]{1,0:T(8,128)S(1)} %convert_element_type.33.arrived_ref), custom_call_target="tpu_custom_call" | custom-call | tf_op jit(solution)/shard_map/merge/pallas_call | solution.py:204
  34.6 3.9 %collective-permute-start.6 = (f16[448,128]{1,0:T(8,128)(2,1)S(1)}, f16[448,128]{1,0:T(8,128)(2,1)S(1)}, u32[]{:S(2)}, u32[]{:S(2)}) collective-permute-start(f16[448,128]{1,0:T(8,128)(2,1)S(1)} %convert_element_type.38), channel_id=1, source_target_pairs={{0,24},{4,28},{8,16},{12,20},{16,8},{20,12},{24,0},{28,4},{1,25},{... | collective-permute-start | bytes 344072 | tf_op jit(solution)/shard_map/ppermute | solution.py:241
  38.5 0.0 collective-permute-start.5
  38.5 0.7 %collective-permute-start.4 = (f16[448,128]{1,0:T(8,128)(2,1)S(1)}, f16[448,128]{1,0:T(8,128)(2,1)S(1)}, u32[]{:S(2)}, u32[]{:S(2)}) collective-permute-start(f16[448,128]{1,0:T(8,128)(2,1)S(1)} %convert_element_type.34), channel_id=1, source_target_pairs={{0,8},{4,12},{8,0},{12,4},{16,24},{20,28},{24,16},{28,20},{1,9},{5... | collective-permute-start | bytes 344072 | tf_op jit(solution)/shard_map/ppermute | solution.py:241
  39.2 3.4 %collective-permute-done.6 = f16[448,128]{1,0:T(8,128)(2,1)S(1)} collective-permute-done((f16[448,128]{1,0:T(8,128)(2,1)S(1)}, f16[448,128]{1,0:T(8,128)(2,1)S(1)}, u32[]{:S(2)}, u32[]{:S(2)}) %collective-permute-start.6) | collective-permute-done | bytes 114720 | tf_op jit(solution)/shard_map/ppermute | solution.py:241
  42.6 5.0 %collective-permute-done.5 = f16[448,128]{1,0:T(8,128)(2,1)S(1)} collective-permute-done((f16[448,128]{1,0:T(8,128)(2,1)S(1)}, f16[448,128]{1,0:T(8,128)(2,1)S(1)}, u32[]{:S(2)}, u32[]{:S(2)}) %collective-permute-start.5) | collective-permute-done | bytes 114720 | tf_op jit(solution)/shard_map/ppermute | solution.py:241
  47.6 0.0 collective-permute-done.4
  47.7 0.8 %total.1 = f32[432,128]{1,0:T(8,128)} custom-call(f32[432,128]{1,0:T(8,128)S(1)} %get-tuple-element.9.own_ref, f32[448,128]{1,0:T(8,128)S(1)} %convert_element_type.35.refs_0_, f32[448,128]{1,0:T(8,128)S(1)} %convert_element_type.37.refs_1_, f32[448,128]{1,0:T(8,128)S(1)} %convert_element_type.39.refs_2_), custom_call_target="tpu_custom_call" | custom-call | tf_op jit(solution)/shard_map/total/pallas_call | solution.py:229
  (13 shorter events, 0.1 us)
Async XLA Ops:
  0.0 1.7 %copy-start = (bf16[64,2,3,24,128]{4,3,2,1,0:T(8,128)(2,1)S(1)}, bf16[64,2,3,24,128]{4,3,2,1,0:T(8,128)(2,1)}, u32[]{:S(2)}) copy-start(bf16[64,2,3,24,128]{4,3,2,1,0:T(8,128)(2,1)} %x_ref.3) | copy-start | bytes 7077892
  2.3 12.1 %collective-permute-start.1 = (bf16[3,4,128,128]{3,2,1,0:T(8,128)(2,1)S(1)}, bf16[3,4,128,128]{3,2,1,0:T(8,128)(2,1)S(1)}, u32[]{:S(2)}, u32[]{:S(2)}) collective-permute-start(bf16[3,4,128,128]{3,2,1,0:T(8,128)(2,1)S(1)} %first_block.1.rest_0_), channel_id=1, source_target_pairs={{0,2},{1,3},{2,0},{3,1},{4,6},{5,7},{6,4},{7,5},{8,10},{9,11},{10,... | collective-permute-start | bytes 1179656 | tf_op jit(solution)/shard_map/ppermute | solution.py:241
  5.3 9.3 %collective-permute-start = (bf16[3,4,128,128]{3,2,1,0:T(8,128)(2,1)S(1)}, bf16[3,4,128,128]{3,2,1,0:T(8,128)(2,1)S(1)}, u32[]{:S(2)}, u32[]{:S(2)}) collective-permute-start(bf16[3,4,128,128]{3,2,1,0:T(8,128)(2,1)S(1)} %first_block.1.rest_0_), channel_id=1, source_target_pairs={{0,1},{1,0},{2,3},{3,2},{4,5},{5,4},{6,7},{7,6},{8,9},{9,8},{10,11... | collective-permute-start | bytes 1179656 | tf_op jit(solution)/shard_map/ppermute | solution.py:241
  5.3 2.2 %copy-start.4 = (s32[512]{0:T(512)S(1)}, s32[512]{0:T(512)}, u32[]{:S(2)}) copy-start(s32[512]{0:T(512)} %param.7) | copy-start | bytes 6148
  5.3 10.8 %copy-start.2 = (s32[2]{0:T(128)S(1)}, s32[2]{0:T(128)}, u32[]{:S(2)}) copy-start(s32[2]{0:T(128)} %src_block_ref.3) | copy-start | bytes 28
  5.3 10.8 %copy-start.3 = (s32[8]{0:T(128)S(1)}, s32[8]{0:T(128)}, u32[]{:S(2)}) copy-start(s32[8]{0:T(128)} %owner_ref.3) | copy-start | bytes 100
  14.4 1.7 %collective-permute-start.2 = (bf16[3,4,128,128]{3,2,1,0:T(8,128)(2,1)S(1)}, bf16[3,4,128,128]{3,2,1,0:T(8,128)(2,1)S(1)}, u32[]{:S(2)}, u32[]{:S(2)}) collective-permute-start(bf16[3,4,128,128]{3,2,1,0:T(8,128)(2,1)S(1)} %collective-permute-done.1.rest_2_), channel_id=1, source_target_pairs={{0,1},{1,0},{2,3},{3,2},{4,5},{5,4},{6,7},{7,6},{8,9},{9,8},{10,11... | collective-permute-start | bytes 1179656 | tf_op jit(solution)/shard_map/ppermute | solution.py:241
  16.1 0.9 %copy-start.1 = (bf16[256,256]{1,0:T(8,128)(2,1)S(1)}, bf16[256,256]{1,0:T(8,128)(2,1)}, u32[]{:S(2)}) copy-start(bf16[256,256]{1,0:T(8,128)(2,1)} %constant.20.clone.table_ref) | copy-start | bytes 393220
  21.5 12.4 %collective-permute-start.3 = (f16[1744,128]{1,0:T(8,128)(2,1)S(1)}, f16[1744,128]{1,0:T(8,128)(2,1)S(1)}, u32[]{:S(2)}, u32[]{:S(2)}) collective-permute-start(f16[1744,128]{1,0:T(8,128)(2,1)S(1)} %convert_element_type.32), channel_id=1, source_target_pairs={{0,4},{4,0},{8,12},{12,8},{16,20},{20,16},{24,28},{28,24},{1,5},{5... | collective-permute-start | bytes 1339400 | tf_op jit(solution)/shard_map/ppermute | solution.py:241
  34.6 8.0 %collective-permute-start.6 = (f16[448,128]{1,0:T(8,128)(2,1)S(1)}, f16[448,128]{1,0:T(8,128)(2,1)S(1)}, u32[]{:S(2)}, u32[]{:S(2)}) collective-permute-start(f16[448,128]{1,0:T(8,128)(2,1)S(1)} %convert_element_type.38), channel_id=1, source_target_pairs={{0,24},{4,28},{8,16},{12,20},{16,8},{20,12},{24,0},{28,4},{1,25},{... | collective-permute-start | bytes 344072 | tf_op jit(solution)/shard_map/ppermute | solution.py:241
  38.5 9.1 %collective-permute-start.5 = (f16[448,128]{1,0:T(8,128)(2,1)S(1)}, f16[448,128]{1,0:T(8,128)(2,1)S(1)}, u32[]{:S(2)}, u32[]{:S(2)}) collective-permute-start(f16[448,128]{1,0:T(8,128)(2,1)S(1)} %convert_element_type.36), channel_id=1, source_target_pairs={{0,16},{4,20},{8,24},{12,28},{16,0},{20,4},{24,8},{28,12},{1,17},{... | collective-permute-start | bytes 344072 | tf_op jit(solution)/shard_map/ppermute | solution.py:241
  38.5 9.1 %collective-permute-start.4 = (f16[448,128]{1,0:T(8,128)(2,1)S(1)}, f16[448,128]{1,0:T(8,128)(2,1)S(1)}, u32[]{:S(2)}, u32[]{:S(2)}) collective-permute-start(f16[448,128]{1,0:T(8,128)(2,1)S(1)} %convert_element_type.34), channel_id=1, source_target_pairs={{0,8},{4,12},{8,0},{12,4},{16,24},{20,28},{24,16},{28,20},{1,9},{5... | collective-permute-start | bytes 344072 | tf_op jit(solution)/shard_map/ppermute | solution.py:241

commit v3 on v2

v3 whole, which is shorter than its diff:
```python
import functools

import jax
import jax.numpy as jnp
import numpy as np
from jax import lax
from jax.experimental import pallas as pl
from jax.experimental.pallas import tpu as pltpu
from jax.sharding import PartitionSpec as P

F = 128
LAG = 128
G = 2
SB = 4
S = 8
COMPS = 3
XS = 2 * F + 8

f32 = jnp.float32
bf16 = jnp.bfloat16
f16 = jnp.float16
TOP = 14
PARAMS = pltpu.CompilerParams(vmem_limit_bytes=48 << 20)
VMEM = pl.BlockSpec(memory_space=pltpu.VMEM)
SMEM = pl.BlockSpec(memory_space=pltpu.SMEM)


def lag_table(freqs, lags):
    freq_ids = np.arange(freqs)
    lag_ids = np.arange(lags) - lags // 2
    angle = 2.0 * np.pi / (2 * freqs) * np.mod(freq_ids[:, None] * lag_ids[None, :], 2 * freqs)
    weight = np.where(freq_ids == 0, 1.0, 2.0)[:, None] / np.sqrt(freqs)
    return np.concatenate([weight * np.cos(angle), -weight * np.sin(angle)], axis=0).astype(np.float32)


def two_terms(value):
    high = value.astype(bf16)
    return high, (value - high.astype(f32)).astype(bf16)


def first_kernel(x_hbm, o_ref, near, wide, sem):
    rows = near.shape[1] * 2
    copies = [
        pltpu.make_async_copy(x_hbm.at[:, :, a, 0:8, :], near.at[a], sem.at[a]) for a in range(COMPS)
    ]
    for copy in copies:
        copy.start()
    for a in range(COMPS):
        copies[a].wait()
        for part in range(2):
            wide[a, part] = near[a, :, part].astype(f32)
        flat = wide.at[a].reshape(rows * 8, F)
        for s in range(SB):
            o_ref[a, s] = flat[pl.ds(s, rows, stride=8), :].T.astype(bf16)


def first_block(spectra):
    segs = spectra.shape[0]
    return pl.pallas_call(
        first_kernel,
        in_specs=[pl.BlockSpec(memory_space=pltpu.HBM)],
        out_specs=VMEM,
        out_shape=jax.ShapeDtypeStruct((COMPS, SB, F, 2 * segs), bf16),
        scratch_shapes=[
            pltpu.VMEM((COMPS, segs, 2, 8, F), bf16),
            pltpu.VMEM((COMPS, 2, segs, 8, F), f32),
            pltpu.SemaphoreType.DMA((COMPS,)),
        ],
        compiler_params=PARAMS,
        name="first_block",
    )(spectra)


def receivers_kernel(x_ref, o_ref, wide, turned):
    b = pl.program_id(0)
    rows = x_ref.shape[0] * 2
    stations = x_ref.shape[3]
    for part in range(2):
        wide[part] = x_ref[:, part, 0].astype(f32)
    flat = wide.reshape(rows * stations, F)
    for r in range(stations):
        turned[pl.ds(b * stations + r, F, stride=COMPS * stations), :] = flat[pl.ds(r, rows, stride=stations), :].T

    @pl.when(b == COMPS - 1)
    def _():
        def body(f, carry):
            o_ref[f] = turned[pl.ds(pl.multiple_of(f * COMPS * stations, 8), COMPS * stations), :].astype(bf16)
            return carry

        lax.fori_loop(0, F, body, 0, unroll=8)


def receivers_by_freq(spectra):
    segs, stations = spectra.shape[0], spectra.shape[3]
    columns = COMPS * stations
    return pl.pallas_call(
        receivers_kernel,
        grid=(COMPS,),
        in_specs=[pl.BlockSpec((segs, 2, 1, stations, F), lambda b: (0, 0, b, 0, 0))],
        out_specs=pl.BlockSpec((F, columns, 2 * segs), lambda b: (0, 0, 0)),
        out_shape=jax.ShapeDtypeStruct((F, columns, 2 * segs), bf16),
        scratch_shapes=[pltpu.VMEM((2, segs, stations, F), f32), pltpu.VMEM((F * columns, 2 * segs), f32)],
        compiler_params=PARAMS,
        cost_estimate=pl.CostEstimate(flops=0, bytes_accessed=12 << 20, transcendentals=0),
        name="receivers_by_freq",
    )(spectra)


def power_of_two(n):
    size = jnp.abs(n)
    result = jnp.ones(n.shape, f32)
    for i in range(7):
        factor = jnp.where(n < 0, np.float32(2.0 ** -(2**i)), np.float32(2.0 ** (2**i)))
        result = result * jnp.where((size >> i) & 1 == 1, factor, np.float32(1.0))
    return result


def exponent_of(value):
    largest = jnp.max(jnp.abs(value), axis=(0, 1), keepdims=True)
    return jnp.ceil(jnp.log(jnp.maximum(largest, 1e-30)) * np.float32(1.4426950408889634)).astype(jnp.int32)


def pairs_of(outputs):
    pairs = [(mask, a) for _, blocks in outputs for mask, comps in blocks for a in comps]
    return pairs, -(-len(pairs) // 8) * 8


def stack_kernel(outputs, ids_ref, src_block_ref, owner_ref, scale_ref, signs_ref, table_ref, recv_ref, *rest):
    blocks, o_refs, (src, cross) = rest[: -2 - len(outputs)], rest[-2 - len(outputs) : -2], rest[-2:]
    pairs, rows = pairs_of(outputs)
    columns = recv_ref.shape[1]
    half = recv_ref.shape[2] // 2
    for mask in sorted({mask for mask, _ in pairs}):
        dest = ids_ref[0] ^ mask
        source = jnp.int32(0)
        for k in range(S):
            source = source + jnp.where(owner_ref[k] == dest, k, 0)
        which = ids_ref[1] ^ src_block_ref[source // SB]
        station = source % SB
        for j in range(len(blocks)):

            @pl.when(which == j)
            def _():
                for at, (pair_mask, a) in enumerate(pairs):
                    if pair_mask == mask:
                        src[pl.ds(at, F, stride=rows), :] = blocks[j][a, station].astype(f32)

    signs = signs_ref[...]

    def one_freq(f, carry):
        plain = src[pl.ds(pl.multiple_of(f * rows, 8), rows), :]
        rolled = pltpu.roll(plain, half, 1)
        left = [plain * signs[0:1], plain * signs[1:2], rolled * signs[2:3], rolled * signs[3:4]]
        left = jnp.concatenate(left, axis=0).astype(bf16)
        out = lax.dot_general(left, recv_ref[f], (((1,), (1,)), ((), ())), preferred_element_type=f32)
        cross[pl.ds(f, G * rows, stride=XS), 0:columns] = out[: G * rows]
        cross[pl.ds(F + f, G * rows, stride=XS), 0:columns] = out[G * rows :]
        return carry

    lax.fori_loop(0, F, one_freq, 0, unroll=32)
    table_high, table_low = two_terms(table_ref[...])
    table = jnp.concatenate([table_high, table_low], axis=1)
    for (coded, blocks_of), o_ref in zip(outputs, o_refs):
        exponents = jnp.zeros((16, LAG), f32)
        done = 0
        for at, (mask, comps) in enumerate(blocks_of):
            turned = []
            for g in range(G):
                for a in comps:
                    first = (g * rows + pairs.index((mask, a))) * XS
                    turned.append(cross[first : first + 2 * F, :].T[:columns])
            high, low = two_terms(jnp.concatenate(turned, axis=0))
            both = jnp.dot(high, table, preferred_element_type=f32)
            lagged = both[:, :LAG] + both[:, LAG:] + jnp.dot(low, table_high, preferred_element_type=f32)
            part = len(comps) * columns
            lagged = jnp.concatenate([lagged[g * part : (g + 1) * part] * scale_ref[g] for g in range(G)], axis=0)
            if coded:
                e = exponent_of(lagged)
                lagged = lagged * power_of_two(TOP - e)
                exponents = jnp.where(lax.broadcasted_iota(jnp.int32, (16, LAG), 0) == at, e.astype(f32), exponents)
            o_ref[done : done + G * part] = lagged
            done += G * part
        if coded:
            o_ref[done:] = exponents


def stacks(outputs, ids, src_block, owner, scale, signs, table, recv, blocks):
    columns, depth = recv.shape[1:]
    rows = pairs_of(outputs)[1]
    shapes = []
    for coded, blocks_of in outputs:
        size = sum(G * len(comps) * columns for _, comps in blocks_of) + (16 if coded else 0)
        shapes.append(jax.ShapeDtypeStruct((size, LAG), f32))
    return pl.pallas_call(
        functools.partial(stack_kernel, outputs),
        in_specs=[SMEM] * 4 + [VMEM] * 3 + [VMEM] * len(blocks),
        out_specs=[VMEM] * len(outputs),
        out_shape=shapes,
        scratch_shapes=[pltpu.VMEM((F * rows, depth), f32), pltpu.VMEM((G * rows * XS, 128), f32)],
        compiler_params=PARAMS,
        cost_estimate=pl.CostEstimate(flops=0, bytes_accessed=16 << 20, transcendentals=0),
        name="stacks",
    )(ids, src_block, owner, scale, signs, table, recv, *blocks)


def factor_of(coded, size, at):
    return power_of_two(coded[size + at : size + at + 1, 0:1].astype(jnp.int32) - TOP)


def store_coded(o_ref, value):
    size = value.shape[0]
    e = exponent_of(value)
    o_ref[0:size] = value * power_of_two(TOP - e)
    o_ref[size:] = jnp.broadcast_to(e.astype(f32), (16, LAG))


def merge_kernel(count, kept_ref, *refs):
    size = kept_ref.shape[0] // count
    arrived, own_ref, out_refs = refs[:-count], refs[-count], refs[len(refs) - count + 1 :]
    factors = [[factor_of(ref, count * size, j) for j in range(count)] for ref in arrived]
    for j in range(count):
        rows = slice(j * size, (j + 1) * size)
        value = kept_ref[rows]
        for ref, factor in zip(arrived, factors):
            value = value + ref[rows] * factor[j]
        if j == 0:
            own_ref[...] = value
        else:
            store_coded(out_refs[j - 1], value)


def merge(kept, arrived, count):
    size = kept.shape[0] // count
    coded = jax.ShapeDtypeStruct((size + 16, LAG), f32)
    return pl.pallas_call(
        functools.partial(merge_kernel, count),
        in_specs=[VMEM] * (1 + len(arrived)),
        out_specs=[VMEM] * count,
        out_shape=[jax.ShapeDtypeStruct((size, LAG), f32)] + [coded] * (count - 1),
        compiler_params=PARAMS,
        name="merge",
    )(kept, *arrived)


def total_kernel(stations, comps, counts, *refs):
    refs, o_ref = list(refs[:-1]), refs[-1]
    per_station = G * COMPS * COMPS
    for of, count in zip(comps, counts):
        own_ref, parts, refs = refs[0], refs[1:count], refs[count:]
        size = own_ref.shape[0]
        factors = [factor_of(part, size, 0) for part in parts]
        at = 0
        for g in range(G):
            for a in of:
                for b in range(COMPS):
                    rows = pl.ds(at, stations)
                    at += stations
                    value = own_ref[rows, :]
                    for part, factor in zip(parts, factors):
                        value = value + part[rows, :] * factor
                    o_ref[pl.ds((a * COMPS + b) * G + g, stations, stride=per_station), :] = value


def total(stations, comps, parts):
    counts = [len(of) for of in parts]
    return pl.pallas_call(
        functools.partial(total_kernel, stations, comps, counts),
        in_specs=[VMEM] * sum(counts),
        out_specs=VMEM,
        out_shape=jax.ShapeDtypeStruct((stations * COMPS * COMPS * G, LAG), f32),
        compiler_params=PARAMS,
        name="total",
    )(*[part for of in parts for part in of])


def swap(value, axis, mask):
    size = lax.axis_size(axis)
    return lax.ppermute(value, axis, [(i, i ^ mask) for i in range(size)])


def send(coded, mask):
    return swap(coded.astype(f16), "day", mask).astype(f32)


def owned_block(owner):
    ids = jnp.arange(owner.shape[0], dtype=jnp.int32)
    return jnp.sum(ids[None, :] * (owner[None, :] == ids[:, None]).astype(jnp.int32), axis=1)


def local(spectra, src_block, group_of, owner):
    segs, stations = spectra.shape[0], spectra.shape[3]
    days = lax.axis_size("day")
    day = lax.axis_index("day")
    me = lax.axis_index("sta")
    group_ids = jnp.arange(G, dtype=jnp.int32)
    scale = 1.0 / jnp.sqrt(jnp.sum((group_of[None, :] == group_ids[:, None]).astype(f32), axis=1))
    mine = lax.dynamic_slice_in_dim(group_of, day * segs, segs)
    hot = (mine[None, :] == group_ids[:, None]).astype(f32)
    signs = jnp.concatenate([jnp.concatenate([hot, hot], axis=1), jnp.concatenate([-hot, hot], axis=1)], axis=0)
    table = jnp.asarray(lag_table(F, LAG))
    first = first_block(spectra)
    block_rows = S * stations // days

    if days == S and lax.axis_size("sta") == 4:
        across = swap(first, "sta", 2)
        blocks = [first, swap(first, "sta", 1), across, swap(across, "sta", 1)]
        recv = receivers_by_freq(spectra)
        operands = (jnp.stack([day, me]), src_block, owner, scale, signs, table, recv, blocks)
        ys, zs = [0, 1], range(0, days, 2)
        y_first, z_first = (0, 1), (2,)
        away = stacks(
            [(True, [(1 ^ z, y_first) for z in zs])]
            + [(True, [(y ^ z, z_first) for y in ys]) for z in zs[1:]],
            *operands,
        )
        arrived_y = send(away[0], 1)
        arrived_z = [send(part, z) for part, z in zip(away[1:], zs[1:])]
        kept = stacks([(False, [(z, y_first) for z in zs]), (False, [(y, z_first) for y in ys])], *operands)
        own_y, *others = merge(kept[0], [arrived_y], len(zs))
        parts_y = [own_y] + [send(other, z) for other, z in zip(others, zs[1:])]
        own_z, other = merge(kept[1], arrived_z, len(ys))
        result = total(stations, (y_first, z_first), (parts_y, [own_z, send(other, 1)]))
        result = result.reshape(block_rows, COMPS * COMPS, G, LAG).transpose(0, 2, 1, 3)
        return result[None]

    gathered = lax.all_gather(first, "sta")
    blocks = [lax.dynamic_index_in_dim(gathered, src_block[k], 0, keepdims=False) for k in range(2)]
    recv = receivers_by_freq(spectra)
    every = jnp.arange(S, dtype=jnp.int32)
    outputs = [(False, [(mask, tuple(range(COMPS))) for mask in range(S)])]
    (partial,) = stacks(outputs, jnp.zeros(2, jnp.int32), every[:2], every, scale, signs, table, recv, blocks)
    partial = partial.reshape(S, G, COMPS * COMPS, stations, LAG).transpose(0, 3, 1, 2, 4)
    partial = partial.reshape(days, block_rows, G, COMPS * COMPS, LAG)
    ordered = jnp.take(partial, owned_block(owner), axis=0)
    return lax.psum_scatter(ordered, "day", scatter_dimension=0, tiled=True)


def solution(mesh):
    return jax.shard_map(
        local,
        mesh=mesh,
        in_specs=(P("day", None, None, "sta", None), P(), P(), P()),
        out_specs=P("day", "sta", None, None, None),
        check_vma=False,
    )
```

time: 48.6 us -> 43.8 us (0.901)
  waiting for transfers between devices: 23.2 us -> 12.6 us
  starting transfers between devices: 9.43 us -> 14.3 us
  Pallas kernels: 12.5 us -> 13.3 us
    ppermute x7 -> x11, waiting for transfers between devices: 23.2 us -> 12.6 us  [swap(): return lax.ppermute(value, axis, [(i, i ^ mask) for i in range(size)])]
    ppermute x7 -> x11, starting transfers between devices: 9.43 us -> 14.3 us  [swap(): return lax.ppermute(value, axis, [(i, i ^ mask) for i in range(size)])]
    pallas_call x5 -> x6, Pallas kernels: 10.3 us -> 11.1 us  [the longest x2 9.01 us: stacks(): pl.pallas_call(functools.partial(stack_kernel, outputs), in_specs=[SMEM]...]
  transfers between devices with their start and end apart: 7 -> 11, of which waited for: 5 -> 5; matrix products, arithmetic and copies ran while one was open for 1% -> 1% of each run, Pallas kernels for 13% -> 16%
where the time goes in v3:
time: 43.8 us; the launch traced here: 43.7 us
  starting transfers between devices  14.3 us (33%)
  Pallas kernels  13.3 us (30%)
  waiting for transfers between devices  12.6 us (29%)
  local copies, waits for them, and re-layouts  2.66 us (6%)
  other arithmetic  0.54 us (1%)
    ppermute x11, starting transfers between devices, swap(): return lax.ppermute(value, axis, [(i, i ^ mask) for i in range(size)])  14.3 us
    ppermute x11, waiting for transfers between devices, swap(): return lax.ppermute(value, axis, [(i, i ^ mask) for i in range(size)])  12.6 us
    pallas_call x2, Pallas kernels, stacks(): pl.pallas_call(functools.partial(stack_kernel, outputs), in_specs=[SMEM]...  9.01 us
    unnamed x10, local copies, waits for them, and re-layouts  2.58 us
    pallas_call x1, Pallas kernels, receivers_by_freq(): pl.pallas_call(receivers_kernel, grid=(COMPS,), in_specs=[pl.BlockSpec((s...  2.21 us
  transfers between devices with their start and end apart: 11, of which 5 were waited for; matrix products, arithmetic and copies ran while one was open for 1% of the time, Pallas kernels for 16%

profile of v3, /device:TPU:0, one launch (start us, length us, event | category | flops | bytes accessed | tf_op | source)
XLA Modules:
  0.0 43.7 jit_solution(5431336491098881185)
XLA Ops:
  0.0 1.7 %copy-done = bf16[64,2,3,24,128]{4,3,2,1,0:T(8,128)(2,1)S(1)} copy-done((bf16[64,2,3,24,128]{4,3,2,1,0:T(8,128)(2,1)S(1)}, bf16[64,2,3,24,128]{4,3,2,1,0:T(8,128)(2,1)}, u32[]{:S(2)}) %copy-start) | copy-done | bytes 2359320
  1.7 0.6 %first_block.1.rest_0_ = bf16[3,4,128,128]{3,2,1,0:T(8,128)(2,1)S(1)} custom-call(bf16[64,2,3,24,128]{4,3,2,1,0:T(8,128)(2,1)S(1)} %copy-done), custom_call_target="tpu_custom_call" | custom-call | tf_op jit(solution)/shard_map/first_block/pallas_call | solution.py:59
  2.3 3.0 %collective-permute-start.1 = (bf16[3,4,128,128]{3,2,1,0:T(8,128)(2,1)S(1)}, bf16[3,4,128,128]{3,2,1,0:T(8,128)(2,1)S(1)}, u32[]{:S(2)}, u32[]{:S(2)}) collective-permute-start(bf16[3,4,128,128]{3,2,1,0:T(8,128)(2,1)S(1)} %first_block.1.rest_0_), channel_id=1, source_target_pairs={{0,2},{1,3},{2,0},{3,1},{4,6},{5,7},{6,4},{7,5},{8,10},{9,11},{10,... | collective-permute-start | bytes 1179656 | tf_op jit(solution)/shard_map/ppermute | solution.py:278
  5.3 0.0 collective-permute-start
  5.3 2.2 %receivers_by_freq.1.recv_ref = bf16[128,72,128]{2,1,0:T(8,128)(2,1)S(1)} custom-call(bf16[64,2,3,24,128]{4,3,2,1,0:T(8,128)(2,1)S(1)} %copy-done), custom_call_target="tpu_custom_call" | custom-call | bytes 12582912 | tf_op jit(solution)/shard_map/receivers_by_freq/pallas_call | solution.py:96
  7.5 0.1 dynamic_slice.3
  7.6 0.1 fusion
  7.7 6.7 %collective-permute-done.1.rest_2_ = bf16[3,4,128,128]{3,2,1,0:T(8,128)(2,1)S(1)} collective-permute-done((bf16[3,4,128,128]{3,2,1,0:T(8,128)(2,1)S(1)}, bf16[3,4,128,128]{3,2,1,0:T(8,128)(2,1)S(1)}, u32[]{:S(2)}, u32[]{:S(2)}) %collective-permute-start.1) | collective-permute-done | bytes 393248 | tf_op jit(solution)/shard_map/ppermute | solution.py:278
  14.4 0.0 collective-permute-start.2
  14.4 0.1 pad_add_fusion.ids_ref
  14.5 0.1 maximum_maximum_fusion.signs_ref
  14.5 0.0 collective-permute-done.rest_1_
  14.5 1.6 %collective-permute-done.2.rest_3_ = bf16[3,4,128,128]{3,2,1,0:T(8,128)(2,1)S(1)} collective-permute-done((bf16[3,4,128,128]{3,2,1,0:T(8,128)(2,1)S(1)}, bf16[3,4,128,128]{3,2,1,0:T(8,128)(2,1)S(1)}, u32[]{:S(2)}, u32[]{:S(2)}) %collective-permute-start.2) | collective-permute-done | bytes 393248 | tf_op jit(solution)/shard_map/ppermute | solution.py:278
  16.1 0.9 %copy-done.1 = f32[256,128]{1,0:T(8,128)S(1)} copy-done((f32[256,128]{1,0:T(8,128)S(1)}, f32[256,128]{1,0:T(8,128)}, u32[]{:S(2)}) %copy-start.1) | copy-done | bytes 131096
  17.0 4.9 %stacks.3 = (f32[1168,128]{1,0:T(8,128)S(1)}, f32[304,128]{1,0:T(8,128)S(1)}, f32[304,128]{1,0:T(8,128)S(1)}, f32[304,128]{1,0:T(8,128)S(1)}) custom-call(s32[2]{0:T(128)S(1)} %pad_add_fusion.ids_ref, s32[2]{0:T(128)S(1)} %copy-done.2, s32[8]{0:T(128)S(1)} %copy-done.3, f32[2]{0:T(128)S(1)} %sqrt.3.scale_ref, f32[4,128]{1,0:T(4,128)S(1)} %maximum_maximum_fusion.signs_ref, ...), custom_call_target="tpu_custom_call" | custom-call | bytes 16777216 | tf_op jit(solution)/shard_map/stacks/pallas_call | solution.py:194
  22.0 1.8 %collective-permute-start.3 = (f16[1168,128]{1,0:T(8,128)(2,1)S(1)}, f16[1168,128]{1,0:T(8,128)(2,1)S(1)}, u32[]{:S(2)}, u32[]{:S(2)}) collective-permute-start(f16[1168,128]{1,0:T(8,128)(2,1)S(1)} %convert_element_type.56), channel_id=1, source_target_pairs={{0,4},{4,0},{8,12},{12,8},{16,20},{20,16},{24,28},{28,24},{1,5},{5... | collective-permute-start | bytes 897032 | tf_op jit(solution)/shard_map/ppermute | solution.py:278
  23.8 3.7 %collective-permute-start.9 = (f16[304,128]{1,0:T(8,128)(2,1)S(1)}, f16[304,128]{1,0:T(8,128)(2,1)S(1)}, u32[]{:S(2)}, u32[]{:S(2)}) collective-permute-start(f16[304,128]{1,0:T(8,128)(2,1)S(1)} %convert_element_type.68), channel_id=1, source_target_pairs={{0,24},{4,28},{8,16},{12,20},{16,8},{20,12},{24,0},{28,4},{1,25},{... | collective-permute-start | bytes 233480 | tf_op jit(solution)/shard_map/ppermute | solution.py:278
  27.5 0.1 collective-permute-start.8
  27.6 0.8 %collective-permute-start.7 = (f16[304,128]{1,0:T(8,128)(2,1)S(1)}, f16[304,128]{1,0:T(8,128)(2,1)S(1)}, u32[]{:S(2)}, u32[]{:S(2)}) collective-permute-start(f16[304,128]{1,0:T(8,128)(2,1)S(1)} %convert_element_type.64), channel_id=1, source_target_pairs={{0,8},{4,12},{8,0},{12,4},{16,24},{20,28},{24,16},{28,20},{1,9},{5... | collective-permute-start | bytes 233480 | tf_op jit(solution)/shard_map/ppermute | solution.py:278
  28.4 4.1 %stacks.2 = (f32[1152,128]{1,0:T(8,128)S(1)}, f32[288,128]{1,0:T(8,128)S(1)}) custom-call(s32[2]{0:T(128)S(1)} %pad_add_fusion.ids_ref, s32[2]{0:T(128)S(1)} %copy-done.2, s32[8]{0:T(128)S(1)} %copy-done.3, f32[2]{0:T(128)S(1)} %sqrt.3.scale_ref, f32[4,128]{1,0:T(4,128)S(1)} %maximum_maximum_fusion.signs_ref, f32[256,128]{1,0:T(8,128)S(1)} %copy-done.1, ...), custom_call_target="tpu_custom_call" | custom-call | bytes 16777216 | tf_op jit(solution)/shard_map/stacks/pallas_call | solution.py:194
  32.5 0.0 collective-permute-done.3
  32.6 0.5 %merge.2 = (f32[288,128]{1,0:T(8,128)S(1)}, f32[304,128]{1,0:T(8,128)S(1)}, f32[304,128]{1,0:T(8,128)S(1)}, f32[304,128]{1,0:T(8,128)S(1)}) custom-call(f32[1152,128]{1,0:T(8,128)S(1)} %get-tuple-element.17.kept_ref, f32[1168,128]{1,0:T(8,128)S(1)} %convert_element_type.57.refs_0_), custom_call_target="tpu_custom_call" | custom-call | tf_op jit(solution)/shard_map/merge/pallas_call | solution.py:235
  33.1 3.7 %collective-permute-start.6 = (f16[304,128]{1,0:T(8,128)(2,1)S(1)}, f16[304,128]{1,0:T(8,128)(2,1)S(1)}, u32[]{:S(2)}, u32[]{:S(2)}) collective-permute-start(f16[304,128]{1,0:T(8,128)(2,1)S(1)} %convert_element_type.62), channel_id=1, source_target_pairs={{0,24},{4,28},{8,16},{12,20},{16,8},{20,12},{24,0},{28,4},{1,25},{... | collective-permute-start | bytes 233480 | tf_op jit(solution)/shard_map/ppermute | solution.py:278
  36.8 0.1 collective-permute-start.5
  36.9 0.0 collective-permute-done.9
  36.9 0.7 %collective-permute-start.4 = (f16[304,128]{1,0:T(8,128)(2,1)S(1)}, f16[304,128]{1,0:T(8,128)(2,1)S(1)}, u32[]{:S(2)}, u32[]{:S(2)}) collective-permute-start(f16[304,128]{1,0:T(8,128)(2,1)S(1)} %convert_element_type.58), channel_id=1, source_target_pairs={{0,8},{4,12},{8,0},{12,4},{16,24},{20,28},{24,16},{28,20},{1,9},{5... | collective-permute-start | bytes 233480 | tf_op jit(solution)/shard_map/ppermute | solution.py:278
  37.8 0.2 merge.3
  38.0 0.4 collective-permute-start.10
  38.4 3.6 %collective-permute-done.10 = f16[160,128]{1,0:T(8,128)(2,1)S(1)} collective-permute-done((f16[160,128]{1,0:T(8,128)(2,1)S(1)}, f16[160,128]{1,0:T(8,128)(2,1)S(1)}, u32[]{:S(2)}, u32[]{:S(2)}) %collective-permute-start.10) | collective-permute-done | bytes 40992 | tf_op jit(solution)/shard_map/ppermute | solution.py:278
  42.1 0.4 %collective-permute-done.5 = f16[304,128]{1,0:T(8,128)(2,1)S(1)} collective-permute-done((f16[304,128]{1,0:T(8,128)(2,1)S(1)}, f16[304,128]{1,0:T(8,128)(2,1)S(1)}, u32[]{:S(2)}, u32[]{:S(2)}) %collective-permute-start.5) | collective-permute-done | bytes 77856 | tf_op jit(solution)/shard_map/ppermute | solution.py:278
  42.6 0.3 collective-permute-done.4
  42.9 0.8 %total.1 = f32[432,128]{1,0:T(8,128)} custom-call(f32[288,128]{1,0:T(8,128)S(1)} %get-tuple-element.19.refs_0_, f32[304,128]{1,0:T(8,128)S(1)} %convert_element_type.59.refs_1_, f32[304,128]{1,0:T(8,128)S(1)} %convert_element_type.61.refs_2_, f32[304,128]{1,0:T(8,128)S(1)} %convert_element_type.63.refs_3_, f32[144,128]{1,0:T(8,128)S(1)} %get-tuple-element.27.refs_4_, ...), custom_call_target="tpu_custom_call" | custom-call | tf_op jit(solution)/shard_map/total/pallas_call | solution.py:266
  (30 shorter events, 0.3 us)
Async XLA Ops:
  0.0 1.7 %copy-start = (bf16[64,2,3,24,128]{4,3,2,1,0:T(8,128)(2,1)S(1)}, bf16[64,2,3,24,128]{4,3,2,1,0:T(8,128)(2,1)}, u32[]{:S(2)}) copy-start(bf16[64,2,3,24,128]{4,3,2,1,0:T(8,128)(2,1)} %x_hbm.1) | copy-start | bytes 7077892
  2.3 12.1 %collective-permute-start.1 = (bf16[3,4,128,128]{3,2,1,0:T(8,128)(2,1)S(1)}, bf16[3,4,128,128]{3,2,1,0:T(8,128)(2,1)S(1)}, u32[]{:S(2)}, u32[]{:S(2)}) collective-permute-start(bf16[3,4,128,128]{3,2,1,0:T(8,128)(2,1)S(1)} %first_block.1.rest_0_), channel_id=1, source_target_pairs={{0,2},{1,3},{2,0},{3,1},{4,6},{5,7},{6,4},{7,5},{8,10},{9,11},{10,... | collective-permute-start | bytes 1179656 | tf_op jit(solution)/shard_map/ppermute | solution.py:278
  5.3 9.3 %collective-permute-start = (bf16[3,4,128,128]{3,2,1,0:T(8,128)(2,1)S(1)}, bf16[3,4,128,128]{3,2,1,0:T(8,128)(2,1)S(1)}, u32[]{:S(2)}, u32[]{:S(2)}) collective-permute-start(bf16[3,4,128,128]{3,2,1,0:T(8,128)(2,1)S(1)} %first_block.1.rest_0_), channel_id=1, source_target_pairs={{0,1},{1,0},{2,3},{3,2},{4,5},{5,4},{6,7},{7,6},{8,9},{9,8},{10,11... | collective-permute-start | bytes 1179656 | tf_op jit(solution)/shard_map/ppermute | solution.py:278
  5.3 2.2 %copy-start.4 = (s32[512]{0:T(512)S(1)}, s32[512]{0:T(512)}, u32[]{:S(2)}) copy-start(s32[512]{0:T(512)} %param.7) | copy-start | bytes 6148
  5.3 10.8 %copy-start.2 = (s32[2]{0:T(128)S(1)}, s32[2]{0:T(128)}, u32[]{:S(2)}) copy-start(s32[2]{0:T(128)} %src_block_ref.3) | copy-start | bytes 28
  5.3 10.8 %copy-start.3 = (s32[8]{0:T(128)S(1)}, s32[8]{0:T(128)}, u32[]{:S(2)}) copy-start(s32[8]{0:T(128)} %owner_ref.3) | copy-start | bytes 100
  14.4 1.7 %collective-permute-start.2 = (bf16[3,4,128,128]{3,2,1,0:T(8,128)(2,1)S(1)}, bf16[3,4,128,128]{3,2,1,0:T(8,128)(2,1)S(1)}, u32[]{:S(2)}, u32[]{:S(2)}) collective-permute-start(bf16[3,4,128,128]{3,2,1,0:T(8,128)(2,1)S(1)} %collective-permute-done.1.rest_2_), channel_id=1, source_target_pairs={{0,1},{1,0},{2,3},{3,2},{4,5},{5,4},{6,7},{7,6},{8,9},{9,8},{10,11... | collective-permute-start | bytes 1179656 | tf_op jit(solution)/shard_map/ppermute | solution.py:278
  16.1 0.9 %copy-start.1 = (f32[256,128]{1,0:T(8,128)S(1)}, f32[256,128]{1,0:T(8,128)}, u32[]{:S(2)}) copy-start(f32[256,128]{1,0:T(8,128)} %constant.20.clone.table_ref) | copy-start | bytes 393220
  22.0 10.6 %collective-permute-start.3 = (f16[1168,128]{1,0:T(8,128)(2,1)S(1)}, f16[1168,128]{1,0:T(8,128)(2,1)S(1)}, u32[]{:S(2)}, u32[]{:S(2)}) collective-permute-start(f16[1168,128]{1,0:T(8,128)(2,1)S(1)} %convert_element_type.56), channel_id=1, source_target_pairs={{0,4},{4,0},{8,12},{12,8},{16,20},{20,16},{24,28},{28,24},{1,5},{5... | collective-permute-start | bytes 897032 | tf_op jit(solution)/shard_map/ppermute | solution.py:278
  23.8 13.1 %collective-permute-start.9 = (f16[304,128]{1,0:T(8,128)(2,1)S(1)}, f16[304,128]{1,0:T(8,128)(2,1)S(1)}, u32[]{:S(2)}, u32[]{:S(2)}) collective-permute-start(f16[304,128]{1,0:T(8,128)(2,1)S(1)} %convert_element_type.68), channel_id=1, source_target_pairs={{0,24},{4,28},{8,16},{12,20},{16,8},{20,12},{24,0},{28,4},{1,25},{... | collective-permute-start | bytes 233480 | tf_op jit(solution)/shard_map/ppermute | solution.py:278
  27.5 10.2 %collective-permute-start.8 = (f16[304,128]{1,0:T(8,128)(2,1)S(1)}, f16[304,128]{1,0:T(8,128)(2,1)S(1)}, u32[]{:S(2)}, u32[]{:S(2)}) collective-permute-start(f16[304,128]{1,0:T(8,128)(2,1)S(1)} %convert_element_type.66), channel_id=1, source_target_pairs={{0,16},{4,20},{8,24},{12,28},{16,0},{20,4},{24,8},{28,12},{1,17},{... | collective-permute-start | bytes 233480 | tf_op jit(solution)/shard_map/ppermute | solution.py:278
  27.6 10.1 %collective-permute-start.7 = (f16[304,128]{1,0:T(8,128)(2,1)S(1)}, f16[304,128]{1,0:T(8,128)(2,1)S(1)}, u32[]{:S(2)}, u32[]{:S(2)}) collective-permute-start(f16[304,128]{1,0:T(8,128)(2,1)S(1)} %convert_element_type.64), channel_id=1, source_target_pairs={{0,8},{4,12},{8,0},{12,4},{16,24},{20,28},{24,16},{28,20},{1,9},{5... | collective-permute-start | bytes 233480 | tf_op jit(solution)/shard_map/ppermute | solution.py:278
  33.1 9.0 %collective-permute-start.6 = (f16[304,128]{1,0:T(8,128)(2,1)S(1)}, f16[304,128]{1,0:T(8,128)(2,1)S(1)}, u32[]{:S(2)}, u32[]{:S(2)}) collective-permute-start(f16[304,128]{1,0:T(8,128)(2,1)S(1)} %convert_element_type.62), channel_id=1, source_target_pairs={{0,24},{4,28},{8,16},{12,20},{16,8},{20,12},{24,0},{28,4},{1,25},{... | collective-permute-start | bytes 233480 | tf_op jit(solution)/shard_map/ppermute | solution.py:278
  36.8 5.7 %collective-permute-start.5 = (f16[304,128]{1,0:T(8,128)(2,1)S(1)}, f16[304,128]{1,0:T(8,128)(2,1)S(1)}, u32[]{:S(2)}, u32[]{:S(2)}) collective-permute-start(f16[304,128]{1,0:T(8,128)(2,1)S(1)} %convert_element_type.60), channel_id=1, source_target_pairs={{0,16},{4,20},{8,24},{12,28},{16,0},{20,4},{24,8},{28,12},{1,17},{... | collective-permute-start | bytes 233480 | tf_op jit(solution)/shard_map/ppermute | solution.py:278
  36.9 5.9 %collective-permute-start.4 = (f16[304,128]{1,0:T(8,128)(2,1)S(1)}, f16[304,128]{1,0:T(8,128)(2,1)S(1)}, u32[]{:S(2)}, u32[]{:S(2)}) collective-permute-start(f16[304,128]{1,0:T(8,128)(2,1)S(1)} %convert_element_type.58), channel_id=1, source_target_pairs={{0,8},{4,12},{8,0},{12,4},{16,24},{20,28},{24,16},{28,20},{1,9},{5... | collective-permute-start | bytes 233480 | tf_op jit(solution)/shard_map/ppermute | solution.py:278
  38.0 4.1 %collective-permute-start.10 = (f16[160,128]{1,0:T(8,128)(2,1)S(1)}, f16[160,128]{1,0:T(8,128)(2,1)S(1)}, u32[]{:S(2)}, u32[]{:S(2)}) collective-permute-start(f16[160,128]{1,0:T(8,128)(2,1)S(1)} %convert_element_type.70), channel_id=1, source_target_pairs={{0,4},{4,0},{8,12},{12,8},{16,20},{20,16},{24,28},{28,24},{1,5},{5... | collective-permute-start | bytes 122888 | tf_op jit(solution)/shard_map/ppermute | solution.py:278

commit v4 on v3

v4 whole, which is shorter than its diff:
```python
import functools

import jax
import jax.numpy as jnp
import numpy as np
from jax import lax
from jax.experimental import pallas as pl
from jax.experimental.pallas import tpu as pltpu
from jax.sharding import PartitionSpec as P

F = 128
LAG = 128
G = 2
SB = 4
S = 8
COMPS = 3
XS = 2 * F + 8

f32 = jnp.float32
bf16 = jnp.bfloat16
f16 = jnp.float16
TAIL = 8
TOP = 14
PARAMS = pltpu.CompilerParams(vmem_limit_bytes=24 << 20)
VMEM = pl.BlockSpec(memory_space=pltpu.VMEM)
SMEM = pl.BlockSpec(memory_space=pltpu.SMEM)


def lag_table(freqs, lags):
    freq_ids = np.arange(freqs)
    lag_ids = np.arange(lags) - lags // 2
    angle = 2.0 * np.pi / (2 * freqs) * np.mod(freq_ids[:, None] * lag_ids[None, :], 2 * freqs)
    weight = np.where(freq_ids == 0, 1.0, 2.0)[:, None] / np.sqrt(freqs)
    return np.concatenate([weight * np.cos(angle), -weight * np.sin(angle)], axis=0).astype(np.float32)


def two_terms(value):
    high = value.astype(bf16)
    return high, (value - high.astype(f32)).astype(bf16)


def first_kernel(shares, x_ref, *refs):
    o_refs, wide = refs[:-1], refs[-1]
    rows = x_ref.shape[0] * 2
    for a in range(COMPS):
        for part in range(2):
            wide[a, part] = x_ref[:, part, a, 0:8].astype(f32)
        flat = wide.at[a].reshape(rows * 8, F)
        for of, o_ref in zip(shares, o_refs):
            if a in of:
                for s in range(SB):
                    o_ref[of.index(a), s] = flat[pl.ds(s, rows, stride=8), :].T.astype(bf16)


def first_block(spectra, shares):
    segs = spectra.shape[0]
    return pl.pallas_call(
        functools.partial(first_kernel, shares),
        in_specs=[VMEM],
        out_specs=[VMEM] * len(shares),
        out_shape=[jax.ShapeDtypeStruct((len(of), SB, F, 2 * segs), bf16) for of in shares],
        scratch_shapes=[pltpu.VMEM((COMPS, 2, segs, 8, F), f32)],
        compiler_params=PARAMS,
        name="first_block",
    )(spectra)


def receivers_kernel(ids_ref, x_ref, group_ref, o_ref, signs_ref, scale_ref, wide, turned):
    b = pl.program_id(0)
    rows = x_ref.shape[0] * 2
    stations = x_ref.shape[3]
    for part in range(2):
        wide[part] = x_ref[:, part, 0].astype(f32)
    flat = wide.reshape(rows * stations, F)
    for r in range(stations):
        turned[pl.ds(b * stations + r, F, stride=COMPS * stations), :] = flat[pl.ds(r, rows, stride=stations), :].T

    @pl.when(b == 0)
    def _():
        at = ids_ref[0] * (rows // 2)
        row = group_ref[pl.ds(at // rows, 1), :].astype(f32)
        swapped = pltpu.roll(row, rows // 2, 1)
        low = lax.broadcasted_iota(jnp.int32, row.shape, 1) < rows // 2
        mine = jnp.where(low == (at % rows == 0), row, swapped)
        for g in range(G):
            hot = jnp.where(mine == g, np.float32(1.0), np.float32(0.0))
            signs_ref[g : g + 1] = hot
            signs_ref[G + g : G + g + 1] = jnp.where(low, -hot, hot)
            hits = jnp.where(group_ref[...] == g, np.float32(1.0), np.float32(0.0))
            count = jnp.sum(hits, axis=(0, 1), keepdims=True)
            scale_ref[g : g + 1] = jnp.broadcast_to(1.0 / jnp.sqrt(count), (1, LAG))

    @pl.when(b == COMPS - 1)
    def _():
        def body(f, carry):
            o_ref[f] = turned[pl.ds(pl.multiple_of(f * COMPS * stations, 8), COMPS * stations), :].astype(bf16)
            return carry

        lax.fori_loop(0, F, body, 0, unroll=8)


def receivers_by_freq(ids, spectra, group_of):
    segs, stations = spectra.shape[0], spectra.shape[3]
    columns = COMPS * stations
    groups = group_of.reshape(-1, 2 * segs)
    fixed = lambda b: (0, 0)
    return pl.pallas_call(
        receivers_kernel,
        grid=(COMPS,),
        in_specs=[
            SMEM,
            pl.BlockSpec((segs, 2, 1, stations, F), lambda b: (0, 0, b, 0, 0)),
            pl.BlockSpec(groups.shape, fixed),
        ],
        out_specs=[
            pl.BlockSpec((F, columns, 2 * segs), lambda b: (0, 0, 0)),
            pl.BlockSpec((2 * G, 2 * segs), fixed),
            pl.BlockSpec((G, LAG), fixed),
        ],
        out_shape=[
            jax.ShapeDtypeStruct((F, columns, 2 * segs), bf16),
            jax.ShapeDtypeStruct((2 * G, 2 * segs), f32),
            jax.ShapeDtypeStruct((G, LAG), f32),
        ],
        scratch_shapes=[pltpu.VMEM((2, segs, stations, F), f32), pltpu.VMEM((F * columns, 2 * segs), f32)],
        compiler_params=PARAMS,
        cost_estimate=pl.CostEstimate(flops=0, bytes_accessed=12 << 20, transcendentals=0),
        name="receivers_by_freq",
    )(ids, spectra, groups)


def power_of_two(n):
    size = jnp.abs(n)
    result = jnp.ones(n.shape, f32)
    for i in range(7):
        factor = jnp.where(n < 0, np.float32(2.0 ** -(2**i)), np.float32(2.0 ** (2**i)))
        result = result * jnp.where((size >> i) & 1 == 1, factor, np.float32(1.0))
    return result


def exponent_of(value):
    largest = jnp.max(jnp.abs(value), axis=(0, 1), keepdims=True)
    return jnp.ceil(jnp.log(jnp.maximum(largest, 1e-30)) * np.float32(1.4426950408889634)).astype(jnp.int32)


def rows_of(pairs):
    return -(-len(pairs) // 8) * 8


def cross_kernel(pairs, comps_of, ids_ref, src_block_ref, owner_ref, recv_ref, signs_ref, *rest):
    blocks, (o_ref, src) = rest[:-2], rest[-2:]
    rows = rows_of(pairs)
    columns = recv_ref.shape[1]
    half = recv_ref.shape[2] // 2
    for mask in sorted({mask for mask, _ in pairs}):
        dest = ids_ref[0] ^ mask
        source = jnp.int32(0)
        for k in range(S):
            source = source + jnp.where(owner_ref[k] == dest, k, 0)
        which = ids_ref[1] ^ src_block_ref[source // SB]
        station = source % SB
        for j in range(len(blocks)):

            @pl.when(which == j)
            def _():
                for at, (pair_mask, a) in enumerate(pairs):
                    if pair_mask == mask:
                        src[pl.ds(at, F, stride=rows), :] = blocks[j][comps_of.index(a), station].astype(f32)

    signs = signs_ref[...]

    def one_freq(f, carry):
        plain = src[pl.ds(pl.multiple_of(f * rows, 8), rows), :]
        rolled = pltpu.roll(plain, half, 1)
        left = [plain * signs[0:1], plain * signs[1:2], rolled * signs[2:3], rolled * signs[3:4]]
        left = jnp.concatenate(left, axis=0).astype(bf16)
        out = lax.dot_general(left, recv_ref[f], (((1,), (1,)), ((), ())), preferred_element_type=f32)
        o_ref[pl.ds(f, G * rows, stride=XS), 0:columns] = out[: G * rows]
        o_ref[pl.ds(F + f, G * rows, stride=XS), 0:columns] = out[G * rows :]
        return carry

    lax.fori_loop(0, F, one_freq, 0, unroll=F)


def cross_spectra(pairs, comps_of, ids, src_block, owner, recv, signs, blocks):
    depth = recv.shape[2]
    rows = rows_of(pairs)
    return pl.pallas_call(
        functools.partial(cross_kernel, pairs, comps_of),
        in_specs=[SMEM] * 3 + [VMEM] * (2 + len(blocks)),
        out_specs=VMEM,
        out_shape=jax.ShapeDtypeStruct((G * rows * XS, 128), f32),
        scratch_shapes=[pltpu.VMEM((F * rows, depth), f32)],
        compiler_params=PARAMS,
        cost_estimate=pl.CostEstimate(flops=0, bytes_accessed=10 << 20, transcendentals=0),
        name="cross_spectra",
    )(ids, src_block, owner, recv, signs, *blocks)


def lag_kernel(outputs, pairs, columns, cross_ref, table_ref, scale_ref, *o_refs):
    rows = rows_of(pairs)
    table_high, table_low = two_terms(table_ref[...])
    table = jnp.concatenate([table_high, table_low], axis=1)
    for (coded, blocks_of), o_ref in zip(outputs, o_refs):
        exponents = jnp.zeros((TAIL, LAG), f32)
        done = 0
        for at, (mask, comps) in enumerate(blocks_of):
            turned = []
            for g in range(G):
                for a in comps:
                    first = (g * rows + pairs.index((mask, a))) * XS
                    turned.append(cross_ref[first : first + 2 * F, :].T[:columns])
            high, low = two_terms(jnp.concatenate(turned, axis=0))
            both = jnp.dot(high, table, preferred_element_type=f32)
            lagged = both[:, :LAG] + both[:, LAG:] + jnp.dot(low, table_high, preferred_element_type=f32)
            part = len(comps) * columns
            lagged = [lagged[g * part : (g + 1) * part] * scale_ref[g : g + 1] for g in range(G)]
            lagged = jnp.concatenate(lagged, axis=0)
            if coded:
                e = exponent_of(lagged)
                lagged = lagged * power_of_two(TOP - e)
                exponents = jnp.where(lax.broadcasted_iota(jnp.int32, (TAIL, LAG), 0) == at, e.astype(f32), exponents)
            o_ref[done : done + G * part] = lagged
            done += G * part
        if coded:
            o_ref[done:] = exponents


def lag_transform(outputs, pairs, columns, cross, table, scale):
    shapes = []
    for coded, blocks_of in outputs:
        size = sum(G * len(comps) * columns for _, comps in blocks_of) + (TAIL if coded else 0)
        shapes.append(jax.ShapeDtypeStruct((size, LAG), f32))
    return pl.pallas_call(
        functools.partial(lag_kernel, outputs, pairs, columns),
        in_specs=[VMEM] * 3,
        out_specs=[VMEM] * len(outputs),
        out_shape=shapes,
        compiler_params=PARAMS,
        cost_estimate=pl.CostEstimate(flops=0, bytes_accessed=5 << 20, transcendentals=0),
        name="lag_transform",
    )(cross, table, scale)


def factor_of(coded, size, at):
    return power_of_two(coded[size + at : size + at + 1, 0:1].astype(jnp.int32) - TOP)


def store_coded(o_ref, value):
    size = value.shape[0]
    e = exponent_of(value)
    o_ref[0:size] = value * power_of_two(TOP - e)
    o_ref[size:] = jnp.broadcast_to(e.astype(f32), (TAIL, LAG))


def merge_kernel(count, first, kept_ref, *refs):
    size = kept_ref.shape[0] // count
    arrived, o_refs = refs[:-count], refs[-count:]
    factors = [[factor_of(ref, count * size, j) for j in range(count)] for ref in arrived]
    for j in range(count):
        rows = slice(j * size, (j + 1) * size)
        value = kept_ref[rows]
        for ref, factor in zip(arrived, factors):
            value = value + ref[rows] * factor[j]
        if j < first:
            o_refs[j][...] = value
        else:
            store_coded(o_refs[j], value)


def merge(kept, arrived, count, first):
    size = kept.shape[0] // count
    plain, coded = jax.ShapeDtypeStruct((size, LAG), f32), jax.ShapeDtypeStruct((size + TAIL, LAG), f32)
    return pl.pallas_call(
        functools.partial(merge_kernel, count, first),
        in_specs=[VMEM] * (1 + len(arrived)),
        out_specs=[VMEM] * count,
        out_shape=[plain] * first + [coded] * (count - first),
        compiler_params=PARAMS,
        name="merge",
    )(kept, *arrived)


def total_kernel(stations, comps, counts, *refs):
    refs, o_ref = list(refs[:-1]), refs[-1]
    per_station = G * COMPS * COMPS
    for of, count in zip(comps, counts):
        own_ref, parts, refs = refs[0], refs[1:count], refs[count:]
        size = own_ref.shape[0]
        factors = [factor_of(part, size, 0) for part in parts]
        at = 0
        for g in range(G):
            for a in of:
                for b in range(COMPS):
                    rows = pl.ds(at, stations)
                    at += stations
                    value = own_ref[rows, :]
                    for part, factor in zip(parts, factors):
                        value = value + part[rows, :] * factor
                    o_ref[pl.ds((a * COMPS + b) * G + g, stations, stride=per_station), :] = value


def total(stations, comps, parts):
    counts = [len(of) for of in parts]
    return pl.pallas_call(
        functools.partial(total_kernel, stations, comps, counts),
        in_specs=[VMEM] * sum(counts),
        out_specs=VMEM,
        out_shape=jax.ShapeDtypeStruct((stations * COMPS * COMPS * G, LAG), f32),
        compiler_params=PARAMS,
        name="total",
    )(*[part for of in parts for part in of])


def swap(value, axis, mask):
    size = lax.axis_size(axis)
    return lax.ppermute(value, axis, [(i, i ^ mask) for i in range(size)])


def send(coded, mask):
    return swap(coded.astype(f16), "day", mask).astype(f32)


def owned_block(owner):
    ids = jnp.arange(owner.shape[0], dtype=jnp.int32)
    return jnp.sum(ids[None, :] * (owner[None, :] == ids[:, None]).astype(jnp.int32), axis=1)


def local(spectra, src_block, group_of, owner):
    stations = spectra.shape[3]
    days = lax.axis_size("day")
    ids = jnp.stack([lax.axis_index("day"), lax.axis_index("sta")])
    recv, signs, scale = receivers_by_freq(ids, spectra, group_of)
    columns = COMPS * stations
    table = jnp.asarray(lag_table(F, LAG))
    block_rows = S * stations // days

    if days == S and lax.axis_size("sta") == 4:
        y_first, z_first = (0, 1), (2,)
        ys, zs = [0, 1], range(0, days, 2)
        early, late = first_block(spectra, (z_first, y_first))
        far = swap(early, "sta", 2)
        beside, late = lax.optimization_barrier((swap(early, "sta", 1), late))
        far_late = swap(late, "sta", 2)
        far, recv, signs, scale, table = lax.optimization_barrier((far, recv, signs, scale, table))
        early = [early, beside, far, swap(far, "sta", 1)]
        pairs = [(mask, a) for mask in range(days) for a in z_first]
        cross = cross_spectra(pairs, z_first, ids, src_block, owner, recv, signs, early)
        kept_z, *away_z = lag_transform(
            [(False, [(y, z_first) for y in ys])] + [(True, [(y ^ z, z_first) for y in ys]) for z in zs[1:]],
            pairs,
            columns,
            cross,
            table,
            scale,
        )
        far_late, kept_z, away_z = lax.optimization_barrier((far_late, kept_z, away_z))
        late = [late, swap(late, "sta", 1), far_late, swap(far_late, "sta", 1)]
        pairs = [(mask, a) for mask in range(days) for a in y_first]
        cross = cross_spectra(pairs, y_first, ids, src_block, owner, recv, signs, late)
        lags = functools.partial(lag_transform, pairs=pairs, columns=columns, cross=cross, table=table, scale=scale)
        near, far = zs[: len(zs) // 2], zs[len(zs) // 2 :][::-1]
        (away_far,) = lags([(True, [(1 ^ z, y_first) for z in far])])
        arrived_far = send(away_far, 1)
        (away_near,) = lags([(True, [(1 ^ z, y_first) for z in near])])
        arrived_near = send(away_near, 1)
        arrived_z = [send(away_z[j], zs[1 + j]) for j in (0, 2, 1)]
        kept_near, kept_far = lags([(False, [(z, y_first) for z in of]) for of in (near, far)])
        merged = merge(kept_far, [arrived_far], len(far), 0)
        parts_far = [send(part, z) for part, z in zip(merged, far)]
        own_y, *merged = merge(kept_near, [arrived_near], len(near), 1)
        parts_y = [own_y] + [send(part, z) for part, z in zip(merged, near[1:])] + parts_far
        own_z, other = merge(kept_z, arrived_z, len(ys), 1)
        result = total(stations, (y_first, z_first), (parts_y, [own_z, send(other, 1)]))
        result = result.reshape(block_rows, COMPS * COMPS, G, LAG).transpose(0, 2, 1, 3)
        return result[None]

    every = tuple(range(COMPS))
    (first,) = first_block(spectra, (every,))
    gathered = lax.all_gather(first, "sta")
    blocks = [lax.dynamic_index_in_dim(gathered, src_block[k], 0, keepdims=False) for k in range(2)]
    order = jnp.arange(S, dtype=jnp.int32)
    pairs = [(mask, a) for mask in range(S) for a in every]
    cross = cross_spectra(pairs, every, jnp.zeros(2, jnp.int32), order[:2], order, recv, signs, blocks)
    outputs = [(False, [(mask, every) for mask in range(S)])]
    (partial,) = lag_transform(outputs, pairs, columns, cross, table, scale)
    partial = partial.reshape(S, G, COMPS * COMPS, stations, LAG).transpose(0, 3, 1, 2, 4)
    partial = partial.reshape(days, block_rows, G, COMPS * COMPS, LAG)
    ordered = jnp.take(partial, owned_block(owner), axis=0)
    return lax.psum_scatter(ordered, "day", scatter_dimension=0, tiled=True)


def solution(mesh):
    return jax.shard_map(
        local,
        mesh=mesh,
        in_specs=(P("day", None, None, "sta", None), P(), P(), P()),
        out_specs=P("day", "sta", None, None, None),
        check_vma=False,
    )
```

time: 43.8 us -> 39.9 us (0.911)
  waiting for transfers between devices: 12.6 us -> 6.56 us
  starting transfers between devices: 14.3 us -> 17.5 us
  local copies, waits for them, and re-layouts: 2.66 us -> 1.69 us
    ppermute x11 -> x15, waiting for transfers between devices: 12.6 us -> 6.56 us  [swap(): return lax.ppermute(value, axis, [(i, i ^ mask) for i in range(size)])]
    ppermute x11 -> x15, starting transfers between devices: 14.3 us -> 17.5 us  [swap(): return lax.ppermute(value, axis, [(i, i ^ mask) for i in range(size)])]
    unnamed x10 -> x12, local copies, waits for them, and re-layouts: 2.58 us -> 1.69 us
    pallas_call x6 -> x11, Pallas kernels: 12.5 us -> 12.5 us  [the longest x2 5.42 us: cross_spectra(): pl.pallas_call(functools.partial(cross_kernel, pairs, comps_of), in_specs...]
  transfers between devices with their start and end apart: 11 -> 15, of which waited for: 5 -> 7; matrix products, arithmetic and copies ran while one was open for 1% -> 1% of each run, Pallas kernels for 16% -> 22%
where the time goes in v4:
time: 39.9 us; the launch traced here: 39.6 us
  starting transfers between devices  17.5 us (44%)
  Pallas kernels  13.3 us (33%)
  waiting for transfers between devices  6.56 us (16%)
  local copies, waits for them, and re-layouts  1.69 us (4%)
    ppermute x15, starting transfers between devices, swap(): return lax.ppermute(value, axis, [(i, i ^ mask) for i in range(size)])  17.5 us
    ppermute x15, waiting for transfers between devices, swap(): return lax.ppermute(value, axis, [(i, i ^ mask) for i in range(size)])  6.56 us
    pallas_call x2, Pallas kernels, cross_spectra(): pl.pallas_call(functools.partial(cross_kernel, pairs, comps_of), in_specs...  5.42 us
    pallas_call x4, Pallas kernels, lag_transform(): pl.pallas_call(functools.partial(lag_kernel, outputs, pairs, columns), in...  3.21 us
    pallas_call x1, Pallas kernels, receivers_by_freq(): pl.pallas_call(receivers_kernel, grid=(COMPS,), in_specs=[SMEM, pl.BlockS...  2.78 us
    unnamed x12, local copies, waits for them, and re-layouts  1.69 us
    pallas_call x3, Pallas kernels, merge(): pl.pallas_call(functools.partial(merge_kernel, count, first), in_specs=[V...  0.81 us
  transfers between devices with their start and end apart: 15, of which 7 were waited for; matrix products, arithmetic and copies ran while one was open for 1% of the time, Pallas kernels for 22%

profile of v4, /device:TPU:0, one launch (start us, length us, event | category | flops | bytes accessed | tf_op | source)
XLA Modules:
  0.0 39.6 jit_solution(18023542392553481411)
XLA Ops:
  0.0 1.7 %copy-done = bf16[64,2,3,24,128]{4,3,2,1,0:T(8,128)(2,1)S(1)} copy-done((bf16[64,2,3,24,128]{4,3,2,1,0:T(8,128)(2,1)S(1)}, bf16[64,2,3,24,128]{4,3,2,1,0:T(8,128)(2,1)}, u32[]{:S(2)}) %copy-start) | copy-done | bytes 2359320
  1.7 0.3 first_block.1
  2.0 0.5 %collective-permute-start.1 = (bf16[1,4,128,128]{3,2,1,0:T(8,128)(2,1)S(1)}, bf16[1,4,128,128]{3,2,1,0:T(8,128)(2,1)S(1)}, u32[]{:S(2)}, u32[]{:S(2)}) collective-permute-start(bf16[1,4,128,128]{3,2,1,0:T(8,128)(2,1)S(1)} %get-tuple-element.34.rest_0_), channel_id=1, source_target_pairs={{0,1},{1,0},{2,3},{3,2},{4,5},{5,4},{6,7},{7,6},{8,9},{9,8},{10,11... | collective-permute-start | bytes 393224 | tf_op jit(solution)/shard_map/ppermute | solution.py:317
  2.5 2.6 %collective-permute-start = (bf16[1,4,128,128]{3,2,1,0:T(8,128)(2,1)S(1)}, bf16[1,4,128,128]{3,2,1,0:T(8,128)(2,1)S(1)}, u32[]{:S(2)}, u32[]{:S(2)}) collective-permute-start(bf16[1,4,128,128]{3,2,1,0:T(8,128)(2,1)S(1)} %get-tuple-element.34.rest_0_), channel_id=1, source_target_pairs={{0,2},{1,3},{2,0},{3,1},{4,6},{5,7},{6,4},{7,5},{8,10},{9,11},{10,... | collective-permute-start | bytes 393224 | tf_op jit(solution)/shard_map/ppermute | solution.py:317
  5.0 1.3 %collective-permute-start.3 = (bf16[2,4,128,128]{3,2,1,0:T(8,128)(2,1)S(1)}, bf16[2,4,128,128]{3,2,1,0:T(8,128)(2,1)S(1)}, u32[]{:S(2)}, u32[]{:S(2)}) collective-permute-start(bf16[2,4,128,128]{3,2,1,0:T(8,128)(2,1)S(1)} %get-tuple-element.41.rest_0_), channel_id=1, source_target_pairs={{0,2},{1,3},{2,0},{3,1},{4,6},{5,7},{6,4},{7,5},{8,10},{9,11},{10,... | collective-permute-start | bytes 786440 | tf_op jit(solution)/shard_map/ppermute | solution.py:317
  6.4 2.8 %receivers_by_freq.1 = (bf16[128,72,128]{2,1,0:T(8,128)(2,1)S(1)}, f32[4,128]{1,0:T(4,128)S(1)}, f32[2,128]{1,0:T(2,128)S(1)}) custom-call(s32[2]{0:T(128)S(1)} %pad_add_fusion.ids_ref, bf16[64,2,3,24,128]{4,3,2,1,0:T(8,128)(2,1)S(1)} %copy-done.1, s32[4,128]{1,0:T(4,128)S(1)} %bitcast.8), custom_call_target="tpu_custom_call" | custom-call | bytes 12582912 | tf_op jit(solution)/shard_map/receivers_by_freq/pallas_call | solution.py:107
  9.2 0.2 collective-permute-done.rest_2_
  9.4 0.5 %collective-permute-start.2 = (bf16[2,4,128,128]{3,2,1,0:T(8,128)(2,1)S(1)}, bf16[2,4,128,128]{3,2,1,0:T(8,128)(2,1)S(1)}, u32[]{:S(2)}, u32[]{:S(2)}) collective-permute-start(bf16[2,4,128,128]{3,2,1,0:T(8,128)(2,1)S(1)} %get-tuple-element.41.rest_0_), channel_id=1, source_target_pairs={{0,1},{1,0},{2,3},{3,2},{4,5},{5,4},{6,7},{7,6},{8,9},{9,8},{10,11... | collective-permute-start | bytes 786440 | tf_op jit(solution)/shard_map/ppermute | solution.py:317
  9.9 0.8 %collective-permute-done.4.rest_3_ = bf16[1,4,128,128]{3,2,1,0:T(8,128)(2,1)S(1)} collective-permute-done((bf16[1,4,128,128]{3,2,1,0:T(8,128)(2,1)S(1)}, bf16[1,4,128,128]{3,2,1,0:T(8,128)(2,1)S(1)}, u32[]{:S(2)}, u32[]{:S(2)}) %collective-permute-start.4) | collective-permute-done | bytes 131104 | tf_op jit(solution)/shard_map/ppermute | solution.py:317
  10.7 2.4 %cross_spectra.2.cross_ref = f32[4224,128]{1,0:T(8,128)S(1)} custom-call(s32[2]{0:T(128)S(1)} %pad_add_fusion.ids_ref, s32[2]{0:T(128)S(1)} %copy-done.4, s32[8]{0:T(128)S(1)} %copy-done.5, bf16[128,72,128]{2,1,0:T(8,128)(2,1)S(1)} %get-tuple-element.38.recv_ref, f32[4,128]{1,0:T(4,128)S(1)} %get-tuple-element.39.signs_ref, ...), custom_call_target="tpu_custom_call" | custom-call | bytes 10485760 | tf_op jit(solution)/shard_map/cross_spectra/pallas_call | solution.py:188
  13.2 1.0 %lag_transform.4 = (f32[288,128]{1,0:T(8,128)S(1)}, f32[296,128]{1,0:T(8,128)S(1)}, f32[296,128]{1,0:T(8,128)S(1)}, f32[296,128]{1,0:T(8,128)S(1)}) custom-call(f32[4224,128]{1,0:T(8,128)S(1)} %cross_spectra.2.cross_ref, f32[256,128]{1,0:T(8,128)S(1)} %copy-done.2, f32[2,128]{1,0:T(2,128)S(1)} %get-tuple-element.45.scale_ref), custom_call_target="tpu_custom_call" | custom-call | bytes 5242880 | tf_op jit(solution)/shard_map/lag_transform/pallas_call | solution.py:234
  14.2 0.5 %collective-permute-done.3.rest_2_ = bf16[2,4,128,128]{3,2,1,0:T(8,128)(2,1)S(1)} collective-permute-done((bf16[2,4,128,128]{3,2,1,0:T(8,128)(2,1)S(1)}, bf16[2,4,128,128]{3,2,1,0:T(8,128)(2,1)S(1)}, u32[]{:S(2)}, u32[]{:S(2)}) %collective-permute-start.3) | collective-permute-done | bytes 262176 | tf_op jit(solution)/shard_map/ppermute | solution.py:317
  14.8 1.5 %collective-permute-done.5.rest_3_ = bf16[2,4,128,128]{3,2,1,0:T(8,128)(2,1)S(1)} collective-permute-done((bf16[2,4,128,128]{3,2,1,0:T(8,128)(2,1)S(1)}, bf16[2,4,128,128]{3,2,1,0:T(8,128)(2,1)S(1)}, u32[]{:S(2)}, u32[]{:S(2)}) %collective-permute-start.5) | collective-permute-done | bytes 262176 | tf_op jit(solution)/shard_map/ppermute | solution.py:317
  16.3 3.0 %cross_spectra.3.cross_ref = f32[8448,128]{1,0:T(8,128)S(1)} custom-call(s32[2]{0:T(128)S(1)} %pad_add_fusion.ids_ref, s32[2]{0:T(128)S(1)} %copy-done.4, s32[8]{0:T(128)S(1)} %copy-done.5, bf16[128,72,128]{2,1,0:T(8,128)(2,1)S(1)} %get-tuple-element.38.recv_ref, f32[4,128]{1,0:T(4,128)S(1)} %get-tuple-element.39.signs_ref, ...), custom_call_target="tpu_custom_call" | custom-call | bytes 10485760 | tf_op jit(solution)/shard_map/cross_spectra/pallas_call | solution.py:188
  19.3 0.7 %lag_transform.7 = f32[584,128]{1,0:T(8,128)S(1)} custom-call(f32[8448,128]{1,0:T(8,128)S(1)} %cross_spectra.3.cross_ref, f32[256,128]{1,0:T(8,128)S(1)} %copy-done.2, f32[2,128]{1,0:T(2,128)S(1)} %get-tuple-element.45.scale_ref), custom_call_target="tpu_custom_call" | custom-call | bytes 5242880 | tf_op jit(solution)/shard_map/lag_transform/pallas_call | solution.py:234
  20.0 1.8 %collective-permute-start.8 = (f16[584,128]{1,0:T(8,128)(2,1)S(1)}, f16[584,128]{1,0:T(8,128)(2,1)S(1)}, u32[]{:S(2)}, u32[]{:S(2)}) collective-permute-start(f16[584,128]{1,0:T(8,128)(2,1)S(1)} %convert_element_type.58), channel_id=1, source_target_pairs={{0,4},{4,0},{8,12},{12,8},{16,20},{20,16},{24,28},{28,24},{1,5},{5... | collective-permute-start | bytes 448520 | tf_op jit(solution)/shard_map/ppermute | solution.py:317
  21.8 0.7 %lag_transform.6 = f32[584,128]{1,0:T(8,128)S(1)} custom-call(f32[8448,128]{1,0:T(8,128)S(1)} %cross_spectra.3.cross_ref, f32[256,128]{1,0:T(8,128)S(1)} %copy-done.2, f32[2,128]{1,0:T(2,128)S(1)} %get-tuple-element.45.scale_ref), custom_call_target="tpu_custom_call" | custom-call | bytes 5242880 | tf_op jit(solution)/shard_map/lag_transform/pallas_call | solution.py:234
  22.5 0.3 collective-permute-start.6
  22.9 2.9 %collective-permute-start.13 = (f16[296,128]{1,0:T(8,128)(2,1)S(1)}, f16[296,128]{1,0:T(8,128)(2,1)S(1)}, u32[]{:S(2)}, u32[]{:S(2)}) collective-permute-start(f16[296,128]{1,0:T(8,128)(2,1)S(1)} %convert_element_type.68), channel_id=1, source_target_pairs={{0,16},{4,20},{8,24},{12,28},{16,0},{20,4},{24,8},{28,12},{1,17},{... | collective-permute-start | bytes 227336 | tf_op jit(solution)/shard_map/ppermute | solution.py:317
  25.8 1.4 %collective-permute-start.12 = (f16[296,128]{1,0:T(8,128)(2,1)S(1)}, f16[296,128]{1,0:T(8,128)(2,1)S(1)}, u32[]{:S(2)}, u32[]{:S(2)}) collective-permute-start(f16[296,128]{1,0:T(8,128)(2,1)S(1)} %convert_element_type.66), channel_id=1, source_target_pairs={{0,24},{4,28},{8,16},{12,20},{16,8},{20,12},{24,0},{28,4},{1,25},{... | collective-permute-start | bytes 227336 | tf_op jit(solution)/shard_map/ppermute | solution.py:317
  27.2 0.3 collective-permute-start.11
  27.5 0.8 %lag_transform.5 = (f32[576,128]{1,0:T(8,128)S(1)}, f32[576,128]{1,0:T(8,128)S(1)}) custom-call(f32[8448,128]{1,0:T(8,128)S(1)} %cross_spectra.3.cross_ref, f32[256,128]{1,0:T(8,128)S(1)} %copy-done.2, f32[2,128]{1,0:T(2,128)S(1)} %get-tuple-element.45.scale_ref), custom_call_target="tpu_custom_call" | custom-call | bytes 5242880 | tf_op jit(solution)/shard_map/lag_transform/pallas_call | solution.py:234
  28.4 0.3 merge.4
  28.8 2.9 %collective-permute-start.10 = (f16[296,128]{1,0:T(8,128)(2,1)S(1)}, f16[296,128]{1,0:T(8,128)(2,1)S(1)}, u32[]{:S(2)}, u32[]{:S(2)}) collective-permute-start(f16[296,128]{1,0:T(8,128)(2,1)S(1)} %convert_element_type.62), channel_id=1, source_target_pairs={{0,16},{4,20},{8,24},{12,28},{16,0},{20,4},{24,8},{28,12},{1,17},{... | collective-permute-start | bytes 227336 | tf_op jit(solution)/shard_map/ppermute | solution.py:317
  31.7 1.4 %collective-permute-start.9 = (f16[296,128]{1,0:T(8,128)(2,1)S(1)}, f16[296,128]{1,0:T(8,128)(2,1)S(1)}, u32[]{:S(2)}, u32[]{:S(2)}) collective-permute-start(f16[296,128]{1,0:T(8,128)(2,1)S(1)} %convert_element_type.60), channel_id=1, source_target_pairs={{0,24},{4,28},{8,16},{12,20},{16,8},{20,12},{24,0},{28,4},{1,25},{... | collective-permute-start | bytes 227336 | tf_op jit(solution)/shard_map/ppermute | solution.py:317
  33.1 0.2 merge.3
  33.5 0.2 merge.5
  33.7 1.6 %collective-permute-start.14 = (f16[152,128]{1,0:T(8,128)(2,1)S(1)}, f16[152,128]{1,0:T(8,128)(2,1)S(1)}, u32[]{:S(2)}, u32[]{:S(2)}) collective-permute-start(f16[152,128]{1,0:T(8,128)(2,1)S(1)} %convert_element_type.70), channel_id=1, source_target_pairs={{0,4},{4,0},{8,12},{12,8},{16,20},{20,16},{24,28},{28,24},{1,5},{5... | collective-permute-start | bytes 116744 | tf_op jit(solution)/shard_map/ppermute | solution.py:317
  35.3 2.5 %collective-permute-done.14 = f16[152,128]{1,0:T(8,128)(2,1)S(1)} collective-permute-done((f16[152,128]{1,0:T(8,128)(2,1)S(1)}, f16[152,128]{1,0:T(8,128)(2,1)S(1)}, u32[]{:S(2)}, u32[]{:S(2)}) %collective-permute-start.14) | collective-permute-done | bytes 38944 | tf_op jit(solution)/shard_map/ppermute | solution.py:317
  37.8 0.2 collective-permute-done.9
  38.0 0.8 %collective-permute-done.7 = f16[296,128]{1,0:T(8,128)(2,1)S(1)} collective-permute-done((f16[296,128]{1,0:T(8,128)(2,1)S(1)}, f16[296,128]{1,0:T(8,128)(2,1)S(1)}, u32[]{:S(2)}, u32[]{:S(2)}) %collective-permute-start.7) | collective-permute-done | bytes 75808 | tf_op jit(solution)/shard_map/ppermute | solution.py:317
  38.8 0.8 %total.1 = f32[432,128]{1,0:T(8,128)} custom-call(f32[288,128]{1,0:T(8,128)S(1)} %get-tuple-element.52.refs_0_, f32[296,128]{1,0:T(8,128)S(1)} %convert_element_type.57.refs_1_, f32[296,128]{1,0:T(8,128)S(1)} %convert_element_type.61.refs_2_, f32[296,128]{1,0:T(8,128)S(1)} %convert_element_type.63.refs_3_, f32[144,128]{1,0:T(8,128)S(1)} %get-tuple-element.61.refs_4_, ...), custom_call_target="tpu_custom_call" | custom-call | tf_op jit(solution)/shard_map/total/pallas_call | solution.py:305
  (41 shorter events, 0.5 us)
Async XLA Ops:
  0.0 1.7 %copy-start = (bf16[64,2,3,24,128]{4,3,2,1,0:T(8,128)(2,1)S(1)}, bf16[64,2,3,24,128]{4,3,2,1,0:T(8,128)(2,1)}, u32[]{:S(2)}) copy-start(bf16[64,2,3,24,128]{4,3,2,1,0:T(8,128)(2,1)} %x_ref.3) | copy-start | bytes 7077892
  1.7 4.7 %copy-start.1 = (bf16[64,2,3,24,128]{4,3,2,1,0:T(8,128)(2,1)S(1)}, bf16[64,2,3,24,128]{4,3,2,1,0:T(8,128)(2,1)}, u32[]{:S(2)}) copy-start(bf16[64,2,3,24,128]{4,3,2,1,0:T(8,128)(2,1)} %x_ref.3) | copy-start | bytes 7077892
  1.7 4.7 %copy-start.3 = (s32[512]{0:T(512)S(1)}, s32[512]{0:T(512)}, u32[]{:S(2)}) copy-start(s32[512]{0:T(512)} %param.7) | copy-start | bytes 6148
  1.7 9.1 %copy-start.4 = (s32[2]{0:T(128)S(1)}, s32[2]{0:T(128)}, u32[]{:S(2)}) copy-start(s32[2]{0:T(128)} %src_block_ref.3) | copy-start | bytes 28
  1.7 9.1 %copy-start.5 = (s32[8]{0:T(128)S(1)}, s32[8]{0:T(128)}, u32[]{:S(2)}) copy-start(s32[8]{0:T(128)} %owner_ref.3) | copy-start | bytes 100
  2.0 3.1 %collective-permute-start.1 = (bf16[1,4,128,128]{3,2,1,0:T(8,128)(2,1)S(1)}, bf16[1,4,128,128]{3,2,1,0:T(8,128)(2,1)S(1)}, u32[]{:S(2)}, u32[]{:S(2)}) collective-permute-start(bf16[1,4,128,128]{3,2,1,0:T(8,128)(2,1)S(1)} %get-tuple-element.34.rest_0_), channel_id=1, source_target_pairs={{0,1},{1,0},{2,3},{3,2},{4,5},{5,4},{6,7},{7,6},{8,9},{9,8},{10,11... | collective-permute-start | bytes 393224 | tf_op jit(solution)/shard_map/ppermute | solution.py:317
  2.5 6.9 %collective-permute-start = (bf16[1,4,128,128]{3,2,1,0:T(8,128)(2,1)S(1)}, bf16[1,4,128,128]{3,2,1,0:T(8,128)(2,1)S(1)}, u32[]{:S(2)}, u32[]{:S(2)}) collective-permute-start(bf16[1,4,128,128]{3,2,1,0:T(8,128)(2,1)S(1)} %get-tuple-element.34.rest_0_), channel_id=1, source_target_pairs={{0,2},{1,3},{2,0},{3,1},{4,6},{5,7},{6,4},{7,5},{8,10},{9,11},{10,... | collective-permute-start | bytes 393224 | tf_op jit(solution)/shard_map/ppermute | solution.py:317
  5.0 9.7 %collective-permute-start.3 = (bf16[2,4,128,128]{3,2,1,0:T(8,128)(2,1)S(1)}, bf16[2,4,128,128]{3,2,1,0:T(8,128)(2,1)S(1)}, u32[]{:S(2)}, u32[]{:S(2)}) collective-permute-start(bf16[2,4,128,128]{3,2,1,0:T(8,128)(2,1)S(1)} %get-tuple-element.41.rest_0_), channel_id=1, source_target_pairs={{0,2},{1,3},{2,0},{3,1},{4,6},{5,7},{6,4},{7,5},{8,10},{9,11},{10,... | collective-permute-start | bytes 786440 | tf_op jit(solution)/shard_map/ppermute | solution.py:317
  9.4 3.8 %copy-start.2 = (f32[256,128]{1,0:T(8,128)S(1)}, f32[256,128]{1,0:T(8,128)}, u32[]{:S(2)}) copy-start(f32[256,128]{1,0:T(8,128)} %constant.11.clone.table_ref) | copy-start | bytes 393220
  9.4 1.3 %collective-permute-start.4 = (bf16[1,4,128,128]{3,2,1,0:T(8,128)(2,1)S(1)}, bf16[1,4,128,128]{3,2,1,0:T(8,128)(2,1)S(1)}, u32[]{:S(2)}, u32[]{:S(2)}) collective-permute-start(bf16[1,4,128,128]{3,2,1,0:T(8,128)(2,1)S(1)} %collective-permute-done.rest_2_), channel_id=1, source_target_pairs={{0,1},{1,0},{2,3},{3,2},{4,5},{5,4},{6,7},{7,6},{8,9},{9,8},{10,11... | collective-permute-start | bytes 393224 | tf_op jit(solution)/shard_map/ppermute | solution.py:317
  9.4 5.4 %collective-permute-start.2 = (bf16[2,4,128,128]{3,2,1,0:T(8,128)(2,1)S(1)}, bf16[2,4,128,128]{3,2,1,0:T(8,128)(2,1)S(1)}, u32[]{:S(2)}, u32[]{:S(2)}) collective-permute-start(bf16[2,4,128,128]{3,2,1,0:T(8,128)(2,1)S(1)} %get-tuple-element.41.rest_0_), channel_id=1, source_target_pairs={{0,1},{1,0},{2,3},{3,2},{4,5},{5,4},{6,7},{7,6},{8,9},{9,8},{10,11... | collective-permute-start | bytes 786440 | tf_op jit(solution)/shard_map/ppermute | solution.py:317
  14.7 1.5 %collective-permute-start.5 = (bf16[2,4,128,128]{3,2,1,0:T(8,128)(2,1)S(1)}, bf16[2,4,128,128]{3,2,1,0:T(8,128)(2,1)S(1)}, u32[]{:S(2)}, u32[]{:S(2)}) collective-permute-start(bf16[2,4,128,128]{3,2,1,0:T(8,128)(2,1)S(1)} %collective-permute-done.3.rest_2_), channel_id=1, source_target_pairs={{0,1},{1,0},{2,3},{3,2},{4,5},{5,4},{6,7},{7,6},{8,9},{9,8},{10,11... | collective-permute-start | bytes 786440 | tf_op jit(solution)/shard_map/ppermute | solution.py:317
  20.0 8.4 %collective-permute-start.8 = (f16[584,128]{1,0:T(8,128)(2,1)S(1)}, f16[584,128]{1,0:T(8,128)(2,1)S(1)}, u32[]{:S(2)}, u32[]{:S(2)}) collective-permute-start(f16[584,128]{1,0:T(8,128)(2,1)S(1)} %convert_element_type.58), channel_id=1, source_target_pairs={{0,4},{4,0},{8,12},{12,8},{16,20},{20,16},{24,28},{28,24},{1,5},{5... | collective-permute-start | bytes 448520 | tf_op jit(solution)/shard_map/ppermute | solution.py:317
  22.5 9.1 %collective-permute-start.6 = (f16[584,128]{1,0:T(8,128)(2,1)S(1)}, f16[584,128]{1,0:T(8,128)(2,1)S(1)}, u32[]{:S(2)}, u32[]{:S(2)}) collective-permute-start(f16[584,128]{1,0:T(8,128)(2,1)S(1)} %convert_element_type.54), channel_id=1, source_target_pairs={{0,4},{4,0},{8,12},{12,8},{16,20},{20,16},{24,28},{28,24},{1,5},{5... | collective-permute-start | bytes 448520 | tf_op jit(solution)/shard_map/ppermute | solution.py:317
  22.9 10.5 %collective-permute-start.13 = (f16[296,128]{1,0:T(8,128)(2,1)S(1)}, f16[296,128]{1,0:T(8,128)(2,1)S(1)}, u32[]{:S(2)}, u32[]{:S(2)}) collective-permute-start(f16[296,128]{1,0:T(8,128)(2,1)S(1)} %convert_element_type.68), channel_id=1, source_target_pairs={{0,16},{4,20},{8,24},{12,28},{16,0},{20,4},{24,8},{28,12},{1,17},{... | collective-permute-start | bytes 227336 | tf_op jit(solution)/shard_map/ppermute | solution.py:317
  25.8 7.6 %collective-permute-start.12 = (f16[296,128]{1,0:T(8,128)(2,1)S(1)}, f16[296,128]{1,0:T(8,128)(2,1)S(1)}, u32[]{:S(2)}, u32[]{:S(2)}) collective-permute-start(f16[296,128]{1,0:T(8,128)(2,1)S(1)} %convert_element_type.66), channel_id=1, source_target_pairs={{0,24},{4,28},{8,16},{12,20},{16,8},{20,12},{24,0},{28,4},{1,25},{... | collective-permute-start | bytes 227336 | tf_op jit(solution)/shard_map/ppermute | solution.py:317
  27.2 6.2 %collective-permute-start.11 = (f16[296,128]{1,0:T(8,128)(2,1)S(1)}, f16[296,128]{1,0:T(8,128)(2,1)S(1)}, u32[]{:S(2)}, u32[]{:S(2)}) collective-permute-start(f16[296,128]{1,0:T(8,128)(2,1)S(1)} %convert_element_type.64), channel_id=1, source_target_pairs={{0,8},{4,12},{8,0},{12,4},{16,24},{20,28},{24,16},{28,20},{1,9},{5... | collective-permute-start | bytes 227336 | tf_op jit(solution)/shard_map/ppermute | solution.py:317
  28.8 9.0 %collective-permute-start.10 = (f16[296,128]{1,0:T(8,128)(2,1)S(1)}, f16[296,128]{1,0:T(8,128)(2,1)S(1)}, u32[]{:S(2)}, u32[]{:S(2)}) collective-permute-start(f16[296,128]{1,0:T(8,128)(2,1)S(1)} %convert_element_type.62), channel_id=1, source_target_pairs={{0,16},{4,20},{8,24},{12,28},{16,0},{20,4},{24,8},{28,12},{1,17},{... | collective-permute-start | bytes 227336 | tf_op jit(solution)/shard_map/ppermute | solution.py:317
  31.7 6.3 %collective-permute-start.9 = (f16[296,128]{1,0:T(8,128)(2,1)S(1)}, f16[296,128]{1,0:T(8,128)(2,1)S(1)}, u32[]{:S(2)}, u32[]{:S(2)}) collective-permute-start(f16[296,128]{1,0:T(8,128)(2,1)S(1)} %convert_element_type.60), channel_id=1, source_target_pairs={{0,24},{4,28},{8,16},{12,20},{16,8},{20,12},{24,0},{28,4},{1,25},{... | collective-permute-start | bytes 227336 | tf_op jit(solution)/shard_map/ppermute | solution.py:317
  33.3 5.5 %collective-permute-start.7 = (f16[296,128]{1,0:T(8,128)(2,1)S(1)}, f16[296,128]{1,0:T(8,128)(2,1)S(1)}, u32[]{:S(2)}, u32[]{:S(2)}) collective-permute-start(f16[296,128]{1,0:T(8,128)(2,1)S(1)} %convert_element_type.56), channel_id=1, source_target_pairs={{0,8},{4,12},{8,0},{12,4},{16,24},{20,28},{24,16},{28,20},{1,9},{5... | collective-permute-start | bytes 227336 | tf_op jit(solution)/shard_map/ppermute | solution.py:317
  33.7 4.0 %collective-permute-start.14 = (f16[152,128]{1,0:T(8,128)(2,1)S(1)}, f16[152,128]{1,0:T(8,128)(2,1)S(1)}, u32[]{:S(2)}, u32[]{:S(2)}) collective-permute-start(f16[152,128]{1,0:T(8,128)(2,1)S(1)} %convert_element_type.70), channel_id=1, source_target_pairs={{0,4},{4,0},{8,12},{12,8},{16,20},{20,16},{24,28},{28,24},{1,5},{5... | collective-permute-start | bytes 116744 | tf_op jit(solution)/shard_map/ppermute | solution.py:317

commit v5 on v4

--- a/solution.py
+++ b/solution.py
@@ -14,6 +14,7 @@
 SB = 4
 S = 8
 COMPS = 3
+XF = F + 8
 XS = 2 * F + 8
 
 f32 = jnp.float32
@@ -143,34 +144,31 @@
     return jnp.ceil(jnp.log(jnp.maximum(largest, 1e-30)) * np.float32(1.4426950408889634)).astype(jnp.int32)
 
 
-def rows_of(pairs):
-    return -(-len(pairs) // 8) * 8
-
-
-def cross_kernel(pairs, comps_of, ids_ref, src_block_ref, owner_ref, recv_ref, signs_ref, *rest):
+def rows_of(comps):
+    return -(-S * len(comps) // 8) * 8
+
+
+def cross_kernel(comps, ids_ref, src_block_ref, owner_ref, recv_ref, signs_ref, *rest):
     blocks, (o_ref, src) = rest[:-2], rest[-2:]
-    rows = rows_of(pairs)
+    rows = rows_of(comps)
     columns = recv_ref.shape[1]
     half = recv_ref.shape[2] // 2
-    for mask in sorted({mask for mask, _ in pairs}):
-        dest = ids_ref[0] ^ mask
-        source = jnp.int32(0)
-        for k in range(S):
-            source = source + jnp.where(owner_ref[k] == dest, k, 0)
-        which = ids_ref[1] ^ src_block_ref[source // SB]
-        station = source % SB
+    for k in range(S // SB):
+        which = ids_ref[1] ^ src_block_ref[k]
         for j in range(len(blocks)):
 
             @pl.when(which == j)
             def _():
-                for at, (pair_mask, a) in enumerate(pairs):
-                    if pair_mask == mask:
-                        src[pl.ds(at, F, stride=rows), :] = blocks[j][comps_of.index(a), station].astype(f32)
-
+                for station in range(SB):
+                    mask = ids_ref[0] ^ owner_ref[k * SB + station]
+                    for a in range(len(comps)):
+                        src[mask * len(comps) + a, 0:F] = blocks[j][a, station].astype(f32)
+
+    flat = src.reshape(rows * XF, src.shape[2])
     signs = signs_ref[...]
 
     def one_freq(f, carry):
-        plain = src[pl.ds(pl.multiple_of(f * rows, 8), rows), :]
+        plain = flat[pl.ds(f, rows, stride=XF), :]
         rolled = pltpu.roll(plain, half, 1)
         left = [plain * signs[0:1], plain * signs[1:2], rolled * signs[2:3], rolled * signs[3:4]]
         left = jnp.concatenate(left, axis=0).astype(bf16)
@@ -182,23 +180,23 @@
     lax.fori_loop(0, F, one_freq, 0, unroll=F)
 
 
-def cross_spectra(pairs, comps_of, ids, src_block, owner, recv, signs, blocks):
+def cross_spectra(comps, ids, src_block, owner, recv, signs, blocks):
     depth = recv.shape[2]
-    rows = rows_of(pairs)
-    return pl.pallas_call(
-        functools.partial(cross_kernel, pairs, comps_of),
+    rows = rows_of(comps)
+    return pl.pallas_call(
+        functools.partial(cross_kernel, comps),
         in_specs=[SMEM] * 3 + [VMEM] * (2 + len(blocks)),
         out_specs=VMEM,
         out_shape=jax.ShapeDtypeStruct((G * rows * XS, 128), f32),
-        scratch_shapes=[pltpu.VMEM((F * rows, depth), f32)],
+        scratch_shapes=[pltpu.VMEM((rows, XF, depth), f32)],
         compiler_params=PARAMS,
         cost_estimate=pl.CostEstimate(flops=0, bytes_accessed=10 << 20, transcendentals=0),
         name="cross_spectra",
     )(ids, src_block, owner, recv, signs, *blocks)
 
 
-def lag_kernel(outputs, pairs, columns, cross_ref, table_ref, scale_ref, *o_refs):
-    rows = rows_of(pairs)
+def lag_kernel(outputs, held, columns, cross_ref, table_ref, scale_ref, *o_refs):
+    rows = rows_of(held)
     table_high, table_low = two_terms(table_ref[...])
     table = jnp.concatenate([table_high, table_low], axis=1)
     for (coded, blocks_of), o_ref in zip(outputs, o_refs):
@@ -208,7 +206,7 @@
             turned = []
             for g in range(G):
                 for a in comps:
-                    first = (g * rows + pairs.index((mask, a))) * XS
+                    first = (g * rows + mask * len(held) + held.index(a)) * XS
                     turned.append(cross_ref[first : first + 2 * F, :].T[:columns])
             high, low = two_terms(jnp.concatenate(turned, axis=0))
             both = jnp.dot(high, table, preferred_element_type=f32)
@@ -226,13 +224,13 @@
             o_ref[done:] = exponents
 
 
-def lag_transform(outputs, pairs, columns, cross, table, scale):
+def lag_transform(outputs, held, columns, cross, table, scale):
     shapes = []
     for coded, blocks_of in outputs:
         size = sum(G * len(comps) * columns for _, comps in blocks_of) + (TAIL if coded else 0)
         shapes.append(jax.ShapeDtypeStruct((size, LAG), f32))
     return pl.pallas_call(
-        functools.partial(lag_kernel, outputs, pairs, columns),
+        functools.partial(lag_kernel, outputs, held, columns),
         in_specs=[VMEM] * 3,
         out_specs=[VMEM] * len(outputs),
         out_shape=shapes,
@@ -242,74 +240,72 @@
     )(cross, table, scale)
 
 
-def factor_of(coded, size, at):
-    return power_of_two(coded[size + at : size + at + 1, 0:1].astype(jnp.int32) - TOP)
-
-
-def store_coded(o_ref, value):
-    size = value.shape[0]
-    e = exponent_of(value)
-    o_ref[0:size] = value * power_of_two(TOP - e)
-    o_ref[size:] = jnp.broadcast_to(e.astype(f32), (TAIL, LAG))
-
-
-def merge_kernel(count, first, kept_ref, *refs):
-    size = kept_ref.shape[0] // count
-    arrived, o_refs = refs[:-count], refs[-count:]
-    factors = [[factor_of(ref, count * size, j) for j in range(count)] for ref in arrived]
-    for j in range(count):
-        rows = slice(j * size, (j + 1) * size)
-        value = kept_ref[rows]
-        for ref, factor in zip(arrived, factors):
-            value = value + ref[rows] * factor[j]
-        if j < first:
-            o_refs[j][...] = value
-        else:
-            store_coded(o_refs[j], value)
-
-
-def merge(kept, arrived, count, first):
-    size = kept.shape[0] // count
-    plain, coded = jax.ShapeDtypeStruct((size, LAG), f32), jax.ShapeDtypeStruct((size + TAIL, LAG), f32)
-    return pl.pallas_call(
-        functools.partial(merge_kernel, count, first),
-        in_specs=[VMEM] * (1 + len(arrived)),
-        out_specs=[VMEM] * count,
-        out_shape=[plain] * first + [coded] * (count - first),
+def factor_of(coded_ref, at):
+    return power_of_two(coded_ref[at : at + 1, 0:1].astype(jnp.int32) - TOP)
+
+
+def merge_kernel(counts, outputs, *refs):
+    sums, o_refs = refs[: 2 * len(counts)], refs[2 * len(counts) :]
+    for (coded, blocks_of), o_ref in zip(outputs, o_refs):
+        exponents = jnp.zeros((TAIL, LAG), f32)
+        done = 0
+        for at, (i, j) in enumerate(blocks_of):
+            kept_ref, arrived_ref = sums[2 * i : 2 * i + 2]
+            size = kept_ref.shape[0] // counts[i]
+            rows = slice(j * size, (j + 1) * size)
+            value = kept_ref[rows] + arrived_ref[rows] * factor_of(arrived_ref, counts[i] * size + j)
+            if coded:
+                e = exponent_of(value)
+                value = value * power_of_two(TOP - e)
+                exponents = jnp.where(lax.broadcasted_iota(jnp.int32, (TAIL, LAG), 0) == at, e.astype(f32), exponents)
+            o_ref[done : done + size] = value
+            done += size
+        if coded:
+            o_ref[done:] = exponents
+
+
+def merge(sums, outputs):
+    shapes = []
+    for coded, blocks_of in outputs:
+        size = sum(sums[i][1].shape[0] // sums[i][0] for i, _ in blocks_of) + (TAIL if coded else 0)
+        shapes.append(jax.ShapeDtypeStruct((size, LAG), f32))
+    return pl.pallas_call(
+        functools.partial(merge_kernel, [count for count, _, _ in sums], outputs),
+        in_specs=[VMEM] * (2 * len(sums)),
+        out_specs=[VMEM] * len(outputs),
+        out_shape=shapes,
         compiler_params=PARAMS,
         name="merge",
-    )(kept, *arrived)
-
-
-def total_kernel(stations, comps, counts, *refs):
-    refs, o_ref = list(refs[:-1]), refs[-1]
+    )(*[array for _, *arrays in sums for array in arrays])
+
+
+def total_kernel(stations, terms, *refs):
+    refs, o_ref = refs[:-1], refs[-1]
     per_station = G * COMPS * COMPS
-    for of, count in zip(comps, counts):
-        own_ref, parts, refs = refs[0], refs[1:count], refs[count:]
-        size = own_ref.shape[0]
-        factors = [factor_of(part, size, 0) for part in parts]
-        at = 0
+    for comps, parts in terms:
+        factors = [None if at is None else factor_of(refs[i], at) for i, _, at in parts]
+        done = 0
         for g in range(G):
-            for a in of:
+            for a in comps:
                 for b in range(COMPS):
-                    rows = pl.ds(at, stations)
-                    at += stations
-                    value = own_ref[rows, :]
-                    for part, factor in zip(parts, factors):
-                        value = value + part[rows, :] * factor
+                    value = None
+                    for (i, first, _), factor in zip(parts, factors):
+                        part = refs[i][first + done : first + done + stations, :]
+                        part = part if factor is None else part * factor
+                        value = part if value is None else value + part
+                    done += stations
                     o_ref[pl.ds((a * COMPS + b) * G + g, stations, stride=per_station), :] = value
 
 
-def total(stations, comps, parts):
-    counts = [len(of) for of in parts]
-    return pl.pallas_call(
-        functools.partial(total_kernel, stations, comps, counts),
-        in_specs=[VMEM] * sum(counts),
+def total(stations, terms, arrays):
+    return pl.pallas_call(
+        functools.partial(total_kernel, stations, terms),
+        in_specs=[VMEM] * len(arrays),
         out_specs=VMEM,
         out_shape=jax.ShapeDtypeStruct((stations * COMPS * COMPS * G, LAG), f32),
         compiler_params=PARAMS,
         name="total",
-    )(*[part for of in parts for part in of])
+    )(*arrays)
 
 
 def swap(value, axis, mask):
@@ -336,42 +332,50 @@
     block_rows = S * stations // days
 
     if days == S and lax.axis_size("sta") == 4:
-        y_first, z_first = (0, 1), (2,)
-        ys, zs = [0, 1], range(0, days, 2)
-        early, late = first_block(spectra, (z_first, y_first))
-        far = swap(early, "sta", 2)
+        ahead, rest = (2,), (0, 1)
+        near, far = [0, 2], [6, 4]
+        early, late = first_block(spectra, (ahead, rest))
+        across = swap(early, "sta", 2)
         beside, late = lax.optimization_barrier((swap(early, "sta", 1), late))
-        far_late = swap(late, "sta", 2)
-        far, recv, signs, scale, table = lax.optimization_barrier((far, recv, signs, scale, table))
-        early = [early, beside, far, swap(far, "sta", 1)]
-        pairs = [(mask, a) for mask in range(days) for a in z_first]
-        cross = cross_spectra(pairs, z_first, ids, src_block, owner, recv, signs, early)
-        kept_z, *away_z = lag_transform(
-            [(False, [(y, z_first) for y in ys])] + [(True, [(y ^ z, z_first) for y in ys]) for z in zs[1:]],
-            pairs,
+        across_late = swap(late, "sta", 2)
+        across, recv, signs, scale, table = lax.optimization_barrier((across, recv, signs, scale, table))
+        early = [early, beside, across, swap(across, "sta", 1)]
+        cross = cross_spectra(ahead, ids, src_block, owner, recv, signs, early)
+        away, kept = lag_transform(
+            [(True, [(1 ^ z, ahead) for z in near + far]), (False, [(z, ahead) for z in near + far])],
+            ahead,
             columns,
             cross,
             table,
             scale,
         )
-        far_late, kept_z, away_z = lax.optimization_barrier((far_late, kept_z, away_z))
-        late = [late, swap(late, "sta", 1), far_late, swap(far_late, "sta", 1)]
-        pairs = [(mask, a) for mask in range(days) for a in y_first]
-        cross = cross_spectra(pairs, y_first, ids, src_block, owner, recv, signs, late)
-        lags = functools.partial(lag_transform, pairs=pairs, columns=columns, cross=cross, table=table, scale=scale)
-        near, far = zs[: len(zs) // 2], zs[len(zs) // 2 :][::-1]
-        (away_far,) = lags([(True, [(1 ^ z, y_first) for z in far])])
+        across_late, away, kept = lax.optimization_barrier((across_late, away, kept))
+        arrived = send(away, 1)
+        late = [late, swap(late, "sta", 1), across_late, swap(across_late, "sta", 1)]
+        cross = cross_spectra(rest, ids, src_block, owner, recv, signs, late)
+        lags = functools.partial(lag_transform, held=rest, columns=columns, cross=cross, table=table, scale=scale)
+        (away_far,) = lags([(True, [(1 ^ z, rest) for z in far])])
+        away_far, cross = lax.optimization_barrier((away_far, cross))
         arrived_far = send(away_far, 1)
-        (away_near,) = lags([(True, [(1 ^ z, y_first) for z in near])])
+        (away_near,) = lags([(True, [(1 ^ z, rest) for z in near])], cross=cross)
         arrived_near = send(away_near, 1)
-        arrived_z = [send(away_z[j], zs[1 + j]) for j in (0, 2, 1)]
-        kept_near, kept_far = lags([(False, [(z, y_first) for z in of]) for of in (near, far)])
-        merged = merge(kept_far, [arrived_far], len(far), 0)
-        parts_far = [send(part, z) for part, z in zip(merged, far)]
-        own_y, *merged = merge(kept_near, [arrived_near], len(near), 1)
-        parts_y = [own_y] + [send(part, z) for part, z in zip(merged, near[1:])] + parts_far
-        own_z, other = merge(kept_z, arrived_z, len(ys), 1)
-        result = total(stations, (y_first, z_first), (parts_y, [own_z, send(other, 1)]))
+        kept, away = merge([(4, kept, arrived)], [(False, [(0, 0), (0, 1)]), (True, [(0, 3), (0, 2)])])
+        arrived = send(away, 4)
+        kept_near, kept_far = lags([(False, [(z, rest) for z in of]) for of in (near, far)], cross=cross)
+        by_6, by_4 = merge([(2, kept_far, arrived_far)], [(True, [(0, 0)]), (True, [(0, 1)])])
+        kept_near, by_6, by_4 = lax.optimization_barrier((kept_near, by_6, by_4))
+        by_6 = send(by_6, 6)
+        by_4 = send(by_4, 4)
+        own_rest, by_2 = merge([(2, kept_near, arrived_near)], [(False, [(0, 0)]), (True, [(0, 1)])])
+        by_2 = send(by_2, 2)
+        own_ahead, ahead_by_2 = merge([(2, kept, arrived)], [(False, [(0, 0)]), (True, [(0, 1)])])
+        ahead_by_2 = send(ahead_by_2, 2)
+        size, ahead_size = own_rest.shape[0], own_ahead.shape[0]
+        terms = [
+            (rest, [(0, 0, None), (1, 0, size), (2, 0, size), (3, 0, size)]),
+            (ahead, [(4, 0, None), (5, 0, ahead_size)]),
+        ]
+        result = total(stations, terms, [own_rest, by_2, by_6, by_4, own_ahead, ahead_by_2])
         result = result.reshape(block_rows, COMPS * COMPS, G, LAG).transpose(0, 2, 1, 3)
         return result[None]
 
@@ -380,10 +384,9 @@
     gathered = lax.all_gather(first, "sta")
     blocks = [lax.dynamic_index_in_dim(gathered, src_block[k], 0, keepdims=False) for k in range(2)]
     order = jnp.arange(S, dtype=jnp.int32)
-    pairs = [(mask, a) for mask in range(S) for a in every]
-    cross = cross_spectra(pairs, every, jnp.zeros(2, jnp.int32), order[:2], order, recv, signs, blocks)
+    cross = cross_spectra(every, jnp.zeros(2, jnp.int32), order[:2], order, recv, signs, blocks)
     outputs = [(False, [(mask, every) for mask in range(S)])]
-    (partial,) = lag_transform(outputs, pairs, columns, cross, table, scale)
+    (partial,) = lag_transform(outputs, every, columns, cross, table, scale)
     partial = partial.reshape(S, G, COMPS * COMPS, stations, LAG).transpose(0, 3, 1, 2, 4)
     partial = partial.reshape(days, block_rows, G, COMPS * COMPS, LAG)
     ordered = jnp.take(partial, owned_block(owner), axis=0)

time: 39.9 us -> 37.9 us (0.950)
  waiting for transfers between devices: 6.56 us -> 5.23 us
  Pallas kernels: 13.3 us -> 12.6 us
    ppermute x15 -> x14, waiting for transfers between devices: 6.56 us -> 5.23 us  [swap(): return lax.ppermute(value, axis, [(i, i ^ mask) for i in range(size)])]
    pallas_call x10 -> x11, Pallas kernels: 10.2 us -> 9.54 us  [the longest x2 4.34 us: cross_spectra(): pl.pallas_call(functools.partial(cross_kernel, comps), in_specs=[SMEM] *...]
    ppermute x15 -> x14, starting transfers between devices: 17.5 us -> 17.7 us  [swap(): return lax.ppermute(value, axis, [(i, i ^ mask) for i in range(size)])]
  transfers between devices with their start and end apart: 15 -> 14, of which waited for: 7 -> 4; matrix products, arithmetic and copies ran while one was open for 1% -> 1% of each run, Pallas kernels for 22% -> 31%
where the time goes in v5:
time: 37.9 us; the launch traced here: 37.8 us
  starting transfers between devices  17.7 us (47%)
  Pallas kernels  12.6 us (33%)
  waiting for transfers between devices  5.23 us (14%)
  local copies, waits for them, and re-layouts  1.69 us (4%)
    ppermute x14, starting transfers between devices, swap(): return lax.ppermute(value, axis, [(i, i ^ mask) for i in range(size)])  17.7 us
    ppermute x14, waiting for transfers between devices, swap(): return lax.ppermute(value, axis, [(i, i ^ mask) for i in range(size)])  5.23 us
    pallas_call x2, Pallas kernels, cross_spectra(): pl.pallas_call(functools.partial(cross_kernel, comps), in_specs=[SMEM] *...  4.34 us
    pallas_call x4, Pallas kernels, lag_transform(): pl.pallas_call(functools.partial(lag_kernel, outputs, held, columns), in_...  3.3 us
    pallas_call x1, Pallas kernels, receivers_by_freq(): pl.pallas_call(receivers_kernel, grid=(COMPS,), in_specs=[SMEM, pl.BlockS...  2.78 us
    unnamed x12, local copies, waits for them, and re-layouts  1.69 us
    pallas_call x4, Pallas kernels, merge(): pl.pallas_call(functools.partial(merge_kernel, [count for count, _, _ in...  1.12 us
    pallas_call x1, Pallas kernels, total(): pl.pallas_call(functools.partial(total_kernel, stations, terms), in_specs...  0.78 us
  transfers between devices with their start and end apart: 14, of which 4 were waited for; matrix products, arithmetic and copies ran while one was open for 1% of the time, Pallas kernels for 31%

profile of v5, /device:TPU:0, one launch (start us, length us, event | category | flops | bytes accessed | tf_op | source)
XLA Modules:
  0.0 37.8 jit_solution(15631751824814554000)
XLA Ops:
  0.0 1.7 %copy-done = bf16[64,2,3,24,128]{4,3,2,1,0:T(8,128)(2,1)S(1)} copy-done((bf16[64,2,3,24,128]{4,3,2,1,0:T(8,128)(2,1)S(1)}, bf16[64,2,3,24,128]{4,3,2,1,0:T(8,128)(2,1)}, u32[]{:S(2)}) %copy-start) | copy-done | bytes 2359320
  1.7 0.3 first_block.1
  2.0 0.5 %collective-permute-start.1 = (bf16[1,4,128,128]{3,2,1,0:T(8,128)(2,1)S(1)}, bf16[1,4,128,128]{3,2,1,0:T(8,128)(2,1)S(1)}, u32[]{:S(2)}, u32[]{:S(2)}) collective-permute-start(bf16[1,4,128,128]{3,2,1,0:T(8,128)(2,1)S(1)} %get-tuple-element.37.rest_0_), channel_id=1, source_target_pairs={{0,1},{1,0},{2,3},{3,2},{4,5},{5,4},{6,7},{7,6},{8,9},{9,8},{10,11... | collective-permute-start | bytes 393224 | tf_op jit(solution)/shard_map/ppermute | solution.py:313
  2.5 2.6 %collective-permute-start = (bf16[1,4,128,128]{3,2,1,0:T(8,128)(2,1)S(1)}, bf16[1,4,128,128]{3,2,1,0:T(8,128)(2,1)S(1)}, u32[]{:S(2)}, u32[]{:S(2)}) collective-permute-start(bf16[1,4,128,128]{3,2,1,0:T(8,128)(2,1)S(1)} %get-tuple-element.37.rest_0_), channel_id=1, source_target_pairs={{0,2},{1,3},{2,0},{3,1},{4,6},{5,7},{6,4},{7,5},{8,10},{9,11},{10,... | collective-permute-start | bytes 393224 | tf_op jit(solution)/shard_map/ppermute | solution.py:313
  5.0 1.3 %collective-permute-start.3 = (bf16[2,4,128,128]{3,2,1,0:T(8,128)(2,1)S(1)}, bf16[2,4,128,128]{3,2,1,0:T(8,128)(2,1)S(1)}, u32[]{:S(2)}, u32[]{:S(2)}) collective-permute-start(bf16[2,4,128,128]{3,2,1,0:T(8,128)(2,1)S(1)} %get-tuple-element.44.rest_0_), channel_id=1, source_target_pairs={{0,2},{1,3},{2,0},{3,1},{4,6},{5,7},{6,4},{7,5},{8,10},{9,11},{10,... | collective-permute-start | bytes 786440 | tf_op jit(solution)/shard_map/ppermute | solution.py:313
  6.3 0.1 pad_add_fusion.ids_ref
  6.4 2.8 %receivers_by_freq.1 = (bf16[128,72,128]{2,1,0:T(8,128)(2,1)S(1)}, f32[4,128]{1,0:T(4,128)S(1)}, f32[2,128]{1,0:T(2,128)S(1)}) custom-call(s32[2]{0:T(128)S(1)} %pad_add_fusion.ids_ref, bf16[64,2,3,24,128]{4,3,2,1,0:T(8,128)(2,1)S(1)} %copy-done.1, s32[4,128]{1,0:T(4,128)S(1)} %bitcast.8), custom_call_target="tpu_custom_call" | custom-call | bytes 12582912 | tf_op jit(solution)/shard_map/receivers_by_freq/pallas_call | solution.py:108
  9.2 0.2 collective-permute-done.rest_2_
  9.4 0.5 %collective-permute-start.2 = (bf16[2,4,128,128]{3,2,1,0:T(8,128)(2,1)S(1)}, bf16[2,4,128,128]{3,2,1,0:T(8,128)(2,1)S(1)}, u32[]{:S(2)}, u32[]{:S(2)}) collective-permute-start(bf16[2,4,128,128]{3,2,1,0:T(8,128)(2,1)S(1)} %get-tuple-element.44.rest_0_), channel_id=1, source_target_pairs={{0,1},{1,0},{2,3},{3,2},{4,5},{5,4},{6,7},{7,6},{8,9},{9,8},{10,11... | collective-permute-start | bytes 786440 | tf_op jit(solution)/shard_map/ppermute | solution.py:313
  9.9 0.8 %collective-permute-done.4.rest_3_ = bf16[1,4,128,128]{3,2,1,0:T(8,128)(2,1)S(1)} collective-permute-done((bf16[1,4,128,128]{3,2,1,0:T(8,128)(2,1)S(1)}, bf16[1,4,128,128]{3,2,1,0:T(8,128)(2,1)S(1)}, u32[]{:S(2)}, u32[]{:S(2)}) %collective-permute-start.4) | collective-permute-done | bytes 131104 | tf_op jit(solution)/shard_map/ppermute | solution.py:313
  10.7 2.1 %cross_spectra.2.cross_ref = f32[4224,128]{1,0:T(8,128)S(1)} custom-call(s32[2]{0:T(128)S(1)} %pad_add_fusion.ids_ref, s32[2]{0:T(128)S(1)} %copy-done.4, s32[8]{0:T(128)S(1)} %copy-done.5, bf16[128,72,128]{2,1,0:T(8,128)(2,1)S(1)} %get-tuple-element.41.recv_ref, f32[4,128]{1,0:T(4,128)S(1)} %get-tuple-element.42.signs_ref, ...), custom_call_target="tpu_custom_call" | custom-call | bytes 10485760 | tf_op jit(solution)/shard_map/cross_spectra/pallas_call | solution.py:186
  12.9 1.1 %lag_transform.4 = (f32[584,128]{1,0:T(8,128)S(1)}, f32[576,128]{1,0:T(8,128)S(1)}) custom-call(f32[4224,128]{1,0:T(8,128)S(1)} %cross_spectra.2.cross_ref, f32[256,128]{1,0:T(8,128)S(1)} %copy-done.2, f32[2,128]{1,0:T(2,128)S(1)} %get-tuple-element.48.scale_ref), custom_call_target="tpu_custom_call" | custom-call | bytes 5242880 | tf_op jit(solution)/shard_map/lag_transform/pallas_call | solution.py:232
  14.0 0.7 %collective-permute-done.3.rest_2_ = bf16[2,4,128,128]{3,2,1,0:T(8,128)(2,1)S(1)} collective-permute-done((bf16[2,4,128,128]{3,2,1,0:T(8,128)(2,1)S(1)}, bf16[2,4,128,128]{3,2,1,0:T(8,128)(2,1)S(1)}, u32[]{:S(2)}, u32[]{:S(2)}) %collective-permute-start.3) | collective-permute-done | bytes 262176 | tf_op jit(solution)/shard_map/ppermute | solution.py:313
  14.8 1.9 %collective-permute-start.11 = (f16[584,128]{1,0:T(8,128)(2,1)S(1)}, f16[584,128]{1,0:T(8,128)(2,1)S(1)}, u32[]{:S(2)}, u32[]{:S(2)}) collective-permute-start(f16[584,128]{1,0:T(8,128)(2,1)S(1)} %convert_element_type.58), channel_id=1, source_target_pairs={{0,4},{4,0},{8,12},{12,8},{16,20},{20,16},{24,28},{28,24},{1,5},{5... | collective-permute-start | bytes 448520 | tf_op jit(solution)/shard_map/ppermute | solution.py:313
  16.6 2.2 %cross_spectra.3.cross_ref = f32[8448,128]{1,0:T(8,128)S(1)} custom-call(s32[2]{0:T(128)S(1)} %pad_add_fusion.ids_ref, s32[2]{0:T(128)S(1)} %copy-done.4, s32[8]{0:T(128)S(1)} %copy-done.5, bf16[128,72,128]{2,1,0:T(8,128)(2,1)S(1)} %get-tuple-element.41.recv_ref, f32[4,128]{1,0:T(4,128)S(1)} %get-tuple-element.42.signs_ref, ...), custom_call_target="tpu_custom_call" | custom-call | bytes 10485760 | tf_op jit(solution)/shard_map/cross_spectra/pallas_call | solution.py:186
  18.8 0.7 %lag_transform.5 = f32[584,128]{1,0:T(8,128)S(1)} custom-call(f32[8448,128]{1,0:T(8,128)S(1)} %cross_spectra.3.cross_ref, f32[256,128]{1,0:T(8,128)S(1)} %copy-done.2, f32[2,128]{1,0:T(2,128)S(1)} %get-tuple-element.48.scale_ref), custom_call_target="tpu_custom_call" | custom-call | bytes 5242880 | tf_op jit(solution)/shard_map/lag_transform/pallas_call | solution.py:232
  19.6 1.5 %collective-permute-start.6 = (f16[584,128]{1,0:T(8,128)(2,1)S(1)}, f16[584,128]{1,0:T(8,128)(2,1)S(1)}, u32[]{:S(2)}, u32[]{:S(2)}) collective-permute-start(f16[584,128]{1,0:T(8,128)(2,1)S(1)} %convert_element_type.48), channel_id=1, source_target_pairs={{0,4},{4,0},{8,12},{12,8},{16,20},{20,16},{24,28},{28,24},{1,5},{5... | collective-permute-start | bytes 448520 | tf_op jit(solution)/shard_map/ppermute | solution.py:313
  21.1 0.7 %lag_transform.7 = f32[584,128]{1,0:T(8,128)S(1)} custom-call(f32[8448,128]{1,0:T(8,128)S(1)} %cross_spectra.3.cross_ref, f32[256,128]{1,0:T(8,128)S(1)} %copy-done.2, f32[2,128]{1,0:T(2,128)S(1)} %get-tuple-element.48.scale_ref), custom_call_target="tpu_custom_call" | custom-call | bytes 5242880 | tf_op jit(solution)/shard_map/lag_transform/pallas_call | solution.py:232
  21.8 0.7 %collective-permute-start.7 = (f16[584,128]{1,0:T(8,128)(2,1)S(1)}, f16[584,128]{1,0:T(8,128)(2,1)S(1)}, u32[]{:S(2)}, u32[]{:S(2)}) collective-permute-start(f16[584,128]{1,0:T(8,128)(2,1)S(1)} %convert_element_type.50), channel_id=1, source_target_pairs={{0,4},{4,0},{8,12},{12,8},{16,20},{20,16},{24,28},{28,24},{1,5},{5... | collective-permute-start | bytes 448520 | tf_op jit(solution)/shard_map/ppermute | solution.py:313
  22.5 0.3 merge.6
  22.8 2.7 %collective-permute-start.12 = (f16[296,128]{1,0:T(8,128)(2,1)S(1)}, f16[296,128]{1,0:T(8,128)(2,1)S(1)}, u32[]{:S(2)}, u32[]{:S(2)}) collective-permute-start(f16[296,128]{1,0:T(8,128)(2,1)S(1)} %convert_element_type.60), channel_id=1, source_target_pairs={{0,16},{4,20},{8,24},{12,28},{16,0},{20,4},{24,8},{28,12},{1,17},{... | collective-permute-start | bytes 227336 | tf_op jit(solution)/shard_map/ppermute | solution.py:313
  25.5 0.8 %lag_transform.6 = (f32[576,128]{1,0:T(8,128)S(1)}, f32[576,128]{1,0:T(8,128)S(1)}) custom-call(f32[8448,128]{1,0:T(8,128)S(1)} %cross_spectra.3.cross_ref, f32[256,128]{1,0:T(8,128)S(1)} %copy-done.2, f32[2,128]{1,0:T(2,128)S(1)} %get-tuple-element.48.scale_ref), custom_call_target="tpu_custom_call" | custom-call | bytes 5242880 | tf_op jit(solution)/shard_map/lag_transform/pallas_call | solution.py:232
  26.3 0.0 collective-permute-done.6
  26.4 0.3 merge.4
  26.8 2.7 %collective-permute-start.10 = (f16[296,128]{1,0:T(8,128)(2,1)S(1)}, f16[296,128]{1,0:T(8,128)(2,1)S(1)}, u32[]{:S(2)}, u32[]{:S(2)}) collective-permute-start(f16[296,128]{1,0:T(8,128)(2,1)S(1)} %convert_element_type.56), channel_id=1, source_target_pairs={{0,16},{4,20},{8,24},{12,28},{16,0},{20,4},{24,8},{28,12},{1,17},{... | collective-permute-start | bytes 227336 | tf_op jit(solution)/shard_map/ppermute | solution.py:313
  29.4 1.3 %collective-permute-start.9 = (f16[296,128]{1,0:T(8,128)(2,1)S(1)}, f16[296,128]{1,0:T(8,128)(2,1)S(1)}, u32[]{:S(2)}, u32[]{:S(2)}) collective-permute-start(f16[296,128]{1,0:T(8,128)(2,1)S(1)} %convert_element_type.54), channel_id=1, source_target_pairs={{0,24},{4,28},{8,16},{12,20},{16,8},{20,12},{24,0},{28,4},{1,25},{... | collective-permute-start | bytes 227336 | tf_op jit(solution)/shard_map/ppermute | solution.py:313
  30.8 0.2 merge.5
  31.1 0.3 collective-permute-start.8
  31.4 0.2 merge.7
  31.6 1.9 %collective-permute-start.13 = (f16[152,128]{1,0:T(8,128)(2,1)S(1)}, f16[152,128]{1,0:T(8,128)(2,1)S(1)}, u32[]{:S(2)}, u32[]{:S(2)}) collective-permute-start(f16[152,128]{1,0:T(8,128)(2,1)S(1)} %convert_element_type.62), channel_id=1, source_target_pairs={{0,8},{4,12},{8,0},{12,4},{16,24},{20,28},{24,16},{28,20},{1,9},{5... | collective-permute-start | bytes 116744 | tf_op jit(solution)/shard_map/ppermute | solution.py:313
  33.5 3.4 %collective-permute-done.13 = f16[152,128]{1,0:T(8,128)(2,1)S(1)} collective-permute-done((f16[152,128]{1,0:T(8,128)(2,1)S(1)}, f16[152,128]{1,0:T(8,128)(2,1)S(1)}, u32[]{:S(2)}, u32[]{:S(2)}) %collective-permute-start.13) | collective-permute-done | bytes 38944 | tf_op jit(solution)/shard_map/ppermute | solution.py:313
  37.0 0.8 %total.1 = f32[432,128]{1,0:T(8,128)} custom-call(f32[288,128]{1,0:T(8,128)S(1)} %get-tuple-element.59.refs_0_, f32[296,128]{1,0:T(8,128)S(1)} %convert_element_type.53.refs_1_, f32[296,128]{1,0:T(8,128)S(1)} %convert_element_type.55.refs_2_, f32[296,128]{1,0:T(8,128)S(1)} %convert_element_type.57.refs_3_, f32[144,128]{1,0:T(8,128)S(1)} %get-tuple-element.67.refs_4_, ...), custom_call_target="tpu_custom_call" | custom-call | tf_op jit(solution)/shard_map/total/pallas_call | solution.py:301
  (38 shorter events, 0.3 us)
Async XLA Ops:
  0.0 1.7 %copy-start = (bf16[64,2,3,24,128]{4,3,2,1,0:T(8,128)(2,1)S(1)}, bf16[64,2,3,24,128]{4,3,2,1,0:T(8,128)(2,1)}, u32[]{:S(2)}) copy-start(bf16[64,2,3,24,128]{4,3,2,1,0:T(8,128)(2,1)} %x_ref.3) | copy-start | bytes 7077892
  1.7 4.7 %copy-start.1 = (bf16[64,2,3,24,128]{4,3,2,1,0:T(8,128)(2,1)S(1)}, bf16[64,2,3,24,128]{4,3,2,1,0:T(8,128)(2,1)}, u32[]{:S(2)}) copy-start(bf16[64,2,3,24,128]{4,3,2,1,0:T(8,128)(2,1)} %x_ref.3) | copy-start | bytes 7077892
  1.7 4.7 %copy-start.3 = (s32[512]{0:T(512)S(1)}, s32[512]{0:T(512)}, u32[]{:S(2)}) copy-start(s32[512]{0:T(512)} %param.7) | copy-start | bytes 6148
  1.7 9.1 %copy-start.4 = (s32[2]{0:T(128)S(1)}, s32[2]{0:T(128)}, u32[]{:S(2)}) copy-start(s32[2]{0:T(128)} %src_block_ref.3) | copy-start | bytes 28
  1.7 9.1 %copy-start.5 = (s32[8]{0:T(128)S(1)}, s32[8]{0:T(128)}, u32[]{:S(2)}) copy-start(s32[8]{0:T(128)} %owner_ref.3) | copy-start | bytes 100
  2.0 3.1 %collective-permute-start.1 = (bf16[1,4,128,128]{3,2,1,0:T(8,128)(2,1)S(1)}, bf16[1,4,128,128]{3,2,1,0:T(8,128)(2,1)S(1)}, u32[]{:S(2)}, u32[]{:S(2)}) collective-permute-start(bf16[1,4,128,128]{3,2,1,0:T(8,128)(2,1)S(1)} %get-tuple-element.37.rest_0_), channel_id=1, source_target_pairs={{0,1},{1,0},{2,3},{3,2},{4,5},{5,4},{6,7},{7,6},{8,9},{9,8},{10,11... | collective-permute-start | bytes 393224 | tf_op jit(solution)/shard_map/ppermute | solution.py:313
  2.5 6.9 %collective-permute-start = (bf16[1,4,128,128]{3,2,1,0:T(8,128)(2,1)S(1)}, bf16[1,4,128,128]{3,2,1,0:T(8,128)(2,1)S(1)}, u32[]{:S(2)}, u32[]{:S(2)}) collective-permute-start(bf16[1,4,128,128]{3,2,1,0:T(8,128)(2,1)S(1)} %get-tuple-element.37.rest_0_), channel_id=1, source_target_pairs={{0,2},{1,3},{2,0},{3,1},{4,6},{5,7},{6,4},{7,5},{8,10},{9,11},{10,... | collective-permute-start | bytes 393224 | tf_op jit(solution)/shard_map/ppermute | solution.py:313
  5.0 9.7 %collective-permute-start.3 = (bf16[2,4,128,128]{3,2,1,0:T(8,128)(2,1)S(1)}, bf16[2,4,128,128]{3,2,1,0:T(8,128)(2,1)S(1)}, u32[]{:S(2)}, u32[]{:S(2)}) collective-permute-start(bf16[2,4,128,128]{3,2,1,0:T(8,128)(2,1)S(1)} %get-tuple-element.44.rest_0_), channel_id=1, source_target_pairs={{0,2},{1,3},{2,0},{3,1},{4,6},{5,7},{6,4},{7,5},{8,10},{9,11},{10,... | collective-permute-start | bytes 786440 | tf_op jit(solution)/shard_map/ppermute | solution.py:313
  9.4 3.5 %copy-start.2 = (f32[256,128]{1,0:T(8,128)S(1)}, f32[256,128]{1,0:T(8,128)}, u32[]{:S(2)}) copy-start(f32[256,128]{1,0:T(8,128)} %constant.11.clone.table_ref) | copy-start | bytes 393220
  9.4 1.3 %collective-permute-start.4 = (bf16[1,4,128,128]{3,2,1,0:T(8,128)(2,1)S(1)}, bf16[1,4,128,128]{3,2,1,0:T(8,128)(2,1)S(1)}, u32[]{:S(2)}, u32[]{:S(2)}) collective-permute-start(bf16[1,4,128,128]{3,2,1,0:T(8,128)(2,1)S(1)} %collective-permute-done.rest_2_), channel_id=1, source_target_pairs={{0,1},{1,0},{2,3},{3,2},{4,5},{5,4},{6,7},{7,6},{8,9},{9,8},{10,11... | collective-permute-start | bytes 393224 | tf_op jit(solution)/shard_map/ppermute | solution.py:313
  9.4 7.2 %collective-permute-start.2 = (bf16[2,4,128,128]{3,2,1,0:T(8,128)(2,1)S(1)}, bf16[2,4,128,128]{3,2,1,0:T(8,128)(2,1)S(1)}, u32[]{:S(2)}, u32[]{:S(2)}) collective-permute-start(bf16[2,4,128,128]{3,2,1,0:T(8,128)(2,1)S(1)} %get-tuple-element.44.rest_0_), channel_id=1, source_target_pairs={{0,1},{1,0},{2,3},{3,2},{4,5},{5,4},{6,7},{7,6},{8,9},{9,8},{10,11... | collective-permute-start | bytes 786440 | tf_op jit(solution)/shard_map/ppermute | solution.py:313
  14.7 1.9 %collective-permute-start.5 = (bf16[2,4,128,128]{3,2,1,0:T(8,128)(2,1)S(1)}, bf16[2,4,128,128]{3,2,1,0:T(8,128)(2,1)S(1)}, u32[]{:S(2)}, u32[]{:S(2)}) collective-permute-start(bf16[2,4,128,128]{3,2,1,0:T(8,128)(2,1)S(1)} %collective-permute-done.3.rest_2_), channel_id=1, source_target_pairs={{0,1},{1,0},{2,3},{3,2},{4,5},{5,4},{6,7},{7,6},{8,9},{9,8},{10,11... | collective-permute-start | bytes 786440 | tf_op jit(solution)/shard_map/ppermute | solution.py:313
  14.8 7.7 %collective-permute-start.11 = (f16[584,128]{1,0:T(8,128)(2,1)S(1)}, f16[584,128]{1,0:T(8,128)(2,1)S(1)}, u32[]{:S(2)}, u32[]{:S(2)}) collective-permute-start(f16[584,128]{1,0:T(8,128)(2,1)S(1)} %convert_element_type.58), channel_id=1, source_target_pairs={{0,4},{4,0},{8,12},{12,8},{16,20},{20,16},{24,28},{28,24},{1,5},{5... | collective-permute-start | bytes 448520 | tf_op jit(solution)/shard_map/ppermute | solution.py:313
  19.6 6.8 %collective-permute-start.6 = (f16[584,128]{1,0:T(8,128)(2,1)S(1)}, f16[584,128]{1,0:T(8,128)(2,1)S(1)}, u32[]{:S(2)}, u32[]{:S(2)}) collective-permute-start(f16[584,128]{1,0:T(8,128)(2,1)S(1)} %convert_element_type.48), channel_id=1, source_target_pairs={{0,4},{4,0},{8,12},{12,8},{16,20},{20,16},{24,28},{28,24},{1,5},{5... | collective-permute-start | bytes 448520 | tf_op jit(solution)/shard_map/ppermute | solution.py:313
  21.8 9.0 %collective-permute-start.7 = (f16[584,128]{1,0:T(8,128)(2,1)S(1)}, f16[584,128]{1,0:T(8,128)(2,1)S(1)}, u32[]{:S(2)}, u32[]{:S(2)}) collective-permute-start(f16[584,128]{1,0:T(8,128)(2,1)S(1)} %convert_element_type.50), channel_id=1, source_target_pairs={{0,4},{4,0},{8,12},{12,8},{16,20},{20,16},{24,28},{28,24},{1,5},{5... | collective-permute-start | bytes 448520 | tf_op jit(solution)/shard_map/ppermute | solution.py:313
  22.8 8.5 %collective-permute-start.12 = (f16[296,128]{1,0:T(8,128)(2,1)S(1)}, f16[296,128]{1,0:T(8,128)(2,1)S(1)}, u32[]{:S(2)}, u32[]{:S(2)}) collective-permute-start(f16[296,128]{1,0:T(8,128)(2,1)S(1)} %convert_element_type.60), channel_id=1, source_target_pairs={{0,16},{4,20},{8,24},{12,28},{16,0},{20,4},{24,8},{28,12},{1,17},{... | collective-permute-start | bytes 227336 | tf_op jit(solution)/shard_map/ppermute | solution.py:313
  26.8 10.1 %collective-permute-start.10 = (f16[296,128]{1,0:T(8,128)(2,1)S(1)}, f16[296,128]{1,0:T(8,128)(2,1)S(1)}, u32[]{:S(2)}, u32[]{:S(2)}) collective-permute-start(f16[296,128]{1,0:T(8,128)(2,1)S(1)} %convert_element_type.56), channel_id=1, source_target_pairs={{0,16},{4,20},{8,24},{12,28},{16,0},{20,4},{24,8},{28,12},{1,17},{... | collective-permute-start | bytes 227336 | tf_op jit(solution)/shard_map/ppermute | solution.py:313
  29.4 7.5 %collective-permute-start.9 = (f16[296,128]{1,0:T(8,128)(2,1)S(1)}, f16[296,128]{1,0:T(8,128)(2,1)S(1)}, u32[]{:S(2)}, u32[]{:S(2)}) collective-permute-start(f16[296,128]{1,0:T(8,128)(2,1)S(1)} %convert_element_type.54), channel_id=1, source_target_pairs={{0,24},{4,28},{8,16},{12,20},{16,8},{20,12},{24,0},{28,4},{1,25},{... | collective-permute-start | bytes 227336 | tf_op jit(solution)/shard_map/ppermute | solution.py:313
  31.1 5.9 %collective-permute-start.8 = (f16[296,128]{1,0:T(8,128)(2,1)S(1)}, f16[296,128]{1,0:T(8,128)(2,1)S(1)}, u32[]{:S(2)}, u32[]{:S(2)}) collective-permute-start(f16[296,128]{1,0:T(8,128)(2,1)S(1)} %convert_element_type.52), channel_id=1, source_target_pairs={{0,8},{4,12},{8,0},{12,4},{16,24},{20,28},{24,16},{28,20},{1,9},{5... | collective-permute-start | bytes 227336 | tf_op jit(solution)/shard_map/ppermute | solution.py:313
  31.6 5.3 %collective-permute-start.13 = (f16[152,128]{1,0:T(8,128)(2,1)S(1)}, f16[152,128]{1,0:T(8,128)(2,1)S(1)}, u32[]{:S(2)}, u32[]{:S(2)}) collective-permute-start(f16[152,128]{1,0:T(8,128)(2,1)S(1)} %convert_element_type.62), channel_id=1, source_target_pairs={{0,8},{4,12},{8,0},{12,4},{16,24},{20,28},{24,16},{28,20},{1,9},{5... | collective-permute-start | bytes 116744 | tf_op jit(solution)/shard_map/ppermute | solution.py:313

commit v6 on v5

--- a/solution.py
+++ b/solution.py
@@ -357,17 +357,17 @@
         (away_far,) = lags([(True, [(1 ^ z, rest) for z in far])])
         away_far, cross = lax.optimization_barrier((away_far, cross))
         arrived_far = send(away_far, 1)
-        (away_near,) = lags([(True, [(1 ^ z, rest) for z in near])], cross=cross)
-        arrived_near = send(away_near, 1)
+        (away_near,) = lags([(True, [(2, rest), (3, rest)])], cross=cross)
+        arrived_near = send(away_near, 2)
         kept, away = merge([(4, kept, arrived)], [(False, [(0, 0), (0, 1)]), (True, [(0, 3), (0, 2)])])
         arrived = send(away, 4)
-        kept_near, kept_far = lags([(False, [(z, rest) for z in of]) for of in (near, far)], cross=cross)
+        kept_near, kept_far = lags([(False, [(z, rest) for z in of]) for of in ((0, 1), far)], cross=cross)
         by_6, by_4 = merge([(2, kept_far, arrived_far)], [(True, [(0, 0)]), (True, [(0, 1)])])
         kept_near, by_6, by_4 = lax.optimization_barrier((kept_near, by_6, by_4))
         by_6 = send(by_6, 6)
         by_4 = send(by_4, 4)
-        own_rest, by_2 = merge([(2, kept_near, arrived_near)], [(False, [(0, 0)]), (True, [(0, 1)])])
-        by_2 = send(by_2, 2)
+        own_rest, by_1 = merge([(2, kept_near, arrived_near)], [(False, [(0, 0)]), (True, [(0, 1)])])
+        by_1 = send(by_1, 1)
         own_ahead, ahead_by_2 = merge([(2, kept, arrived)], [(False, [(0, 0)]), (True, [(0, 1)])])
         ahead_by_2 = send(ahead_by_2, 2)
         size, ahead_size = own_rest.shape[0], own_ahead.shape[0]
@@ -375,7 +375,7 @@
             (rest, [(0, 0, None), (1, 0, size), (2, 0, size), (3, 0, size)]),
             (ahead, [(4, 0, None), (5, 0, ahead_size)]),
         ]
-        result = total(stations, terms, [own_rest, by_2, by_6, by_4, own_ahead, ahead_by_2])
+        result = total(stations, terms, [own_rest, by_1, by_6, by_4, own_ahead, ahead_by_2])
         result = result.reshape(block_rows, COMPS * COMPS, G, LAG).transpose(0, 2, 1, 3)
         return result[None]
 

time: 37.9 us -> 37.6 us (level)
  starting transfers between devices: 17.7 us -> 16.9 us
  waiting for transfers between devices: 5.23 us -> 5.63 us
    ppermute x14, starting transfers between devices: 17.7 us -> 16.9 us  [swap(): return lax.ppermute(value, axis, [(i, i ^ mask) for i in range(size)])]
    ppermute x14, waiting for transfers between devices: 5.23 us -> 5.63 us  [swap(): return lax.ppermute(value, axis, [(i, i ^ mask) for i in range(size)])]
where the time goes in v6:
time: 37.6 us; the launch traced here: 37.4 us
  starting transfers between devices  16.9 us (45%)
  Pallas kernels  12.6 us (34%)
  waiting for transfers between devices  5.63 us (15%)
  local copies, waits for them, and re-layouts  1.69 us (4%)
    ppermute x14, starting transfers between devices, swap(): return lax.ppermute(value, axis, [(i, i ^ mask) for i in range(size)])  16.9 us
    ppermute x14, waiting for transfers between devices, swap(): return lax.ppermute(value, axis, [(i, i ^ mask) for i in range(size)])  5.63 us
    pallas_call x2, Pallas kernels, cross_spectra(): pl.pallas_call(functools.partial(cross_kernel, comps), in_specs=[SMEM] *...  4.34 us
    pallas_call x4, Pallas kernels, lag_transform(): pl.pallas_call(functools.partial(lag_kernel, outputs, held, columns), in_...  3.31 us
    pallas_call x1, Pallas kernels, receivers_by_freq(): pl.pallas_call(receivers_kernel, grid=(COMPS,), in_specs=[SMEM, pl.BlockS...  2.78 us
    unnamed x12, local copies, waits for them, and re-layouts  1.69 us
    pallas_call x4, Pallas kernels, merge(): pl.pallas_call(functools.partial(merge_kernel, [count for count, _, _ in...  1.12 us
    pallas_call x1, Pallas kernels, total(): pl.pallas_call(functools.partial(total_kernel, stations, terms), in_specs...  0.78 us
  transfers between devices with their start and end apart: 14, of which 4 were waited for; matrix products, arithmetic and copies ran while one was open for 1% of the time, Pallas kernels for 31%

profile of v6, /device:TPU:0, one launch (start us, length us, event | category | flops | bytes accessed | tf_op | source)
XLA Modules:
  0.0 37.4 jit_solution(9250129211250982465)
XLA Ops:
  0.0 1.7 %copy-done = bf16[64,2,3,24,128]{4,3,2,1,0:T(8,128)(2,1)S(1)} copy-done((bf16[64,2,3,24,128]{4,3,2,1,0:T(8,128)(2,1)S(1)}, bf16[64,2,3,24,128]{4,3,2,1,0:T(8,128)(2,1)}, u32[]{:S(2)}) %copy-start) | copy-done | bytes 2359320
  1.7 0.3 first_block.1
  2.0 0.5 %collective-permute-start.1 = (bf16[1,4,128,128]{3,2,1,0:T(8,128)(2,1)S(1)}, bf16[1,4,128,128]{3,2,1,0:T(8,128)(2,1)S(1)}, u32[]{:S(2)}, u32[]{:S(2)}) collective-permute-start(bf16[1,4,128,128]{3,2,1,0:T(8,128)(2,1)S(1)} %get-tuple-element.37.rest_0_), channel_id=1, source_target_pairs={{0,1},{1,0},{2,3},{3,2},{4,5},{5,4},{6,7},{7,6},{8,9},{9,8},{10,11... | collective-permute-start | bytes 393224 | tf_op jit(solution)/shard_map/ppermute | solution.py:313
  2.5 2.6 %collective-permute-start = (bf16[1,4,128,128]{3,2,1,0:T(8,128)(2,1)S(1)}, bf16[1,4,128,128]{3,2,1,0:T(8,128)(2,1)S(1)}, u32[]{:S(2)}, u32[]{:S(2)}) collective-permute-start(bf16[1,4,128,128]{3,2,1,0:T(8,128)(2,1)S(1)} %get-tuple-element.37.rest_0_), channel_id=1, source_target_pairs={{0,2},{1,3},{2,0},{3,1},{4,6},{5,7},{6,4},{7,5},{8,10},{9,11},{10,... | collective-permute-start | bytes 393224 | tf_op jit(solution)/shard_map/ppermute | solution.py:313
  5.0 1.3 %collective-permute-start.3 = (bf16[2,4,128,128]{3,2,1,0:T(8,128)(2,1)S(1)}, bf16[2,4,128,128]{3,2,1,0:T(8,128)(2,1)S(1)}, u32[]{:S(2)}, u32[]{:S(2)}) collective-permute-start(bf16[2,4,128,128]{3,2,1,0:T(8,128)(2,1)S(1)} %get-tuple-element.44.rest_0_), channel_id=1, source_target_pairs={{0,2},{1,3},{2,0},{3,1},{4,6},{5,7},{6,4},{7,5},{8,10},{9,11},{10,... | collective-permute-start | bytes 786440 | tf_op jit(solution)/shard_map/ppermute | solution.py:313
  6.3 0.1 pad_add_fusion.ids_ref
  6.4 2.8 %receivers_by_freq.1 = (bf16[128,72,128]{2,1,0:T(8,128)(2,1)S(1)}, f32[4,128]{1,0:T(4,128)S(1)}, f32[2,128]{1,0:T(2,128)S(1)}) custom-call(s32[2]{0:T(128)S(1)} %pad_add_fusion.ids_ref, bf16[64,2,3,24,128]{4,3,2,1,0:T(8,128)(2,1)S(1)} %copy-done.1, s32[4,128]{1,0:T(4,128)S(1)} %bitcast.8), custom_call_target="tpu_custom_call" | custom-call | bytes 12582912 | tf_op jit(solution)/shard_map/receivers_by_freq/pallas_call | solution.py:108
  9.2 0.2 collective-permute-done.rest_2_
  9.4 0.5 %collective-permute-start.2 = (bf16[2,4,128,128]{3,2,1,0:T(8,128)(2,1)S(1)}, bf16[2,4,128,128]{3,2,1,0:T(8,128)(2,1)S(1)}, u32[]{:S(2)}, u32[]{:S(2)}) collective-permute-start(bf16[2,4,128,128]{3,2,1,0:T(8,128)(2,1)S(1)} %get-tuple-element.44.rest_0_), channel_id=1, source_target_pairs={{0,1},{1,0},{2,3},{3,2},{4,5},{5,4},{6,7},{7,6},{8,9},{9,8},{10,11... | collective-permute-start | bytes 786440 | tf_op jit(solution)/shard_map/ppermute | solution.py:313
  9.9 0.8 %collective-permute-done.4.rest_3_ = bf16[1,4,128,128]{3,2,1,0:T(8,128)(2,1)S(1)} collective-permute-done((bf16[1,4,128,128]{3,2,1,0:T(8,128)(2,1)S(1)}, bf16[1,4,128,128]{3,2,1,0:T(8,128)(2,1)S(1)}, u32[]{:S(2)}, u32[]{:S(2)}) %collective-permute-start.4) | collective-permute-done | bytes 131104 | tf_op jit(solution)/shard_map/ppermute | solution.py:313
  10.7 2.1 %cross_spectra.2.cross_ref = f32[4224,128]{1,0:T(8,128)S(1)} custom-call(s32[2]{0:T(128)S(1)} %pad_add_fusion.ids_ref, s32[2]{0:T(128)S(1)} %copy-done.4, s32[8]{0:T(128)S(1)} %copy-done.5, bf16[128,72,128]{2,1,0:T(8,128)(2,1)S(1)} %get-tuple-element.41.recv_ref, f32[4,128]{1,0:T(4,128)S(1)} %get-tuple-element.42.signs_ref, ...), custom_call_target="tpu_custom_call" | custom-call | bytes 10485760 | tf_op jit(solution)/shard_map/cross_spectra/pallas_call | solution.py:186
  12.9 0.0 copy-done.2
  12.9 1.1 %lag_transform.4 = (f32[584,128]{1,0:T(8,128)S(1)}, f32[576,128]{1,0:T(8,128)S(1)}) custom-call(f32[4224,128]{1,0:T(8,128)S(1)} %cross_spectra.2.cross_ref, f32[256,128]{1,0:T(8,128)S(1)} %copy-done.2, f32[2,128]{1,0:T(2,128)S(1)} %get-tuple-element.48.scale_ref), custom_call_target="tpu_custom_call" | custom-call | bytes 5242880 | tf_op jit(solution)/shard_map/lag_transform/pallas_call | solution.py:232
  14.0 0.7 %collective-permute-done.3.rest_2_ = bf16[2,4,128,128]{3,2,1,0:T(8,128)(2,1)S(1)} collective-permute-done((bf16[2,4,128,128]{3,2,1,0:T(8,128)(2,1)S(1)}, bf16[2,4,128,128]{3,2,1,0:T(8,128)(2,1)S(1)}, u32[]{:S(2)}, u32[]{:S(2)}) %collective-permute-start.3) | collective-permute-done | bytes 262176 | tf_op jit(solution)/shard_map/ppermute | solution.py:313
  14.8 1.9 %collective-permute-start.11 = (f16[584,128]{1,0:T(8,128)(2,1)S(1)}, f16[584,128]{1,0:T(8,128)(2,1)S(1)}, u32[]{:S(2)}, u32[]{:S(2)}) collective-permute-start(f16[584,128]{1,0:T(8,128)(2,1)S(1)} %convert_element_type.58), channel_id=1, source_target_pairs={{0,4},{4,0},{8,12},{12,8},{16,20},{20,16},{24,28},{28,24},{1,5},{5... | collective-permute-start | bytes 448520 | tf_op jit(solution)/shard_map/ppermute | solution.py:313
  16.6 2.2 %cross_spectra.3.cross_ref = f32[8448,128]{1,0:T(8,128)S(1)} custom-call(s32[2]{0:T(128)S(1)} %pad_add_fusion.ids_ref, s32[2]{0:T(128)S(1)} %copy-done.4, s32[8]{0:T(128)S(1)} %copy-done.5, bf16[128,72,128]{2,1,0:T(8,128)(2,1)S(1)} %get-tuple-element.41.recv_ref, f32[4,128]{1,0:T(4,128)S(1)} %get-tuple-element.42.signs_ref, ...), custom_call_target="tpu_custom_call" | custom-call | bytes 10485760 | tf_op jit(solution)/shard_map/cross_spectra/pallas_call | solution.py:186
  18.8 0.7 %lag_transform.5 = f32[584,128]{1,0:T(8,128)S(1)} custom-call(f32[8448,128]{1,0:T(8,128)S(1)} %cross_spectra.3.cross_ref, f32[256,128]{1,0:T(8,128)S(1)} %copy-done.2, f32[2,128]{1,0:T(2,128)S(1)} %get-tuple-element.48.scale_ref), custom_call_target="tpu_custom_call" | custom-call | bytes 5242880 | tf_op jit(solution)/shard_map/lag_transform/pallas_call | solution.py:232
  19.6 1.5 %collective-permute-start.6 = (f16[584,128]{1,0:T(8,128)(2,1)S(1)}, f16[584,128]{1,0:T(8,128)(2,1)S(1)}, u32[]{:S(2)}, u32[]{:S(2)}) collective-permute-start(f16[584,128]{1,0:T(8,128)(2,1)S(1)} %convert_element_type.48), channel_id=1, source_target_pairs={{0,4},{4,0},{8,12},{12,8},{16,20},{20,16},{24,28},{28,24},{1,5},{5... | collective-permute-start | bytes 448520 | tf_op jit(solution)/shard_map/ppermute | solution.py:313
  21.1 0.7 %lag_transform.7 = f32[584,128]{1,0:T(8,128)S(1)} custom-call(f32[8448,128]{1,0:T(8,128)S(1)} %cross_spectra.3.cross_ref, f32[256,128]{1,0:T(8,128)S(1)} %copy-done.2, f32[2,128]{1,0:T(2,128)S(1)} %get-tuple-element.48.scale_ref), custom_call_target="tpu_custom_call" | custom-call | bytes 5242880 | tf_op jit(solution)/shard_map/lag_transform/pallas_call | solution.py:232
  21.8 1.7 %collective-permute-start.7 = (f16[584,128]{1,0:T(8,128)(2,1)S(1)}, f16[584,128]{1,0:T(8,128)(2,1)S(1)}, u32[]{:S(2)}, u32[]{:S(2)}) collective-permute-start(f16[584,128]{1,0:T(8,128)(2,1)S(1)} %convert_element_type.50), channel_id=1, source_target_pairs={{0,8},{4,12},{8,0},{12,4},{16,24},{20,28},{24,16},{28,20},{1,9},{5... | collective-permute-start | bytes 448520 | tf_op jit(solution)/shard_map/ppermute | solution.py:313
  23.4 0.3 merge.6
  23.8 2.6 %collective-permute-start.12 = (f16[296,128]{1,0:T(8,128)(2,1)S(1)}, f16[296,128]{1,0:T(8,128)(2,1)S(1)}, u32[]{:S(2)}, u32[]{:S(2)}) collective-permute-start(f16[296,128]{1,0:T(8,128)(2,1)S(1)} %convert_element_type.60), channel_id=1, source_target_pairs={{0,16},{4,20},{8,24},{12,28},{16,0},{20,4},{24,8},{28,12},{1,17},{... | collective-permute-start | bytes 227336 | tf_op jit(solution)/shard_map/ppermute | solution.py:313
  26.5 0.8 %lag_transform.6 = (f32[576,128]{1,0:T(8,128)S(1)}, f32[576,128]{1,0:T(8,128)S(1)}) custom-call(f32[8448,128]{1,0:T(8,128)S(1)} %cross_spectra.3.cross_ref, f32[256,128]{1,0:T(8,128)S(1)} %copy-done.2, f32[2,128]{1,0:T(2,128)S(1)} %get-tuple-element.48.scale_ref), custom_call_target="tpu_custom_call" | custom-call | bytes 5242880 | tf_op jit(solution)/shard_map/lag_transform/pallas_call | solution.py:232
  27.3 0.3 merge.4
  27.7 1.0 %collective-permute-start.10 = (f16[296,128]{1,0:T(8,128)(2,1)S(1)}, f16[296,128]{1,0:T(8,128)(2,1)S(1)}, u32[]{:S(2)}, u32[]{:S(2)}) collective-permute-start(f16[296,128]{1,0:T(8,128)(2,1)S(1)} %convert_element_type.56), channel_id=1, source_target_pairs={{0,16},{4,20},{8,24},{12,28},{16,0},{20,4},{24,8},{28,12},{1,17},{... | collective-permute-start | bytes 227336 | tf_op jit(solution)/shard_map/ppermute | solution.py:313
  28.7 1.9 %collective-permute-start.9 = (f16[296,128]{1,0:T(8,128)(2,1)S(1)}, f16[296,128]{1,0:T(8,128)(2,1)S(1)}, u32[]{:S(2)}, u32[]{:S(2)}) collective-permute-start(f16[296,128]{1,0:T(8,128)(2,1)S(1)} %convert_element_type.54), channel_id=1, source_target_pairs={{0,24},{4,28},{8,16},{12,20},{16,8},{20,12},{24,0},{28,4},{1,25},{... | collective-permute-start | bytes 227336 | tf_op jit(solution)/shard_map/ppermute | solution.py:313
  30.7 0.2 merge.5
  30.9 0.8 %collective-permute-start.8 = (f16[296,128]{1,0:T(8,128)(2,1)S(1)}, f16[296,128]{1,0:T(8,128)(2,1)S(1)}, u32[]{:S(2)}, u32[]{:S(2)}) collective-permute-start(f16[296,128]{1,0:T(8,128)(2,1)S(1)} %convert_element_type.52), channel_id=1, source_target_pairs={{0,4},{4,0},{8,12},{12,8},{16,20},{20,16},{24,28},{28,24},{1,5},{5... | collective-permute-start | bytes 227336 | tf_op jit(solution)/shard_map/ppermute | solution.py:313
  31.8 0.2 merge.7
  32.0 0.7 %collective-permute-start.13 = (f16[152,128]{1,0:T(8,128)(2,1)S(1)}, f16[152,128]{1,0:T(8,128)(2,1)S(1)}, u32[]{:S(2)}, u32[]{:S(2)}) collective-permute-start(f16[152,128]{1,0:T(8,128)(2,1)S(1)} %convert_element_type.62), channel_id=1, source_target_pairs={{0,8},{4,12},{8,0},{12,4},{16,24},{20,28},{24,16},{28,20},{1,9},{5... | collective-permute-start | bytes 116744 | tf_op jit(solution)/shard_map/ppermute | solution.py:313
  32.7 3.8 %collective-permute-done.13 = f16[152,128]{1,0:T(8,128)(2,1)S(1)} collective-permute-done((f16[152,128]{1,0:T(8,128)(2,1)S(1)}, f16[152,128]{1,0:T(8,128)(2,1)S(1)}, u32[]{:S(2)}, u32[]{:S(2)}) %collective-permute-start.13) | collective-permute-done | bytes 38944 | tf_op jit(solution)/shard_map/ppermute | solution.py:313
  36.6 0.8 %total.1 = f32[432,128]{1,0:T(8,128)} custom-call(f32[288,128]{1,0:T(8,128)S(1)} %get-tuple-element.59.refs_0_, f32[296,128]{1,0:T(8,128)S(1)} %convert_element_type.53.refs_1_, f32[296,128]{1,0:T(8,128)S(1)} %convert_element_type.55.refs_2_, f32[296,128]{1,0:T(8,128)S(1)} %convert_element_type.57.refs_3_, f32[144,128]{1,0:T(8,128)S(1)} %get-tuple-element.67.refs_4_, ...), custom_call_target="tpu_custom_call" | custom-call | tf_op jit(solution)/shard_map/total/pallas_call | solution.py:301
  (38 shorter events, 0.3 us)
Async XLA Ops:
  0.0 1.7 %copy-start = (bf16[64,2,3,24,128]{4,3,2,1,0:T(8,128)(2,1)S(1)}, bf16[64,2,3,24,128]{4,3,2,1,0:T(8,128)(2,1)}, u32[]{:S(2)}) copy-start(bf16[64,2,3,24,128]{4,3,2,1,0:T(8,128)(2,1)} %x_ref.3) | copy-start | bytes 7077892
  1.7 4.7 %copy-start.1 = (bf16[64,2,3,24,128]{4,3,2,1,0:T(8,128)(2,1)S(1)}, bf16[64,2,3,24,128]{4,3,2,1,0:T(8,128)(2,1)}, u32[]{:S(2)}) copy-start(bf16[64,2,3,24,128]{4,3,2,1,0:T(8,128)(2,1)} %x_ref.3) | copy-start | bytes 7077892
  1.7 4.7 %copy-start.3 = (s32[512]{0:T(512)S(1)}, s32[512]{0:T(512)}, u32[]{:S(2)}) copy-start(s32[512]{0:T(512)} %param.7) | copy-start | bytes 6148
  1.7 9.1 %copy-start.4 = (s32[2]{0:T(128)S(1)}, s32[2]{0:T(128)}, u32[]{:S(2)}) copy-start(s32[2]{0:T(128)} %src_block_ref.3) | copy-start | bytes 28
  1.7 9.1 %copy-start.5 = (s32[8]{0:T(128)S(1)}, s32[8]{0:T(128)}, u32[]{:S(2)}) copy-start(s32[8]{0:T(128)} %owner_ref.3) | copy-start | bytes 100
  2.0 3.1 %collective-permute-start.1 = (bf16[1,4,128,128]{3,2,1,0:T(8,128)(2,1)S(1)}, bf16[1,4,128,128]{3,2,1,0:T(8,128)(2,1)S(1)}, u32[]{:S(2)}, u32[]{:S(2)}) collective-permute-start(bf16[1,4,128,128]{3,2,1,0:T(8,128)(2,1)S(1)} %get-tuple-element.37.rest_0_), channel_id=1, source_target_pairs={{0,1},{1,0},{2,3},{3,2},{4,5},{5,4},{6,7},{7,6},{8,9},{9,8},{10,11... | collective-permute-start | bytes 393224 | tf_op jit(solution)/shard_map/ppermute | solution.py:313
  2.5 6.9 %collective-permute-start = (bf16[1,4,128,128]{3,2,1,0:T(8,128)(2,1)S(1)}, bf16[1,4,128,128]{3,2,1,0:T(8,128)(2,1)S(1)}, u32[]{:S(2)}, u32[]{:S(2)}) collective-permute-start(bf16[1,4,128,128]{3,2,1,0:T(8,128)(2,1)S(1)} %get-tuple-element.37.rest_0_), channel_id=1, source_target_pairs={{0,2},{1,3},{2,0},{3,1},{4,6},{5,7},{6,4},{7,5},{8,10},{9,11},{10,... | collective-permute-start | bytes 393224 | tf_op jit(solution)/shard_map/ppermute | solution.py:313
  5.0 9.7 %collective-permute-start.3 = (bf16[2,4,128,128]{3,2,1,0:T(8,128)(2,1)S(1)}, bf16[2,4,128,128]{3,2,1,0:T(8,128)(2,1)S(1)}, u32[]{:S(2)}, u32[]{:S(2)}) collective-permute-start(bf16[2,4,128,128]{3,2,1,0:T(8,128)(2,1)S(1)} %get-tuple-element.44.rest_0_), channel_id=1, source_target_pairs={{0,2},{1,3},{2,0},{3,1},{4,6},{5,7},{6,4},{7,5},{8,10},{9,11},{10,... | collective-permute-start | bytes 786440 | tf_op jit(solution)/shard_map/ppermute | solution.py:313
  9.4 3.5 %copy-start.2 = (f32[256,128]{1,0:T(8,128)S(1)}, f32[256,128]{1,0:T(8,128)}, u32[]{:S(2)}) copy-start(f32[256,128]{1,0:T(8,128)} %constant.11.clone.table_ref) | copy-start | bytes 393220
  9.4 1.3 %collective-permute-start.4 = (bf16[1,4,128,128]{3,2,1,0:T(8,128)(2,1)S(1)}, bf16[1,4,128,128]{3,2,1,0:T(8,128)(2,1)S(1)}, u32[]{:S(2)}, u32[]{:S(2)}) collective-permute-start(bf16[1,4,128,128]{3,2,1,0:T(8,128)(2,1)S(1)} %collective-permute-done.rest_2_), channel_id=1, source_target_pairs={{0,1},{1,0},{2,3},{3,2},{4,5},{5,4},{6,7},{7,6},{8,9},{9,8},{10,11... | collective-permute-start | bytes 393224 | tf_op jit(solution)/shard_map/ppermute | solution.py:313
  9.4 7.2 %collective-permute-start.2 = (bf16[2,4,128,128]{3,2,1,0:T(8,128)(2,1)S(1)}, bf16[2,4,128,128]{3,2,1,0:T(8,128)(2,1)S(1)}, u32[]{:S(2)}, u32[]{:S(2)}) collective-permute-start(bf16[2,4,128,128]{3,2,1,0:T(8,128)(2,1)S(1)} %get-tuple-element.44.rest_0_), channel_id=1, source_target_pairs={{0,1},{1,0},{2,3},{3,2},{4,5},{5,4},{6,7},{7,6},{8,9},{9,8},{10,11... | collective-permute-start | bytes 786440 | tf_op jit(solution)/shard_map/ppermute | solution.py:313
  14.7 1.9 %collective-permute-start.5 = (bf16[2,4,128,128]{3,2,1,0:T(8,128)(2,1)S(1)}, bf16[2,4,128,128]{3,2,1,0:T(8,128)(2,1)S(1)}, u32[]{:S(2)}, u32[]{:S(2)}) collective-permute-start(bf16[2,4,128,128]{3,2,1,0:T(8,128)(2,1)S(1)} %collective-permute-done.3.rest_2_), channel_id=1, source_target_pairs={{0,1},{1,0},{2,3},{3,2},{4,5},{5,4},{6,7},{7,6},{8,9},{9,8},{10,11... | collective-permute-start | bytes 786440 | tf_op jit(solution)/shard_map/ppermute | solution.py:313
  14.8 8.6 %collective-permute-start.11 = (f16[584,128]{1,0:T(8,128)(2,1)S(1)}, f16[584,128]{1,0:T(8,128)(2,1)S(1)}, u32[]{:S(2)}, u32[]{:S(2)}) collective-permute-start(f16[584,128]{1,0:T(8,128)(2,1)S(1)} %convert_element_type.58), channel_id=1, source_target_pairs={{0,4},{4,0},{8,12},{12,8},{16,20},{20,16},{24,28},{28,24},{1,5},{5... | collective-permute-start | bytes 448520 | tf_op jit(solution)/shard_map/ppermute | solution.py:313
  19.6 7.8 %collective-permute-start.6 = (f16[584,128]{1,0:T(8,128)(2,1)S(1)}, f16[584,128]{1,0:T(8,128)(2,1)S(1)}, u32[]{:S(2)}, u32[]{:S(2)}) collective-permute-start(f16[584,128]{1,0:T(8,128)(2,1)S(1)} %convert_element_type.48), channel_id=1, source_target_pairs={{0,4},{4,0},{8,12},{12,8},{16,20},{20,16},{24,28},{28,24},{1,5},{5... | collective-permute-start | bytes 448520 | tf_op jit(solution)/shard_map/ppermute | solution.py:313
  21.8 8.9 %collective-permute-start.7 = (f16[584,128]{1,0:T(8,128)(2,1)S(1)}, f16[584,128]{1,0:T(8,128)(2,1)S(1)}, u32[]{:S(2)}, u32[]{:S(2)}) collective-permute-start(f16[584,128]{1,0:T(8,128)(2,1)S(1)} %convert_element_type.50), channel_id=1, source_target_pairs={{0,8},{4,12},{8,0},{12,4},{16,24},{20,28},{24,16},{28,20},{1,9},{5... | collective-permute-start | bytes 448520 | tf_op jit(solution)/shard_map/ppermute | solution.py:313
  23.8 7.9 %collective-permute-start.12 = (f16[296,128]{1,0:T(8,128)(2,1)S(1)}, f16[296,128]{1,0:T(8,128)(2,1)S(1)}, u32[]{:S(2)}, u32[]{:S(2)}) collective-permute-start(f16[296,128]{1,0:T(8,128)(2,1)S(1)} %convert_element_type.60), channel_id=1, source_target_pairs={{0,16},{4,20},{8,24},{12,28},{16,0},{20,4},{24,8},{28,12},{1,17},{... | collective-permute-start | bytes 227336 | tf_op jit(solution)/shard_map/ppermute | solution.py:313
  27.7 8.8 %collective-permute-start.10 = (f16[296,128]{1,0:T(8,128)(2,1)S(1)}, f16[296,128]{1,0:T(8,128)(2,1)S(1)}, u32[]{:S(2)}, u32[]{:S(2)}) collective-permute-start(f16[296,128]{1,0:T(8,128)(2,1)S(1)} %convert_element_type.56), channel_id=1, source_target_pairs={{0,16},{4,20},{8,24},{12,28},{16,0},{20,4},{24,8},{28,12},{1,17},{... | collective-permute-start | bytes 227336 | tf_op jit(solution)/shard_map/ppermute | solution.py:313
  28.7 7.9 %collective-permute-start.9 = (f16[296,128]{1,0:T(8,128)(2,1)S(1)}, f16[296,128]{1,0:T(8,128)(2,1)S(1)}, u32[]{:S(2)}, u32[]{:S(2)}) collective-permute-start(f16[296,128]{1,0:T(8,128)(2,1)S(1)} %convert_element_type.54), channel_id=1, source_target_pairs={{0,24},{4,28},{8,16},{12,20},{16,8},{20,12},{24,0},{28,4},{1,25},{... | collective-permute-start | bytes 227336 | tf_op jit(solution)/shard_map/ppermute | solution.py:313
  30.9 5.7 %collective-permute-start.8 = (f16[296,128]{1,0:T(8,128)(2,1)S(1)}, f16[296,128]{1,0:T(8,128)(2,1)S(1)}, u32[]{:S(2)}, u32[]{:S(2)}) collective-permute-start(f16[296,128]{1,0:T(8,128)(2,1)S(1)} %convert_element_type.52), channel_id=1, source_target_pairs={{0,4},{4,0},{8,12},{12,8},{16,20},{20,16},{24,28},{28,24},{1,5},{5... | collective-permute-start | bytes 227336 | tf_op jit(solution)/shard_map/ppermute | solution.py:313
  32.0 4.5 %collective-permute-start.13 = (f16[152,128]{1,0:T(8,128)(2,1)S(1)}, f16[152,128]{1,0:T(8,128)(2,1)S(1)}, u32[]{:S(2)}, u32[]{:S(2)}) collective-permute-start(f16[152,128]{1,0:T(8,128)(2,1)S(1)} %convert_element_type.62), channel_id=1, source_target_pairs={{0,8},{4,12},{8,0},{12,4},{16,24},{20,28},{24,16},{28,20},{1,9},{5... | collective-permute-start | bytes 116744 | tf_op jit(solution)/shard_map/ppermute | solution.py:313

commit v7 on v6

--- a/solution.py
+++ b/solution.py
@@ -251,12 +251,12 @@
         done = 0
         for at, (i, j) in enumerate(blocks_of):
             kept_ref, arrived_ref = sums[2 * i : 2 * i + 2]
-            size = kept_ref.shape[0] // counts[i]
+            size = (kept_ref.shape[0] - TAIL) // counts[i]
             rows = slice(j * size, (j + 1) * size)
-            value = kept_ref[rows] + arrived_ref[rows] * factor_of(arrived_ref, counts[i] * size + j)
+            here, there = [ref[counts[i] * size + j : counts[i] * size + j + 1, 0:1].astype(jnp.int32) for ref in (kept_ref, arrived_ref)]
+            e = jnp.maximum(here, there) + 1 if coded else jnp.full((1, 1), TOP, jnp.int32)
+            value = kept_ref[rows] * power_of_two(here - e) + arrived_ref[rows] * power_of_two(there - e)
             if coded:
-                e = exponent_of(value)
-                value = value * power_of_two(TOP - e)
                 exponents = jnp.where(lax.broadcasted_iota(jnp.int32, (TAIL, LAG), 0) == at, e.astype(f32), exponents)
             o_ref[done : done + size] = value
             done += size
@@ -267,7 +267,7 @@
 def merge(sums, outputs):
     shapes = []
     for coded, blocks_of in outputs:
-        size = sum(sums[i][1].shape[0] // sums[i][0] for i, _ in blocks_of) + (TAIL if coded else 0)
+        size = sum((sums[i][1].shape[0] - TAIL) // sums[i][0] for i, _ in blocks_of) + (TAIL if coded else 0)
         shapes.append(jax.ShapeDtypeStruct((size, LAG), f32))
     return pl.pallas_call(
         functools.partial(merge_kernel, [count for count, _, _ in sums], outputs),
@@ -342,7 +342,7 @@
         early = [early, beside, across, swap(across, "sta", 1)]
         cross = cross_spectra(ahead, ids, src_block, owner, recv, signs, early)
         away, kept = lag_transform(
-            [(True, [(1 ^ z, ahead) for z in near + far]), (False, [(z, ahead) for z in near + far])],
+            [(True, [(1 ^ z, ahead) for z in near + far]), (True, [(z, ahead) for z in near + far])],
             ahead,
             columns,
             cross,
@@ -359,9 +359,9 @@
         arrived_far = send(away_far, 1)
         (away_near,) = lags([(True, [(2, rest), (3, rest)])], cross=cross)
         arrived_near = send(away_near, 2)
-        kept, away = merge([(4, kept, arrived)], [(False, [(0, 0), (0, 1)]), (True, [(0, 3), (0, 2)])])
+        kept, away = merge([(4, kept, arrived)], [(True, [(0, 0), (0, 1)]), (True, [(0, 3), (0, 2)])])
         arrived = send(away, 4)
-        kept_near, kept_far = lags([(False, [(z, rest) for z in of]) for of in ((0, 1), far)], cross=cross)
+        kept_near, kept_far = lags([(True, [(z, rest) for z in of]) for of in ((0, 1), far)], cross=cross)
         by_6, by_4 = merge([(2, kept_far, arrived_far)], [(True, [(0, 0)]), (True, [(0, 1)])])
         kept_near, by_6, by_4 = lax.optimization_barrier((kept_near, by_6, by_4))
         by_6 = send(by_6, 6)

time: 37.6 us -> 37.4 us (level)
  starting transfers between devices: 16.9 us -> 17.6 us
  Pallas kernels: 12.6 us -> 12 us
    pallas_call x4, Pallas kernels: 1.12 us -> 0.38 us  [merge(): pl.pallas_call(functools.partial(merge_kernel, [count for count, _, _ in...]
    ppermute x14, starting transfers between devices: 16.9 us -> 17.6 us  [swap(): return lax.ppermute(value, axis, [(i, i ^ mask) for i in range(size)])]
  transfers between devices with their start and end apart: 14 -> 14, of which waited for: 4 -> 4; matrix products, arithmetic and copies ran while one was open for 1% -> 1% of each run, Pallas kernels for 31% -> 29%
where the time goes in v7:
time: 37.4 us; the launch traced here: 37.3 us
  starting transfers between devices  17.6 us (47%)
  Pallas kernels  12 us (32%)
  waiting for transfers between devices  5.47 us (15%)
  local copies, waits for them, and re-layouts  1.69 us (5%)
    ppermute x14, starting transfers between devices, swap(): return lax.ppermute(value, axis, [(i, i ^ mask) for i in range(size)])  17.6 us
    ppermute x14, waiting for transfers between devices, swap(): return lax.ppermute(value, axis, [(i, i ^ mask) for i in range(size)])  5.47 us
    pallas_call x2, Pallas kernels, cross_spectra(): pl.pallas_call(functools.partial(cross_kernel, comps), in_specs=[SMEM] *...  4.34 us
    pallas_call x4, Pallas kernels, lag_transform(): pl.pallas_call(functools.partial(lag_kernel, outputs, held, columns), in_...  3.45 us
    pallas_call x1, Pallas kernels, receivers_by_freq(): pl.pallas_call(receivers_kernel, grid=(COMPS,), in_specs=[SMEM, pl.BlockS...  2.78 us
    unnamed x12, local copies, waits for them, and re-layouts  1.69 us
    pallas_call x1, Pallas kernels, total(): pl.pallas_call(functools.partial(total_kernel, stations, terms), in_specs...  0.78 us
  transfers between devices with their start and end apart: 14, of which 4 were waited for; matrix products, arithmetic and copies ran while one was open for 1% of the time, Pallas kernels for 29%

profile of v7, /device:TPU:0, one launch (start us, length us, event | category | flops | bytes accessed | tf_op | source)
XLA Modules:
  0.0 37.3 jit_solution(7485142071919639643)
XLA Ops:
  0.0 1.7 %copy-done = bf16[64,2,3,24,128]{4,3,2,1,0:T(8,128)(2,1)S(1)} copy-done((bf16[64,2,3,24,128]{4,3,2,1,0:T(8,128)(2,1)S(1)}, bf16[64,2,3,24,128]{4,3,2,1,0:T(8,128)(2,1)}, u32[]{:S(2)}) %copy-start) | copy-done | bytes 2359320
  1.7 0.3 first_block.1
  2.0 0.5 %collective-permute-start.1 = (bf16[1,4,128,128]{3,2,1,0:T(8,128)(2,1)S(1)}, bf16[1,4,128,128]{3,2,1,0:T(8,128)(2,1)S(1)}, u32[]{:S(2)}, u32[]{:S(2)}) collective-permute-start(bf16[1,4,128,128]{3,2,1,0:T(8,128)(2,1)S(1)} %get-tuple-element.37.rest_0_), channel_id=1, source_target_pairs={{0,1},{1,0},{2,3},{3,2},{4,5},{5,4},{6,7},{7,6},{8,9},{9,8},{10,11... | collective-permute-start | bytes 393224 | tf_op jit(solution)/shard_map/ppermute | solution.py:313
  2.5 2.6 %collective-permute-start = (bf16[1,4,128,128]{3,2,1,0:T(8,128)(2,1)S(1)}, bf16[1,4,128,128]{3,2,1,0:T(8,128)(2,1)S(1)}, u32[]{:S(2)}, u32[]{:S(2)}) collective-permute-start(bf16[1,4,128,128]{3,2,1,0:T(8,128)(2,1)S(1)} %get-tuple-element.37.rest_0_), channel_id=1, source_target_pairs={{0,2},{1,3},{2,0},{3,1},{4,6},{5,7},{6,4},{7,5},{8,10},{9,11},{10,... | collective-permute-start | bytes 393224 | tf_op jit(solution)/shard_map/ppermute | solution.py:313
  5.0 1.3 %collective-permute-start.3 = (bf16[2,4,128,128]{3,2,1,0:T(8,128)(2,1)S(1)}, bf16[2,4,128,128]{3,2,1,0:T(8,128)(2,1)S(1)}, u32[]{:S(2)}, u32[]{:S(2)}) collective-permute-start(bf16[2,4,128,128]{3,2,1,0:T(8,128)(2,1)S(1)} %get-tuple-element.44.rest_0_), channel_id=1, source_target_pairs={{0,2},{1,3},{2,0},{3,1},{4,6},{5,7},{6,4},{7,5},{8,10},{9,11},{10,... | collective-permute-start | bytes 786440 | tf_op jit(solution)/shard_map/ppermute | solution.py:313
  6.3 0.1 pad_add_fusion.ids_ref
  6.4 2.8 %receivers_by_freq.1 = (bf16[128,72,128]{2,1,0:T(8,128)(2,1)S(1)}, f32[4,128]{1,0:T(4,128)S(1)}, f32[2,128]{1,0:T(2,128)S(1)}) custom-call(s32[2]{0:T(128)S(1)} %pad_add_fusion.ids_ref, bf16[64,2,3,24,128]{4,3,2,1,0:T(8,128)(2,1)S(1)} %copy-done.1, s32[4,128]{1,0:T(4,128)S(1)} %bitcast.8), custom_call_target="tpu_custom_call" | custom-call | bytes 12582912 | tf_op jit(solution)/shard_map/receivers_by_freq/pallas_call | solution.py:108
  9.2 0.2 collective-permute-done.rest_2_
  9.4 0.5 %collective-permute-start.2 = (bf16[2,4,128,128]{3,2,1,0:T(8,128)(2,1)S(1)}, bf16[2,4,128,128]{3,2,1,0:T(8,128)(2,1)S(1)}, u32[]{:S(2)}, u32[]{:S(2)}) collective-permute-start(bf16[2,4,128,128]{3,2,1,0:T(8,128)(2,1)S(1)} %get-tuple-element.44.rest_0_), channel_id=1, source_target_pairs={{0,1},{1,0},{2,3},{3,2},{4,5},{5,4},{6,7},{7,6},{8,9},{9,8},{10,11... | collective-permute-start | bytes 786440 | tf_op jit(solution)/shard_map/ppermute | solution.py:313
  9.9 0.8 %collective-permute-done.4.rest_3_ = bf16[1,4,128,128]{3,2,1,0:T(8,128)(2,1)S(1)} collective-permute-done((bf16[1,4,128,128]{3,2,1,0:T(8,128)(2,1)S(1)}, bf16[1,4,128,128]{3,2,1,0:T(8,128)(2,1)S(1)}, u32[]{:S(2)}, u32[]{:S(2)}) %collective-permute-start.4) | collective-permute-done | bytes 131104 | tf_op jit(solution)/shard_map/ppermute | solution.py:313
  10.7 2.1 %cross_spectra.2.cross_ref = f32[4224,128]{1,0:T(8,128)S(1)} custom-call(s32[2]{0:T(128)S(1)} %pad_add_fusion.ids_ref, s32[2]{0:T(128)S(1)} %copy-done.4, s32[8]{0:T(128)S(1)} %copy-done.5, bf16[128,72,128]{2,1,0:T(8,128)(2,1)S(1)} %get-tuple-element.41.recv_ref, f32[4,128]{1,0:T(4,128)S(1)} %get-tuple-element.42.signs_ref, ...), custom_call_target="tpu_custom_call" | custom-call | bytes 10485760 | tf_op jit(solution)/shard_map/cross_spectra/pallas_call | solution.py:186
  12.9 0.0 copy-done.2
  12.9 1.0 %lag_transform.4 = (f32[584,128]{1,0:T(8,128)S(1)}, f32[584,128]{1,0:T(8,128)S(1)}) custom-call(f32[4224,128]{1,0:T(8,128)S(1)} %cross_spectra.2.cross_ref, f32[256,128]{1,0:T(8,128)S(1)} %copy-done.2, f32[2,128]{1,0:T(2,128)S(1)} %get-tuple-element.48.scale_ref), custom_call_target="tpu_custom_call" | custom-call | bytes 5242880 | tf_op jit(solution)/shard_map/lag_transform/pallas_call | solution.py:232
  14.0 0.8 %collective-permute-done.3.rest_2_ = bf16[2,4,128,128]{3,2,1,0:T(8,128)(2,1)S(1)} collective-permute-done((bf16[2,4,128,128]{3,2,1,0:T(8,128)(2,1)S(1)}, bf16[2,4,128,128]{3,2,1,0:T(8,128)(2,1)S(1)}, u32[]{:S(2)}, u32[]{:S(2)}) %collective-permute-start.3) | collective-permute-done | bytes 262176 | tf_op jit(solution)/shard_map/ppermute | solution.py:313
  14.8 1.9 %collective-permute-start.11 = (f16[584,128]{1,0:T(8,128)(2,1)S(1)}, f16[584,128]{1,0:T(8,128)(2,1)S(1)}, u32[]{:S(2)}, u32[]{:S(2)}) collective-permute-start(f16[584,128]{1,0:T(8,128)(2,1)S(1)} %convert_element_type.58), channel_id=1, source_target_pairs={{0,4},{4,0},{8,12},{12,8},{16,20},{20,16},{24,28},{28,24},{1,5},{5... | collective-permute-start | bytes 448520 | tf_op jit(solution)/shard_map/ppermute | solution.py:313
  16.6 2.2 %cross_spectra.3.cross_ref = f32[8448,128]{1,0:T(8,128)S(1)} custom-call(s32[2]{0:T(128)S(1)} %pad_add_fusion.ids_ref, s32[2]{0:T(128)S(1)} %copy-done.4, s32[8]{0:T(128)S(1)} %copy-done.5, bf16[128,72,128]{2,1,0:T(8,128)(2,1)S(1)} %get-tuple-element.41.recv_ref, f32[4,128]{1,0:T(4,128)S(1)} %get-tuple-element.42.signs_ref, ...), custom_call_target="tpu_custom_call" | custom-call | bytes 10485760 | tf_op jit(solution)/shard_map/cross_spectra/pallas_call | solution.py:186
  18.8 0.7 %lag_transform.5 = f32[584,128]{1,0:T(8,128)S(1)} custom-call(f32[8448,128]{1,0:T(8,128)S(1)} %cross_spectra.3.cross_ref, f32[256,128]{1,0:T(8,128)S(1)} %copy-done.2, f32[2,128]{1,0:T(2,128)S(1)} %get-tuple-element.48.scale_ref), custom_call_target="tpu_custom_call" | custom-call | bytes 5242880 | tf_op jit(solution)/shard_map/lag_transform/pallas_call | solution.py:232
  19.6 1.5 %collective-permute-start.6 = (f16[584,128]{1,0:T(8,128)(2,1)S(1)}, f16[584,128]{1,0:T(8,128)(2,1)S(1)}, u32[]{:S(2)}, u32[]{:S(2)}) collective-permute-start(f16[584,128]{1,0:T(8,128)(2,1)S(1)} %convert_element_type.48), channel_id=1, source_target_pairs={{0,4},{4,0},{8,12},{12,8},{16,20},{20,16},{24,28},{28,24},{1,5},{5... | collective-permute-start | bytes 448520 | tf_op jit(solution)/shard_map/ppermute | solution.py:313
  21.1 0.7 %lag_transform.7 = f32[584,128]{1,0:T(8,128)S(1)} custom-call(f32[8448,128]{1,0:T(8,128)S(1)} %cross_spectra.3.cross_ref, f32[256,128]{1,0:T(8,128)S(1)} %copy-done.2, f32[2,128]{1,0:T(2,128)S(1)} %get-tuple-element.48.scale_ref), custom_call_target="tpu_custom_call" | custom-call | bytes 5242880 | tf_op jit(solution)/shard_map/lag_transform/pallas_call | solution.py:232
  21.8 1.7 %collective-permute-start.7 = (f16[584,128]{1,0:T(8,128)(2,1)S(1)}, f16[584,128]{1,0:T(8,128)(2,1)S(1)}, u32[]{:S(2)}, u32[]{:S(2)}) collective-permute-start(f16[584,128]{1,0:T(8,128)(2,1)S(1)} %convert_element_type.50), channel_id=1, source_target_pairs={{0,8},{4,12},{8,0},{12,4},{16,24},{20,28},{24,16},{28,20},{1,9},{5... | collective-permute-start | bytes 448520 | tf_op jit(solution)/shard_map/ppermute | solution.py:313
  23.5 0.1 merge.6
  23.6 2.6 %collective-permute-start.12 = (f16[296,128]{1,0:T(8,128)(2,1)S(1)}, f16[296,128]{1,0:T(8,128)(2,1)S(1)}, u32[]{:S(2)}, u32[]{:S(2)}) collective-permute-start(f16[296,128]{1,0:T(8,128)(2,1)S(1)} %convert_element_type.60), channel_id=1, source_target_pairs={{0,16},{4,20},{8,24},{12,28},{16,0},{20,4},{24,8},{28,12},{1,17},{... | collective-permute-start | bytes 227336 | tf_op jit(solution)/shard_map/ppermute | solution.py:313
  26.2 1.0 %lag_transform.6 = (f32[584,128]{1,0:T(8,128)S(1)}, f32[584,128]{1,0:T(8,128)S(1)}) custom-call(f32[8448,128]{1,0:T(8,128)S(1)} %cross_spectra.3.cross_ref, f32[256,128]{1,0:T(8,128)S(1)} %copy-done.2, f32[2,128]{1,0:T(2,128)S(1)} %get-tuple-element.48.scale_ref), custom_call_target="tpu_custom_call" | custom-call | bytes 5242880 | tf_op jit(solution)/shard_map/lag_transform/pallas_call | solution.py:232
  27.3 0.1 merge.4
  27.5 1.0 %collective-permute-start.10 = (f16[296,128]{1,0:T(8,128)(2,1)S(1)}, f16[296,128]{1,0:T(8,128)(2,1)S(1)}, u32[]{:S(2)}, u32[]{:S(2)}) collective-permute-start(f16[296,128]{1,0:T(8,128)(2,1)S(1)} %convert_element_type.56), channel_id=1, source_target_pairs={{0,16},{4,20},{8,24},{12,28},{16,0},{20,4},{24,8},{28,12},{1,17},{... | collective-permute-start | bytes 227336 | tf_op jit(solution)/shard_map/ppermute | solution.py:313
  28.5 1.9 %collective-permute-start.9 = (f16[296,128]{1,0:T(8,128)(2,1)S(1)}, f16[296,128]{1,0:T(8,128)(2,1)S(1)}, u32[]{:S(2)}, u32[]{:S(2)}) collective-permute-start(f16[296,128]{1,0:T(8,128)(2,1)S(1)} %convert_element_type.54), channel_id=1, source_target_pairs={{0,24},{4,28},{8,16},{12,20},{16,8},{20,12},{24,0},{28,4},{1,25},{... | collective-permute-start | bytes 227336 | tf_op jit(solution)/shard_map/ppermute | solution.py:313
  30.4 0.1 merge.5
  30.5 0.9 %collective-permute-start.8 = (f16[296,128]{1,0:T(8,128)(2,1)S(1)}, f16[296,128]{1,0:T(8,128)(2,1)S(1)}, u32[]{:S(2)}, u32[]{:S(2)}) collective-permute-start(f16[296,128]{1,0:T(8,128)(2,1)S(1)} %convert_element_type.52), channel_id=1, source_target_pairs={{0,4},{4,0},{8,12},{12,8},{16,20},{20,16},{24,28},{28,24},{1,5},{5... | collective-permute-start | bytes 227336 | tf_op jit(solution)/shard_map/ppermute | solution.py:313
  31.4 0.1 merge.7
  31.5 1.3 %collective-permute-start.13 = (f16[152,128]{1,0:T(8,128)(2,1)S(1)}, f16[152,128]{1,0:T(8,128)(2,1)S(1)}, u32[]{:S(2)}, u32[]{:S(2)}) collective-permute-start(f16[152,128]{1,0:T(8,128)(2,1)S(1)} %convert_element_type.62), channel_id=1, source_target_pairs={{0,8},{4,12},{8,0},{12,4},{16,24},{20,28},{24,16},{28,20},{1,9},{5... | collective-permute-start | bytes 116744 | tf_op jit(solution)/shard_map/ppermute | solution.py:313
  32.8 3.6 %collective-permute-done.13 = f16[152,128]{1,0:T(8,128)(2,1)S(1)} collective-permute-done((f16[152,128]{1,0:T(8,128)(2,1)S(1)}, f16[152,128]{1,0:T(8,128)(2,1)S(1)}, u32[]{:S(2)}, u32[]{:S(2)}) %collective-permute-start.13) | collective-permute-done | bytes 38944 | tf_op jit(solution)/shard_map/ppermute | solution.py:313
  36.5 0.8 %total.1 = f32[432,128]{1,0:T(8,128)} custom-call(f32[288,128]{1,0:T(8,128)S(1)} %get-tuple-element.59.refs_0_, f32[296,128]{1,0:T(8,128)S(1)} %convert_element_type.53.refs_1_, f32[296,128]{1,0:T(8,128)S(1)} %convert_element_type.55.refs_2_, f32[296,128]{1,0:T(8,128)S(1)} %convert_element_type.57.refs_3_, f32[144,128]{1,0:T(8,128)S(1)} %get-tuple-element.67.refs_4_, ...), custom_call_target="tpu_custom_call" | custom-call | tf_op jit(solution)/shard_map/total/pallas_call | solution.py:301
  (38 shorter events, 0.3 us)
Async XLA Ops:
  0.0 1.7 %copy-start = (bf16[64,2,3,24,128]{4,3,2,1,0:T(8,128)(2,1)S(1)}, bf16[64,2,3,24,128]{4,3,2,1,0:T(8,128)(2,1)}, u32[]{:S(2)}) copy-start(bf16[64,2,3,24,128]{4,3,2,1,0:T(8,128)(2,1)} %x_ref.3) | copy-start | bytes 7077892
  1.7 4.7 %copy-start.1 = (bf16[64,2,3,24,128]{4,3,2,1,0:T(8,128)(2,1)S(1)}, bf16[64,2,3,24,128]{4,3,2,1,0:T(8,128)(2,1)}, u32[]{:S(2)}) copy-start(bf16[64,2,3,24,128]{4,3,2,1,0:T(8,128)(2,1)} %x_ref.3) | copy-start | bytes 7077892
  1.7 4.7 %copy-start.3 = (s32[512]{0:T(512)S(1)}, s32[512]{0:T(512)}, u32[]{:S(2)}) copy-start(s32[512]{0:T(512)} %param.7) | copy-start | bytes 6148
  1.7 9.1 %copy-start.4 = (s32[2]{0:T(128)S(1)}, s32[2]{0:T(128)}, u32[]{:S(2)}) copy-start(s32[2]{0:T(128)} %src_block_ref.3) | copy-start | bytes 28
  1.7 9.1 %copy-start.5 = (s32[8]{0:T(128)S(1)}, s32[8]{0:T(128)}, u32[]{:S(2)}) copy-start(s32[8]{0:T(128)} %owner_ref.3) | copy-start | bytes 100
  2.0 3.1 %collective-permute-start.1 = (bf16[1,4,128,128]{3,2,1,0:T(8,128)(2,1)S(1)}, bf16[1,4,128,128]{3,2,1,0:T(8,128)(2,1)S(1)}, u32[]{:S(2)}, u32[]{:S(2)}) collective-permute-start(bf16[1,4,128,128]{3,2,1,0:T(8,128)(2,1)S(1)} %get-tuple-element.37.rest_0_), channel_id=1, source_target_pairs={{0,1},{1,0},{2,3},{3,2},{4,5},{5,4},{6,7},{7,6},{8,9},{9,8},{10,11... | collective-permute-start | bytes 393224 | tf_op jit(solution)/shard_map/ppermute | solution.py:313
  2.5 6.9 %collective-permute-start = (bf16[1,4,128,128]{3,2,1,0:T(8,128)(2,1)S(1)}, bf16[1,4,128,128]{3,2,1,0:T(8,128)(2,1)S(1)}, u32[]{:S(2)}, u32[]{:S(2)}) collective-permute-start(bf16[1,4,128,128]{3,2,1,0:T(8,128)(2,1)S(1)} %get-tuple-element.37.rest_0_), channel_id=1, source_target_pairs={{0,2},{1,3},{2,0},{3,1},{4,6},{5,7},{6,4},{7,5},{8,10},{9,11},{10,... | collective-permute-start | bytes 393224 | tf_op jit(solution)/shard_map/ppermute | solution.py:313
  5.0 9.7 %collective-permute-start.3 = (bf16[2,4,128,128]{3,2,1,0:T(8,128)(2,1)S(1)}, bf16[2,4,128,128]{3,2,1,0:T(8,128)(2,1)S(1)}, u32[]{:S(2)}, u32[]{:S(2)}) collective-permute-start(bf16[2,4,128,128]{3,2,1,0:T(8,128)(2,1)S(1)} %get-tuple-element.44.rest_0_), channel_id=1, source_target_pairs={{0,2},{1,3},{2,0},{3,1},{4,6},{5,7},{6,4},{7,5},{8,10},{9,11},{10,... | collective-permute-start | bytes 786440 | tf_op jit(solution)/shard_map/ppermute | solution.py:313
  9.4 3.5 %copy-start.2 = (f32[256,128]{1,0:T(8,128)S(1)}, f32[256,128]{1,0:T(8,128)}, u32[]{:S(2)}) copy-start(f32[256,128]{1,0:T(8,128)} %constant.11.clone.table_ref) | copy-start | bytes 393220
  9.4 1.3 %collective-permute-start.4 = (bf16[1,4,128,128]{3,2,1,0:T(8,128)(2,1)S(1)}, bf16[1,4,128,128]{3,2,1,0:T(8,128)(2,1)S(1)}, u32[]{:S(2)}, u32[]{:S(2)}) collective-permute-start(bf16[1,4,128,128]{3,2,1,0:T(8,128)(2,1)S(1)} %collective-permute-done.rest_2_), channel_id=1, source_target_pairs={{0,1},{1,0},{2,3},{3,2},{4,5},{5,4},{6,7},{7,6},{8,9},{9,8},{10,11... | collective-permute-start | bytes 393224 | tf_op jit(solution)/shard_map/ppermute | solution.py:313
  9.4 7.2 %collective-permute-start.2 = (bf16[2,4,128,128]{3,2,1,0:T(8,128)(2,1)S(1)}, bf16[2,4,128,128]{3,2,1,0:T(8,128)(2,1)S(1)}, u32[]{:S(2)}, u32[]{:S(2)}) collective-permute-start(bf16[2,4,128,128]{3,2,1,0:T(8,128)(2,1)S(1)} %get-tuple-element.44.rest_0_), channel_id=1, source_target_pairs={{0,1},{1,0},{2,3},{3,2},{4,5},{5,4},{6,7},{7,6},{8,9},{9,8},{10,11... | collective-permute-start | bytes 786440 | tf_op jit(solution)/shard_map/ppermute | solution.py:313
  14.7 1.9 %collective-permute-start.5 = (bf16[2,4,128,128]{3,2,1,0:T(8,128)(2,1)S(1)}, bf16[2,4,128,128]{3,2,1,0:T(8,128)(2,1)S(1)}, u32[]{:S(2)}, u32[]{:S(2)}) collective-permute-start(bf16[2,4,128,128]{3,2,1,0:T(8,128)(2,1)S(1)} %collective-permute-done.3.rest_2_), channel_id=1, source_target_pairs={{0,1},{1,0},{2,3},{3,2},{4,5},{5,4},{6,7},{7,6},{8,9},{9,8},{10,11... | collective-permute-start | bytes 786440 | tf_op jit(solution)/shard_map/ppermute | solution.py:313
  14.8 8.7 %collective-permute-start.11 = (f16[584,128]{1,0:T(8,128)(2,1)S(1)}, f16[584,128]{1,0:T(8,128)(2,1)S(1)}, u32[]{:S(2)}, u32[]{:S(2)}) collective-permute-start(f16[584,128]{1,0:T(8,128)(2,1)S(1)} %convert_element_type.58), channel_id=1, source_target_pairs={{0,4},{4,0},{8,12},{12,8},{16,20},{20,16},{24,28},{28,24},{1,5},{5... | collective-permute-start | bytes 448520 | tf_op jit(solution)/shard_map/ppermute | solution.py:313
  19.6 7.7 %collective-permute-start.6 = (f16[584,128]{1,0:T(8,128)(2,1)S(1)}, f16[584,128]{1,0:T(8,128)(2,1)S(1)}, u32[]{:S(2)}, u32[]{:S(2)}) collective-permute-start(f16[584,128]{1,0:T(8,128)(2,1)S(1)} %convert_element_type.48), channel_id=1, source_target_pairs={{0,4},{4,0},{8,12},{12,8},{16,20},{20,16},{24,28},{28,24},{1,5},{5... | collective-permute-start | bytes 448520 | tf_op jit(solution)/shard_map/ppermute | solution.py:313
  21.8 8.6 %collective-permute-start.7 = (f16[584,128]{1,0:T(8,128)(2,1)S(1)}, f16[584,128]{1,0:T(8,128)(2,1)S(1)}, u32[]{:S(2)}, u32[]{:S(2)}) collective-permute-start(f16[584,128]{1,0:T(8,128)(2,1)S(1)} %convert_element_type.50), channel_id=1, source_target_pairs={{0,8},{4,12},{8,0},{12,4},{16,24},{20,28},{24,16},{28,20},{1,9},{5... | collective-permute-start | bytes 448520 | tf_op jit(solution)/shard_map/ppermute | solution.py:313
  23.6 7.8 %collective-permute-start.12 = (f16[296,128]{1,0:T(8,128)(2,1)S(1)}, f16[296,128]{1,0:T(8,128)(2,1)S(1)}, u32[]{:S(2)}, u32[]{:S(2)}) collective-permute-start(f16[296,128]{1,0:T(8,128)(2,1)S(1)} %convert_element_type.60), channel_id=1, source_target_pairs={{0,16},{4,20},{8,24},{12,28},{16,0},{20,4},{24,8},{28,12},{1,17},{... | collective-permute-start | bytes 227336 | tf_op jit(solution)/shard_map/ppermute | solution.py:313
  27.5 8.9 %collective-permute-start.10 = (f16[296,128]{1,0:T(8,128)(2,1)S(1)}, f16[296,128]{1,0:T(8,128)(2,1)S(1)}, u32[]{:S(2)}, u32[]{:S(2)}) collective-permute-start(f16[296,128]{1,0:T(8,128)(2,1)S(1)} %convert_element_type.56), channel_id=1, source_target_pairs={{0,16},{4,20},{8,24},{12,28},{16,0},{20,4},{24,8},{28,12},{1,17},{... | collective-permute-start | bytes 227336 | tf_op jit(solution)/shard_map/ppermute | solution.py:313
  28.5 8.0 %collective-permute-start.9 = (f16[296,128]{1,0:T(8,128)(2,1)S(1)}, f16[296,128]{1,0:T(8,128)(2,1)S(1)}, u32[]{:S(2)}, u32[]{:S(2)}) collective-permute-start(f16[296,128]{1,0:T(8,128)(2,1)S(1)} %convert_element_type.54), channel_id=1, source_target_pairs={{0,24},{4,28},{8,16},{12,20},{16,8},{20,12},{24,0},{28,4},{1,25},{... | collective-permute-start | bytes 227336 | tf_op jit(solution)/shard_map/ppermute | solution.py:313
  30.5 6.0 %collective-permute-start.8 = (f16[296,128]{1,0:T(8,128)(2,1)S(1)}, f16[296,128]{1,0:T(8,128)(2,1)S(1)}, u32[]{:S(2)}, u32[]{:S(2)}) collective-permute-start(f16[296,128]{1,0:T(8,128)(2,1)S(1)} %convert_element_type.52), channel_id=1, source_target_pairs={{0,4},{4,0},{8,12},{12,8},{16,20},{20,16},{24,28},{28,24},{1,5},{5... | collective-permute-start | bytes 227336 | tf_op jit(solution)/shard_map/ppermute | solution.py:313
  31.5 4.9 %collective-permute-start.13 = (f16[152,128]{1,0:T(8,128)(2,1)S(1)}, f16[152,128]{1,0:T(8,128)(2,1)S(1)}, u32[]{:S(2)}, u32[]{:S(2)}) collective-permute-start(f16[152,128]{1,0:T(8,128)(2,1)S(1)} %convert_element_type.62), channel_id=1, source_target_pairs={{0,8},{4,12},{8,0},{12,4},{16,24},{20,28},{24,16},{28,20},{1,9},{5... | collective-permute-start | bytes 116744 | tf_op jit(solution)/shard_map/ppermute | solution.py:313

commit v8 on v7

--- a/solution.py
+++ b/solution.py
@@ -67,63 +67,49 @@
 
 
 def receivers_kernel(ids_ref, x_ref, group_ref, o_ref, signs_ref, scale_ref, wide, turned):
-    b = pl.program_id(0)
     rows = x_ref.shape[0] * 2
     stations = x_ref.shape[3]
-    for part in range(2):
-        wide[part] = x_ref[:, part, 0].astype(f32)
-    flat = wide.reshape(rows * stations, F)
-    for r in range(stations):
-        turned[pl.ds(b * stations + r, F, stride=COMPS * stations), :] = flat[pl.ds(r, rows, stride=stations), :].T
-
-    @pl.when(b == 0)
-    def _():
-        at = ids_ref[0] * (rows // 2)
-        row = group_ref[pl.ds(at // rows, 1), :].astype(f32)
-        swapped = pltpu.roll(row, rows // 2, 1)
-        low = lax.broadcasted_iota(jnp.int32, row.shape, 1) < rows // 2
-        mine = jnp.where(low == (at % rows == 0), row, swapped)
-        for g in range(G):
-            hot = jnp.where(mine == g, np.float32(1.0), np.float32(0.0))
-            signs_ref[g : g + 1] = hot
-            signs_ref[G + g : G + g + 1] = jnp.where(low, -hot, hot)
-            hits = jnp.where(group_ref[...] == g, np.float32(1.0), np.float32(0.0))
-            count = jnp.sum(hits, axis=(0, 1), keepdims=True)
-            scale_ref[g : g + 1] = jnp.broadcast_to(1.0 / jnp.sqrt(count), (1, LAG))
-
-    @pl.when(b == COMPS - 1)
-    def _():
-        def body(f, carry):
-            o_ref[f] = turned[pl.ds(pl.multiple_of(f * COMPS * stations, 8), COMPS * stations), :].astype(bf16)
-            return carry
-
-        lax.fori_loop(0, F, body, 0, unroll=8)
+    columns = COMPS * stations
+    at = ids_ref[0] * (rows // 2)
+    row = group_ref[pl.ds(at // rows, 1), :].astype(f32)
+    swapped = pltpu.roll(row, rows // 2, 1)
+    low = lax.broadcasted_iota(jnp.int32, row.shape, 1) < rows // 2
+    mine = jnp.where(low == (at % rows == 0), row, swapped)
+    for g in range(G):
+        hot = jnp.where(mine == g, np.float32(1.0), np.float32(0.0))
+        signs_ref[g : g + 1] = hot
+        signs_ref[G + g : G + g + 1] = jnp.where(low, -hot, hot)
+        hits = jnp.where(group_ref[...] == g, np.float32(1.0), np.float32(0.0))
+        count = jnp.sum(hits, axis=(0, 1), keepdims=True)
+        scale_ref[g : g + 1] = jnp.broadcast_to(1.0 / jnp.sqrt(count), (1, LAG))
+    for b in range(COMPS):
+        for part in range(2):
+            wide[b, part] = x_ref[:, part, b].astype(f32)
+        flat = wide.at[b].reshape(rows * stations, F)
+        for r in range(stations):
+            turned[pl.ds(b * stations + r, F, stride=columns), :] = flat[pl.ds(r, rows, stride=stations), :].T
+
+    def body(f, carry):
+        o_ref[f] = turned[pl.ds(pl.multiple_of(f * columns, 8), columns), :].astype(bf16)
+        return carry
+
+    lax.fori_loop(0, F, body, 0, unroll=16)
 
 
 def receivers_by_freq(ids, spectra, group_of):
     segs, stations = spectra.shape[0], spectra.shape[3]
     columns = COMPS * stations
     groups = group_of.reshape(-1, 2 * segs)
-    fixed = lambda b: (0, 0)
     return pl.pallas_call(
         receivers_kernel,
-        grid=(COMPS,),
-        in_specs=[
-            SMEM,
-            pl.BlockSpec((segs, 2, 1, stations, F), lambda b: (0, 0, b, 0, 0)),
-            pl.BlockSpec(groups.shape, fixed),
-        ],
-        out_specs=[
-            pl.BlockSpec((F, columns, 2 * segs), lambda b: (0, 0, 0)),
-            pl.BlockSpec((2 * G, 2 * segs), fixed),
-            pl.BlockSpec((G, LAG), fixed),
-        ],
+        in_specs=[SMEM, VMEM, VMEM],
+        out_specs=[VMEM] * 3,
         out_shape=[
             jax.ShapeDtypeStruct((F, columns, 2 * segs), bf16),
             jax.ShapeDtypeStruct((2 * G, 2 * segs), f32),
             jax.ShapeDtypeStruct((G, LAG), f32),
         ],
-        scratch_shapes=[pltpu.VMEM((2, segs, stations, F), f32), pltpu.VMEM((F * columns, 2 * segs), f32)],
+        scratch_shapes=[pltpu.VMEM((COMPS, 2, segs, stations, F), f32), pltpu.VMEM((F * columns, 2 * segs), f32)],
         compiler_params=PARAMS,
         cost_estimate=pl.CostEstimate(flops=0, bytes_accessed=12 << 20, transcendentals=0),
         name="receivers_by_freq",

time: 37.4 us -> 37.4 us (level)
  waiting for transfers between devices: 5.47 us -> 5.89 us
  Pallas kernels: 12 us -> 11.6 us
    pallas_call x1, Pallas kernels: 2.78 us -> 2.35 us  [receivers_by_freq(): pl.pallas_call(receivers_kernel, in_specs=[SMEM, VMEM, VMEM], out_specs=[...]
    ppermute x14, waiting for transfers between devices: 5.47 us -> 5.89 us  [swap(): return lax.ppermute(value, axis, [(i, i ^ mask) for i in range(size)])]
  transfers between devices with their start and end apart: 14 -> 14, of which waited for: 4 -> 4; matrix products, arithmetic and copies ran while one was open for 1% -> 1% of each run, Pallas kernels for 29% -> 28%
where the time goes in v8:
time: 37.4 us; the launch traced here: 37.3 us
  starting transfers between devices  17.6 us (47%)
  Pallas kernels  11.6 us (31%)
  waiting for transfers between devices  5.89 us (16%)
  local copies, waits for them, and re-layouts  1.69 us (5%)
    ppermute x14, starting transfers between devices, swap(): return lax.ppermute(value, axis, [(i, i ^ mask) for i in range(size)])  17.6 us
    ppermute x14, waiting for transfers between devices, swap(): return lax.ppermute(value, axis, [(i, i ^ mask) for i in range(size)])  5.89 us
    pallas_call x2, Pallas kernels, cross_spectra(): pl.pallas_call(functools.partial(cross_kernel, comps), in_specs=[SMEM] *...  4.34 us
    pallas_call x4, Pallas kernels, lag_transform(): pl.pallas_call(functools.partial(lag_kernel, outputs, held, columns), in_...  3.45 us
    pallas_call x1, Pallas kernels, receivers_by_freq(): pl.pallas_call(receivers_kernel, in_specs=[SMEM, VMEM, VMEM], out_specs=[...  2.35 us
    unnamed x12, local copies, waits for them, and re-layouts  1.69 us
    pallas_call x1, Pallas kernels, total(): pl.pallas_call(functools.partial(total_kernel, stations, terms), in_specs...  0.78 us
  transfers between devices with their start and end apart: 14, of which 4 were waited for; matrix products, arithmetic and copies ran while one was open for 1% of the time, Pallas kernels for 28%

profile of v8, /device:TPU:0, one launch (start us, length us, event | category | flops | bytes accessed | tf_op | source)
XLA Modules:
  0.0 37.3 jit_solution(18241872601163362660)
XLA Ops:
  0.0 1.7 %copy-done = bf16[64,2,3,24,128]{4,3,2,1,0:T(8,128)(2,1)S(1)} copy-done((bf16[64,2,3,24,128]{4,3,2,1,0:T(8,128)(2,1)S(1)}, bf16[64,2,3,24,128]{4,3,2,1,0:T(8,128)(2,1)}, u32[]{:S(2)}) %copy-start) | copy-done | bytes 2359320
  1.7 0.3 first_block.1
  2.0 0.5 %collective-permute-start.1 = (bf16[1,4,128,128]{3,2,1,0:T(8,128)(2,1)S(1)}, bf16[1,4,128,128]{3,2,1,0:T(8,128)(2,1)S(1)}, u32[]{:S(2)}, u32[]{:S(2)}) collective-permute-start(bf16[1,4,128,128]{3,2,1,0:T(8,128)(2,1)S(1)} %get-tuple-element.37.rest_0_), channel_id=1, source_target_pairs={{0,1},{1,0},{2,3},{3,2},{4,5},{5,4},{6,7},{7,6},{8,9},{9,8},{10,11... | collective-permute-start | bytes 393224 | tf_op jit(solution)/shard_map/ppermute | solution.py:299
  2.5 2.6 %collective-permute-start = (bf16[1,4,128,128]{3,2,1,0:T(8,128)(2,1)S(1)}, bf16[1,4,128,128]{3,2,1,0:T(8,128)(2,1)S(1)}, u32[]{:S(2)}, u32[]{:S(2)}) collective-permute-start(bf16[1,4,128,128]{3,2,1,0:T(8,128)(2,1)S(1)} %get-tuple-element.37.rest_0_), channel_id=1, source_target_pairs={{0,2},{1,3},{2,0},{3,1},{4,6},{5,7},{6,4},{7,5},{8,10},{9,11},{10,... | collective-permute-start | bytes 393224 | tf_op jit(solution)/shard_map/ppermute | solution.py:299
  5.0 1.3 %collective-permute-start.3 = (bf16[2,4,128,128]{3,2,1,0:T(8,128)(2,1)S(1)}, bf16[2,4,128,128]{3,2,1,0:T(8,128)(2,1)S(1)}, u32[]{:S(2)}, u32[]{:S(2)}) collective-permute-start(bf16[2,4,128,128]{3,2,1,0:T(8,128)(2,1)S(1)} %get-tuple-element.44.rest_0_), channel_id=1, source_target_pairs={{0,2},{1,3},{2,0},{3,1},{4,6},{5,7},{6,4},{7,5},{8,10},{9,11},{10,... | collective-permute-start | bytes 786440 | tf_op jit(solution)/shard_map/ppermute | solution.py:299
  6.3 0.1 pad_add_fusion.ids_ref
  6.4 2.4 %receivers_by_freq.1 = (bf16[128,72,128]{2,1,0:T(8,128)(2,1)S(1)}, f32[4,128]{1,0:T(4,128)S(1)}, f32[2,128]{1,0:T(2,128)S(1)}) custom-call(s32[2]{0:T(128)S(1)} %pad_add_fusion.ids_ref, bf16[64,2,3,24,128]{4,3,2,1,0:T(8,128)(2,1)S(1)} %copy-done.1, s32[4,128]{1,0:T(4,128)S(1)} %bitcast.8), custom_call_target="tpu_custom_call" | custom-call | bytes 12582912 | tf_op jit(solution)/shard_map/receivers_by_freq/pallas_call | solution.py:103
  8.7 0.6 %collective-permute-done.rest_2_ = bf16[1,4,128,128]{3,2,1,0:T(8,128)(2,1)S(1)} collective-permute-done((bf16[1,4,128,128]{3,2,1,0:T(8,128)(2,1)S(1)}, bf16[1,4,128,128]{3,2,1,0:T(8,128)(2,1)S(1)}, u32[]{:S(2)}, u32[]{:S(2)}) %collective-permute-start) | collective-permute-done | bytes 131104 | tf_op jit(solution)/shard_map/ppermute | solution.py:299
  9.4 0.5 %collective-permute-start.2 = (bf16[2,4,128,128]{3,2,1,0:T(8,128)(2,1)S(1)}, bf16[2,4,128,128]{3,2,1,0:T(8,128)(2,1)S(1)}, u32[]{:S(2)}, u32[]{:S(2)}) collective-permute-start(bf16[2,4,128,128]{3,2,1,0:T(8,128)(2,1)S(1)} %get-tuple-element.44.rest_0_), channel_id=1, source_target_pairs={{0,1},{1,0},{2,3},{3,2},{4,5},{5,4},{6,7},{7,6},{8,9},{9,8},{10,11... | collective-permute-start | bytes 786440 | tf_op jit(solution)/shard_map/ppermute | solution.py:299
  9.9 0.8 %collective-permute-done.4.rest_3_ = bf16[1,4,128,128]{3,2,1,0:T(8,128)(2,1)S(1)} collective-permute-done((bf16[1,4,128,128]{3,2,1,0:T(8,128)(2,1)S(1)}, bf16[1,4,128,128]{3,2,1,0:T(8,128)(2,1)S(1)}, u32[]{:S(2)}, u32[]{:S(2)}) %collective-permute-start.4) | collective-permute-done | bytes 131104 | tf_op jit(solution)/shard_map/ppermute | solution.py:299
  10.7 2.1 %cross_spectra.2.cross_ref = f32[4224,128]{1,0:T(8,128)S(1)} custom-call(s32[2]{0:T(128)S(1)} %pad_add_fusion.ids_ref, s32[2]{0:T(128)S(1)} %copy-done.4, s32[8]{0:T(128)S(1)} %copy-done.5, bf16[128,72,128]{2,1,0:T(8,128)(2,1)S(1)} %get-tuple-element.41.recv_ref, f32[4,128]{1,0:T(4,128)S(1)} %get-tuple-element.42.signs_ref, ...), custom_call_target="tpu_custom_call" | custom-call | bytes 10485760 | tf_op jit(solution)/shard_map/cross_spectra/pallas_call | solution.py:172
  12.9 0.0 copy-done.2
  12.9 1.0 %lag_transform.4 = (f32[584,128]{1,0:T(8,128)S(1)}, f32[584,128]{1,0:T(8,128)S(1)}) custom-call(f32[4224,128]{1,0:T(8,128)S(1)} %cross_spectra.2.cross_ref, f32[256,128]{1,0:T(8,128)S(1)} %copy-done.2, f32[2,128]{1,0:T(2,128)S(1)} %get-tuple-element.48.scale_ref), custom_call_target="tpu_custom_call" | custom-call | bytes 5242880 | tf_op jit(solution)/shard_map/lag_transform/pallas_call | solution.py:218
  14.0 0.8 %collective-permute-done.3.rest_2_ = bf16[2,4,128,128]{3,2,1,0:T(8,128)(2,1)S(1)} collective-permute-done((bf16[2,4,128,128]{3,2,1,0:T(8,128)(2,1)S(1)}, bf16[2,4,128,128]{3,2,1,0:T(8,128)(2,1)S(1)}, u32[]{:S(2)}, u32[]{:S(2)}) %collective-permute-start.3) | collective-permute-done | bytes 262176 | tf_op jit(solution)/shard_map/ppermute | solution.py:299
  14.8 1.9 %collective-permute-start.11 = (f16[584,128]{1,0:T(8,128)(2,1)S(1)}, f16[584,128]{1,0:T(8,128)(2,1)S(1)}, u32[]{:S(2)}, u32[]{:S(2)}) collective-permute-start(f16[584,128]{1,0:T(8,128)(2,1)S(1)} %convert_element_type.58), channel_id=1, source_target_pairs={{0,4},{4,0},{8,12},{12,8},{16,20},{20,16},{24,28},{28,24},{1,5},{5... | collective-permute-start | bytes 448520 | tf_op jit(solution)/shard_map/ppermute | solution.py:299
  16.6 2.2 %cross_spectra.3.cross_ref = f32[8448,128]{1,0:T(8,128)S(1)} custom-call(s32[2]{0:T(128)S(1)} %pad_add_fusion.ids_ref, s32[2]{0:T(128)S(1)} %copy-done.4, s32[8]{0:T(128)S(1)} %copy-done.5, bf16[128,72,128]{2,1,0:T(8,128)(2,1)S(1)} %get-tuple-element.41.recv_ref, f32[4,128]{1,0:T(4,128)S(1)} %get-tuple-element.42.signs_ref, ...), custom_call_target="tpu_custom_call" | custom-call | bytes 10485760 | tf_op jit(solution)/shard_map/cross_spectra/pallas_call | solution.py:172
  18.8 0.7 %lag_transform.5 = f32[584,128]{1,0:T(8,128)S(1)} custom-call(f32[8448,128]{1,0:T(8,128)S(1)} %cross_spectra.3.cross_ref, f32[256,128]{1,0:T(8,128)S(1)} %copy-done.2, f32[2,128]{1,0:T(2,128)S(1)} %get-tuple-element.48.scale_ref), custom_call_target="tpu_custom_call" | custom-call | bytes 5242880 | tf_op jit(solution)/shard_map/lag_transform/pallas_call | solution.py:218
  19.6 1.5 %collective-permute-start.6 = (f16[584,128]{1,0:T(8,128)(2,1)S(1)}, f16[584,128]{1,0:T(8,128)(2,1)S(1)}, u32[]{:S(2)}, u32[]{:S(2)}) collective-permute-start(f16[584,128]{1,0:T(8,128)(2,1)S(1)} %convert_element_type.48), channel_id=1, source_target_pairs={{0,4},{4,0},{8,12},{12,8},{16,20},{20,16},{24,28},{28,24},{1,5},{5... | collective-permute-start | bytes 448520 | tf_op jit(solution)/shard_map/ppermute | solution.py:299
  21.1 0.7 %lag_transform.7 = f32[584,128]{1,0:T(8,128)S(1)} custom-call(f32[8448,128]{1,0:T(8,128)S(1)} %cross_spectra.3.cross_ref, f32[256,128]{1,0:T(8,128)S(1)} %copy-done.2, f32[2,128]{1,0:T(2,128)S(1)} %get-tuple-element.48.scale_ref), custom_call_target="tpu_custom_call" | custom-call | bytes 5242880 | tf_op jit(solution)/shard_map/lag_transform/pallas_call | solution.py:218
  21.8 1.7 %collective-permute-start.7 = (f16[584,128]{1,0:T(8,128)(2,1)S(1)}, f16[584,128]{1,0:T(8,128)(2,1)S(1)}, u32[]{:S(2)}, u32[]{:S(2)}) collective-permute-start(f16[584,128]{1,0:T(8,128)(2,1)S(1)} %convert_element_type.50), channel_id=1, source_target_pairs={{0,8},{4,12},{8,0},{12,4},{16,24},{20,28},{24,16},{28,20},{1,9},{5... | collective-permute-start | bytes 448520 | tf_op jit(solution)/shard_map/ppermute | solution.py:299
  23.5 0.1 merge.6
  23.6 2.6 %collective-permute-start.12 = (f16[296,128]{1,0:T(8,128)(2,1)S(1)}, f16[296,128]{1,0:T(8,128)(2,1)S(1)}, u32[]{:S(2)}, u32[]{:S(2)}) collective-permute-start(f16[296,128]{1,0:T(8,128)(2,1)S(1)} %convert_element_type.60), channel_id=1, source_target_pairs={{0,16},{4,20},{8,24},{12,28},{16,0},{20,4},{24,8},{28,12},{1,17},{... | collective-permute-start | bytes 227336 | tf_op jit(solution)/shard_map/ppermute | solution.py:299
  26.2 1.0 %lag_transform.6 = (f32[584,128]{1,0:T(8,128)S(1)}, f32[584,128]{1,0:T(8,128)S(1)}) custom-call(f32[8448,128]{1,0:T(8,128)S(1)} %cross_spectra.3.cross_ref, f32[256,128]{1,0:T(8,128)S(1)} %copy-done.2, f32[2,128]{1,0:T(2,128)S(1)} %get-tuple-element.48.scale_ref), custom_call_target="tpu_custom_call" | custom-call | bytes 5242880 | tf_op jit(solution)/shard_map/lag_transform/pallas_call | solution.py:218
  27.3 0.1 merge.4
  27.5 1.0 %collective-permute-start.10 = (f16[296,128]{1,0:T(8,128)(2,1)S(1)}, f16[296,128]{1,0:T(8,128)(2,1)S(1)}, u32[]{:S(2)}, u32[]{:S(2)}) collective-permute-start(f16[296,128]{1,0:T(8,128)(2,1)S(1)} %convert_element_type.56), channel_id=1, source_target_pairs={{0,16},{4,20},{8,24},{12,28},{16,0},{20,4},{24,8},{28,12},{1,17},{... | collective-permute-start | bytes 227336 | tf_op jit(solution)/shard_map/ppermute | solution.py:299
  28.5 1.9 %collective-permute-start.9 = (f16[296,128]{1,0:T(8,128)(2,1)S(1)}, f16[296,128]{1,0:T(8,128)(2,1)S(1)}, u32[]{:S(2)}, u32[]{:S(2)}) collective-permute-start(f16[296,128]{1,0:T(8,128)(2,1)S(1)} %convert_element_type.54), channel_id=1, source_target_pairs={{0,24},{4,28},{8,16},{12,20},{16,8},{20,12},{24,0},{28,4},{1,25},{... | collective-permute-start | bytes 227336 | tf_op jit(solution)/shard_map/ppermute | solution.py:299
  30.4 0.1 merge.5
  30.5 0.9 %collective-permute-start.8 = (f16[296,128]{1,0:T(8,128)(2,1)S(1)}, f16[296,128]{1,0:T(8,128)(2,1)S(1)}, u32[]{:S(2)}, u32[]{:S(2)}) collective-permute-start(f16[296,128]{1,0:T(8,128)(2,1)S(1)} %convert_element_type.52), channel_id=1, source_target_pairs={{0,4},{4,0},{8,12},{12,8},{16,20},{20,16},{24,28},{28,24},{1,5},{5... | collective-permute-start | bytes 227336 | tf_op jit(solution)/shard_map/ppermute | solution.py:299
  31.4 0.1 merge.7
  31.5 1.3 %collective-permute-start.13 = (f16[152,128]{1,0:T(8,128)(2,1)S(1)}, f16[152,128]{1,0:T(8,128)(2,1)S(1)}, u32[]{:S(2)}, u32[]{:S(2)}) collective-permute-start(f16[152,128]{1,0:T(8,128)(2,1)S(1)} %convert_element_type.62), channel_id=1, source_target_pairs={{0,8},{4,12},{8,0},{12,4},{16,24},{20,28},{24,16},{28,20},{1,9},{5... | collective-permute-start | bytes 116744 | tf_op jit(solution)/shard_map/ppermute | solution.py:299
  32.8 3.6 %collective-permute-done.13 = f16[152,128]{1,0:T(8,128)(2,1)S(1)} collective-permute-done((f16[152,128]{1,0:T(8,128)(2,1)S(1)}, f16[152,128]{1,0:T(8,128)(2,1)S(1)}, u32[]{:S(2)}, u32[]{:S(2)}) %collective-permute-start.13) | collective-permute-done | bytes 38944 | tf_op jit(solution)/shard_map/ppermute | solution.py:299
  36.5 0.8 %total.1 = f32[432,128]{1,0:T(8,128)} custom-call(f32[288,128]{1,0:T(8,128)S(1)} %get-tuple-element.59.refs_0_, f32[296,128]{1,0:T(8,128)S(1)} %convert_element_type.53.refs_1_, f32[296,128]{1,0:T(8,128)S(1)} %convert_element_type.55.refs_2_, f32[296,128]{1,0:T(8,128)S(1)} %convert_element_type.57.refs_3_, f32[144,128]{1,0:T(8,128)S(1)} %get-tuple-element.67.refs_4_, ...), custom_call_target="tpu_custom_call" | custom-call | tf_op jit(solution)/shard_map/total/pallas_call | solution.py:287
  (38 shorter events, 0.3 us)
Async XLA Ops:
  0.0 1.7 %copy-start = (bf16[64,2,3,24,128]{4,3,2,1,0:T(8,128)(2,1)S(1)}, bf16[64,2,3,24,128]{4,3,2,1,0:T(8,128)(2,1)}, u32[]{:S(2)}) copy-start(bf16[64,2,3,24,128]{4,3,2,1,0:T(8,128)(2,1)} %x_ref.3) | copy-start | bytes 7077892
  1.7 4.7 %copy-start.1 = (bf16[64,2,3,24,128]{4,3,2,1,0:T(8,128)(2,1)S(1)}, bf16[64,2,3,24,128]{4,3,2,1,0:T(8,128)(2,1)}, u32[]{:S(2)}) copy-start(bf16[64,2,3,24,128]{4,3,2,1,0:T(8,128)(2,1)} %x_ref.3) | copy-start | bytes 7077892
  1.7 4.7 %copy-start.3 = (s32[512]{0:T(512)S(1)}, s32[512]{0:T(512)}, u32[]{:S(2)}) copy-start(s32[512]{0:T(512)} %param.7) | copy-start | bytes 6148
  1.7 9.1 %copy-start.4 = (s32[2]{0:T(128)S(1)}, s32[2]{0:T(128)}, u32[]{:S(2)}) copy-start(s32[2]{0:T(128)} %src_block_ref.3) | copy-start | bytes 28
  1.7 9.1 %copy-start.5 = (s32[8]{0:T(128)S(1)}, s32[8]{0:T(128)}, u32[]{:S(2)}) copy-start(s32[8]{0:T(128)} %owner_ref.3) | copy-start | bytes 100
  2.0 3.1 %collective-permute-start.1 = (bf16[1,4,128,128]{3,2,1,0:T(8,128)(2,1)S(1)}, bf16[1,4,128,128]{3,2,1,0:T(8,128)(2,1)S(1)}, u32[]{:S(2)}, u32[]{:S(2)}) collective-permute-start(bf16[1,4,128,128]{3,2,1,0:T(8,128)(2,1)S(1)} %get-tuple-element.37.rest_0_), channel_id=1, source_target_pairs={{0,1},{1,0},{2,3},{3,2},{4,5},{5,4},{6,7},{7,6},{8,9},{9,8},{10,11... | collective-permute-start | bytes 393224 | tf_op jit(solution)/shard_map/ppermute | solution.py:299
  2.5 6.9 %collective-permute-start = (bf16[1,4,128,128]{3,2,1,0:T(8,128)(2,1)S(1)}, bf16[1,4,128,128]{3,2,1,0:T(8,128)(2,1)S(1)}, u32[]{:S(2)}, u32[]{:S(2)}) collective-permute-start(bf16[1,4,128,128]{3,2,1,0:T(8,128)(2,1)S(1)} %get-tuple-element.37.rest_0_), channel_id=1, source_target_pairs={{0,2},{1,3},{2,0},{3,1},{4,6},{5,7},{6,4},{7,5},{8,10},{9,11},{10,... | collective-permute-start | bytes 393224 | tf_op jit(solution)/shard_map/ppermute | solution.py:299
  5.0 9.7 %collective-permute-start.3 = (bf16[2,4,128,128]{3,2,1,0:T(8,128)(2,1)S(1)}, bf16[2,4,128,128]{3,2,1,0:T(8,128)(2,1)S(1)}, u32[]{:S(2)}, u32[]{:S(2)}) collective-permute-start(bf16[2,4,128,128]{3,2,1,0:T(8,128)(2,1)S(1)} %get-tuple-element.44.rest_0_), channel_id=1, source_target_pairs={{0,2},{1,3},{2,0},{3,1},{4,6},{5,7},{6,4},{7,5},{8,10},{9,11},{10,... | collective-permute-start | bytes 786440 | tf_op jit(solution)/shard_map/ppermute | solution.py:299
  9.4 3.5 %copy-start.2 = (f32[256,128]{1,0:T(8,128)S(1)}, f32[256,128]{1,0:T(8,128)}, u32[]{:S(2)}) copy-start(f32[256,128]{1,0:T(8,128)} %constant.11.clone.table_ref) | copy-start | bytes 393220
  9.4 1.3 %collective-permute-start.4 = (bf16[1,4,128,128]{3,2,1,0:T(8,128)(2,1)S(1)}, bf16[1,4,128,128]{3,2,1,0:T(8,128)(2,1)S(1)}, u32[]{:S(2)}, u32[]{:S(2)}) collective-permute-start(bf16[1,4,128,128]{3,2,1,0:T(8,128)(2,1)S(1)} %collective-permute-done.rest_2_), channel_id=1, source_target_pairs={{0,1},{1,0},{2,3},{3,2},{4,5},{5,4},{6,7},{7,6},{8,9},{9,8},{10,11... | collective-permute-start | bytes 393224 | tf_op jit(solution)/shard_map/ppermute | solution.py:299
  9.4 7.2 %collective-permute-start.2 = (bf16[2,4,128,128]{3,2,1,0:T(8,128)(2,1)S(1)}, bf16[2,4,128,128]{3,2,1,0:T(8,128)(2,1)S(1)}, u32[]{:S(2)}, u32[]{:S(2)}) collective-permute-start(bf16[2,4,128,128]{3,2,1,0:T(8,128)(2,1)S(1)} %get-tuple-element.44.rest_0_), channel_id=1, source_target_pairs={{0,1},{1,0},{2,3},{3,2},{4,5},{5,4},{6,7},{7,6},{8,9},{9,8},{10,11... | collective-permute-start | bytes 786440 | tf_op jit(solution)/shard_map/ppermute | solution.py:299
  14.7 1.9 %collective-permute-start.5 = (bf16[2,4,128,128]{3,2,1,0:T(8,128)(2,1)S(1)}, bf16[2,4,128,128]{3,2,1,0:T(8,128)(2,1)S(1)}, u32[]{:S(2)}, u32[]{:S(2)}) collective-permute-start(bf16[2,4,128,128]{3,2,1,0:T(8,128)(2,1)S(1)} %collective-permute-done.3.rest_2_), channel_id=1, source_target_pairs={{0,1},{1,0},{2,3},{3,2},{4,5},{5,4},{6,7},{7,6},{8,9},{9,8},{10,11... | collective-permute-start | bytes 786440 | tf_op jit(solution)/shard_map/ppermute | solution.py:299
  14.8 8.7 %collective-permute-start.11 = (f16[584,128]{1,0:T(8,128)(2,1)S(1)}, f16[584,128]{1,0:T(8,128)(2,1)S(1)}, u32[]{:S(2)}, u32[]{:S(2)}) collective-permute-start(f16[584,128]{1,0:T(8,128)(2,1)S(1)} %convert_element_type.58), channel_id=1, source_target_pairs={{0,4},{4,0},{8,12},{12,8},{16,20},{20,16},{24,28},{28,24},{1,5},{5... | collective-permute-start | bytes 448520 | tf_op jit(solution)/shard_map/ppermute | solution.py:299
  19.6 7.7 %collective-permute-start.6 = (f16[584,128]{1,0:T(8,128)(2,1)S(1)}, f16[584,128]{1,0:T(8,128)(2,1)S(1)}, u32[]{:S(2)}, u32[]{:S(2)}) collective-permute-start(f16[584,128]{1,0:T(8,128)(2,1)S(1)} %convert_element_type.48), channel_id=1, source_target_pairs={{0,4},{4,0},{8,12},{12,8},{16,20},{20,16},{24,28},{28,24},{1,5},{5... | collective-permute-start | bytes 448520 | tf_op jit(solution)/shard_map/ppermute | solution.py:299
  21.8 8.6 %collective-permute-start.7 = (f16[584,128]{1,0:T(8,128)(2,1)S(1)}, f16[584,128]{1,0:T(8,128)(2,1)S(1)}, u32[]{:S(2)}, u32[]{:S(2)}) collective-permute-start(f16[584,128]{1,0:T(8,128)(2,1)S(1)} %convert_element_type.50), channel_id=1, source_target_pairs={{0,8},{4,12},{8,0},{12,4},{16,24},{20,28},{24,16},{28,20},{1,9},{5... | collective-permute-start | bytes 448520 | tf_op jit(solution)/shard_map/ppermute | solution.py:299
  23.6 7.8 %collective-permute-start.12 = (f16[296,128]{1,0:T(8,128)(2,1)S(1)}, f16[296,128]{1,0:T(8,128)(2,1)S(1)}, u32[]{:S(2)}, u32[]{:S(2)}) collective-permute-start(f16[296,128]{1,0:T(8,128)(2,1)S(1)} %convert_element_type.60), channel_id=1, source_target_pairs={{0,16},{4,20},{8,24},{12,28},{16,0},{20,4},{24,8},{28,12},{1,17},{... | collective-permute-start | bytes 227336 | tf_op jit(solution)/shard_map/ppermute | solution.py:299
  27.5 8.9 %collective-permute-start.10 = (f16[296,128]{1,0:T(8,128)(2,1)S(1)}, f16[296,128]{1,0:T(8,128)(2,1)S(1)}, u32[]{:S(2)}, u32[]{:S(2)}) collective-permute-start(f16[296,128]{1,0:T(8,128)(2,1)S(1)} %convert_element_type.56), channel_id=1, source_target_pairs={{0,16},{4,20},{8,24},{12,28},{16,0},{20,4},{24,8},{28,12},{1,17},{... | collective-permute-start | bytes 227336 | tf_op jit(solution)/shard_map/ppermute | solution.py:299
  28.5 8.0 %collective-permute-start.9 = (f16[296,128]{1,0:T(8,128)(2,1)S(1)}, f16[296,128]{1,0:T(8,128)(2,1)S(1)}, u32[]{:S(2)}, u32[]{:S(2)}) collective-permute-start(f16[296,128]{1,0:T(8,128)(2,1)S(1)} %convert_element_type.54), channel_id=1, source_target_pairs={{0,24},{4,28},{8,16},{12,20},{16,8},{20,12},{24,0},{28,4},{1,25},{... | collective-permute-start | bytes 227336 | tf_op jit(solution)/shard_map/ppermute | solution.py:299
  30.5 6.0 %collective-permute-start.8 = (f16[296,128]{1,0:T(8,128)(2,1)S(1)}, f16[296,128]{1,0:T(8,128)(2,1)S(1)}, u32[]{:S(2)}, u32[]{:S(2)}) collective-permute-start(f16[296,128]{1,0:T(8,128)(2,1)S(1)} %convert_element_type.52), channel_id=1, source_target_pairs={{0,4},{4,0},{8,12},{12,8},{16,20},{20,16},{24,28},{28,24},{1,5},{5... | collective-permute-start | bytes 227336 | tf_op jit(solution)/shard_map/ppermute | solution.py:299
  31.5 4.9 %collective-permute-start.13 = (f16[152,128]{1,0:T(8,128)(2,1)S(1)}, f16[152,128]{1,0:T(8,128)(2,1)S(1)}, u32[]{:S(2)}, u32[]{:S(2)}) collective-permute-start(f16[152,128]{1,0:T(8,128)(2,1)S(1)} %convert_element_type.62), channel_id=1, source_target_pairs={{0,8},{4,12},{8,0},{12,4},{16,24},{20,28},{24,16},{28,20},{1,9},{5... | collective-permute-start | bytes 116744 | tf_op jit(solution)/shard_map/ppermute | solution.py:299
